TPU v7x, 32 devices: a whole 2x2x4 slice. The times are simulated.
32 devices in a mesh: section: 2 (over x), row: 4 (over y, core), mp: 4 (over z).
Axes of the slice: x: 2, y: 2, z: 4, core: 2. Of those that a mesh axis runs over, the one named last changes fastest.
Arguments:
- layer_input: bfloat16 [5, 3136, 512], P(None, ('row', 'mp')), may hold values from -6 to 6
- out_cotangent: bfloat16 [5, 3136, 512], P(None, ('row', 'mp')), may hold values from -6 to 6
- norm_one_gain: float32 [2, 512], P('section'), may hold values from 0.5 to 1.5
- norm_one_bias: float32 [2, 512], P('section'), may hold values from -3 to 3
- attend_weight: bfloat16 [2, 512, 16, 96], P('section', None, 'mp'), may hold values from -0.25 to 0.25
- attend_bias: float32 [2, 16, 64], P('section', 'mp'), may hold values from -3 to 3
- position_table: float32 [2, 16, 169], P('section', 'mp'), may hold values from -4 to 4
- output_weight: bfloat16 [2, 16, 32, 512], P('section', 'mp'), may hold values from -2 to 2
- output_bias: float32 [2, 512], P('section'), may hold values from -3 to 3
- norm_two_gain: float32 [2, 512], P('section'), may hold values from 0.5 to 1.5
- norm_two_bias: float32 [2, 512], P('section'), may hold values from -3 to 3
- expand_weight: bfloat16 [2, 512, 2048], P('section', None, 'mp'), may hold values from -0.25 to 0.25
- expand_bias: float32 [2, 2048], P('section', 'mp'), may hold values from -3 to 3
- reduce_weight: bfloat16 [2, 2048, 512], P('section', 'mp'), may hold values from -0.1875 to 0.1875
- reduce_bias: float32 [2, 512], P('section'), may hold values from -3 to 3
Outputs:
- layer_outputs: bfloat16 [2, 5, 3136, 512], P('section', None, ('row', 'mp'))
- input_grads: float32 [2, 5, 3136, 512], P('section', None, ('row', 'mp'))
- grad_norm_one_gain: float32 [2, 512], P('section')
- grad_norm_one_bias: float32 [2, 512], P('section')
- grad_attend_weight: float32 [2, 512, 16, 96], P('section', None, 'mp')
- grad_attend_bias: float32 [2, 16, 64], P('section', 'mp')
- grad_position_table: float32 [2, 16, 169], P('section', 'mp')
- grad_output_weight: float32 [2, 16, 32, 512], P('section', 'mp')
- grad_output_bias: float32 [2, 512], P('section')
- grad_norm_two_gain: float32 [2, 512], P('section')
- grad_norm_two_bias: float32 [2, 512], P('section')
- grad_expand_weight: float32 [2, 512, 2048], P('section', None, 'mp')
- grad_expand_bias: float32 [2, 2048], P('section', 'mp')
- grad_reduce_weight: float32 [2, 2048, 512], P('section', 'mp')
- grad_reduce_bias: float32 [2, 512], P('section')
All inputs are finite; a program needn't handle non-finite values.
Results may differ from a plain program's by a relative error of at most 0.039.
Values may be sent and summed in bfloat16 or wider, within the bound.
No kernel may reach another device: no remote copies, remote signals or barrier semaphores. Data moves between devices by JAX's collectives and lax.ppermute only.
A program may use at most 192 MiB of HBM per device.

v0:
```python
import jax
import jax.numpy as jnp
from jax import lax
from jax.sharding import PartitionSpec as P

WIN = 7
SHIFT = 3
WCOLS = 8
WROWS = 2
IMGS = 1


layer_eps = 1e-05
highest = lax.Precision.HIGHEST


def passed_along(shard, axis, by):
    count = lax.axis_size(axis)
    return lax.ppermute(shard, axis, [(i, (i + by) % count) for i in range(count)])


def from_behind(block, axis, distance):
    devices = range(lax.axis_size(axis))
    route = [(i - distance, i) for i in devices if i - distance in devices]
    return lax.ppermute(block, axis, route)


def normalize(values, norm_gain, norm_shift):
    middle = jnp.mean(values, axis=-1, keepdims=True)
    centred = values - middle
    spread = jnp.mean(centred * centred, axis=-1, keepdims=True)
    return centred * lax.rsqrt(spread + layer_eps) * norm_gain + norm_shift


def exact_gelu(values):
    return jax.nn.gelu(values, approximate=False)


def to_windows(grid):
    row_count, image_count, image_width, channels = grid.shape
    shaped = grid.reshape(row_count // WIN, WIN, image_count, image_width // WIN, WIN, channels)
    return shaped.transpose(0, 2, 3, 1, 4, 5).reshape(-1, WIN * WIN, channels)


def from_windows(windows, row_count, image_count, image_width):
    channels = windows.shape[-1]
    shaped = windows.reshape(row_count // WIN, image_count, image_width // WIN, WIN, WIN, channels)
    return shaped.transpose(0, 3, 1, 2, 4, 5).reshape(row_count, image_count, image_width, channels)


def roll_forward(grid):
    arriving = passed_along(grid[:SHIFT], "row", -1)
    joined = jnp.concatenate([grid[SHIFT:], arriving], axis=0)
    return jnp.roll(joined, -SHIFT, axis=2)


def roll_backward(grid):
    arriving = passed_along(grid[-SHIFT:], "row", 1)
    joined = jnp.concatenate([arriving, grid[:-SHIFT]], axis=0)
    return jnp.roll(joined, SHIFT, axis=2)


def roll_partial(grid):
    arriving = passed_along(grid[-SHIFT:].astype(jnp.bfloat16), "row", 1).astype(jnp.float32)
    joined = jnp.concatenate([arriving, grid[:-SHIFT]], axis=0)
    return jnp.roll(joined, SHIFT, axis=2)


def gather_rows(shard):
    return lax.all_gather(shard, "mp", axis=0, tiled=True)


def gather_grads(shard):
    return lax.all_gather(shard, "mp", axis=0, tiled=True)


def reduce_rows(left_rows, right_matrix, rows_here):

    def row_term(first_row, row_total):
        return jnp.dot(left_rows, right_matrix, preferred_element_type=jnp.float32)

    return lax.psum_scatter(
        row_term(jnp.int32(0), rows_here * lax.axis_size("mp")).astype(jnp.bfloat16),
        "mp",
        scatter_dimension=0,
        tiled=True,
    ).astype(jnp.float32)


def reduce_grads(left_rows, right_matrix, rows_here):

    def row_term(first_row, row_total):
        return jnp.einsum("nc,dc->nd", left_rows, right_matrix, preferred_element_type=jnp.float32)

    return lax.psum_scatter(
        row_term(jnp.int32(0), rows_here * lax.axis_size("mp")).astype(jnp.bfloat16),
        "mp",
        scatter_dimension=0,
        tiled=True,
    ).astype(jnp.float32)


def position_onehot():
    places = jnp.arange(WIN * WIN, dtype=jnp.int32)
    row_place = places // WIN
    col_place = places % WIN
    table_index = (
        (row_place[:, None] - row_place[None, :] + WIN - 1) * (2 * WIN - 1)
        + col_place[:, None]
        - col_place[None, :]
        + WIN
        - 1
    )
    code_values = jnp.arange((2 * WIN - 1) * (2 * WIN - 1), dtype=jnp.int32)
    return (code_values[:, None] == table_index.reshape(1, -1)).astype(jnp.float32)


def region_term(row_count, image_width, switch):
    total_rows = row_count * lax.axis_size("row")
    heights = lax.axis_index("row") * row_count + jnp.arange(row_count, dtype=jnp.int32)
    widths = jnp.arange(image_width, dtype=jnp.int32)
    row_ids = (heights >= total_rows - WIN).astype(jnp.int32) + (
        heights >= total_rows - SHIFT
    ).astype(jnp.int32)
    col_ids = (widths >= image_width - WIN).astype(jnp.int32) + (
        widths >= image_width - SHIFT
    ).astype(jnp.int32)
    labels = row_ids[:, None] * 3 + col_ids[None, :]
    labels = labels[:, None, :, None]
    labels = to_windows(labels)[..., 0]
    return (
        jnp.where(labels[:, :, None] == labels[:, None, :], 0.0, -100.0).astype(jnp.float32)
        * switch
    )


def round_projection(projected, attend_shift, head_count, head_size):
    shaped = projected.reshape(projected.shape[:-1] + (head_count, 3 * head_size))
    queries = (shaped[..., :head_size] + attend_shift[:, :head_size]) * head_size ** (-0.5)
    key_part = shaped[..., head_size : 2 * head_size]
    value_part = shaped[..., 2 * head_size :] + attend_shift[:, head_size:]
    joined = jnp.concatenate([queries, key_part, value_part], axis=-1)
    return joined.astype(jnp.bfloat16).reshape(projected.shape)


def window_scores(queries, key_part, bias_terms, region):
    scores = jnp.einsum("wqhe,wkhe->whqk", queries, key_part, preferred_element_type=jnp.float32)
    return scores + bias_terms[None] + region[:, None]


def split_triples(triples, head_count, head_size):
    windows = to_windows(triples).reshape(-1, WIN * WIN, head_count, 3 * head_size)
    return (
        windows[..., :head_size],
        windows[..., head_size : 2 * head_size],
        windows[..., 2 * head_size :],
    )


def attend_core(queries, key_part, value_part, bias_terms, region):
    soft_weights = jax.nn.softmax(window_scores(queries, key_part, bias_terms, region), axis=-1)
    context = jnp.einsum(
        "whqk,wkhe->wqhe",
        soft_weights.astype(jnp.bfloat16),
        value_part,
        preferred_element_type=jnp.float32,
    )
    return context.astype(jnp.bfloat16).reshape(context.shape[0], WIN * WIN, -1)


def attend_core_back(queries, key_part, value_part, grad_windows, bias_terms, region, onehot):
    head_count = queries.shape[2]
    head_size = queries.shape[3]
    soft_weights = jax.nn.softmax(window_scores(queries, key_part, bias_terms, region), axis=-1)
    grad_soft = jnp.einsum(
        "wqhe,wkhe->whqk", grad_windows, value_part, preferred_element_type=jnp.float32
    )
    grad_values = jnp.einsum(
        "whqk,wqhe->wkhe",
        soft_weights.astype(jnp.bfloat16),
        grad_windows,
        preferred_element_type=jnp.float32,
    )
    grad_scores = soft_weights * (
        grad_soft - jnp.sum(soft_weights * grad_soft, axis=-1, keepdims=True)
    )
    grad_scores = grad_scores.astype(jnp.bfloat16)
    grad_queries = jnp.einsum(
        "whqk,wkhe->wqhe", grad_scores, key_part, preferred_element_type=jnp.float32
    ) * head_size ** (-0.5)
    grad_keys = jnp.einsum(
        "whqk,wqhe->wkhe", grad_scores, queries, preferred_element_type=jnp.float32
    )
    query_low = grad_queries.astype(jnp.bfloat16)
    keys_low = grad_keys.astype(jnp.bfloat16)
    values_low = grad_values.astype(jnp.bfloat16)
    grad_bias = jnp.concatenate(
        [
            jnp.sum(query_low, axis=(0, 1), dtype=jnp.float32),
            jnp.sum(values_low, axis=(0, 1), dtype=jnp.float32),
        ],
        axis=-1,
    )
    score_total = jnp.sum(grad_scores, axis=0, dtype=jnp.float32).reshape(head_count, -1)
    grad_table = jnp.einsum("hn,cn->hc", score_total, onehot, precision=highest)
    joined = jnp.concatenate([query_low, keys_low, values_low], axis=-1).reshape(
        -1, WIN * WIN, head_count * 3 * head_size
    )
    return (joined, grad_bias, grad_table)


def project_inputs(layer_in, params, geometry, switch_on):
    row_count, image_count, image_width, head_count, head_size = geometry[:5]
    normed = normalize(layer_in, params[0], params[1])
    gathered = gather_rows(normed.astype(jnp.bfloat16))
    norm_tiles = gathered.reshape(row_count, image_count, image_width, -1)
    norm_tiles = jnp.where(switch_on, roll_forward(norm_tiles), norm_tiles)
    projected = jnp.einsum(
        "riwd,dc->riwc", norm_tiles, params[2], preferred_element_type=jnp.float32
    )
    triples = round_projection(projected, params[3], head_count, head_size)
    return (norm_tiles, triples)


def attend(triples, geometry):
    row_count, image_count, image_width, head_count, head_size, bias_terms, region = geometry
    queries, key_part, value_part = split_triples(triples, head_count, head_size)
    context = attend_core(queries, key_part, value_part, bias_terms, region)
    return from_windows(context, row_count, image_count, image_width)


def attend_back(triples, grad_context, geometry, onehot):
    row_count, image_count, image_width, head_count, head_size, bias_terms, region = geometry
    queries, key_part, value_part = split_triples(triples, head_count, head_size)
    grad_windows = to_windows(grad_context).reshape(-1, WIN * WIN, head_count, head_size)
    joined, grad_bias, grad_table = attend_core_back(
        queries, key_part, value_part, grad_windows, bias_terms, region, onehot
    )
    return (from_windows(joined, row_count, image_count, image_width), grad_bias, grad_table)


def layer_forward(layer_in, params, geometry, switch_on):
    rows_here = layer_in.shape[0]
    norm_tiles, triples = project_inputs(layer_in, params, geometry, switch_on)
    context = attend(triples, geometry)
    context = jnp.where(switch_on, roll_backward(context), context)
    flat_context = context.reshape(-1, context.shape[-1])
    middle = layer_in + (reduce_rows(flat_context, params[5], rows_here) + params[6])
    normed_two = normalize(middle, params[7], params[8])
    gathered_two = gather_rows(normed_two.astype(jnp.bfloat16))
    hidden = jnp.dot(gathered_two, params[9], preferred_element_type=jnp.float32) + params[10]
    active = exact_gelu(hidden).astype(jnp.bfloat16)
    output = middle + (reduce_rows(active, params[11], rows_here) + params[12])
    return (output, middle)


def layer_backward(layer_in, middle, out_grad, params, geometry, switch_on, onehot):
    rows_here = layer_in.shape[0]
    norm_tiles, triples = project_inputs(layer_in, params, geometry, switch_on)
    context = attend(triples, geometry)
    context = jnp.where(switch_on, roll_backward(context), context)
    flat_context = context.reshape(-1, context.shape[-1])
    normed_two = normalize(middle, params[7], params[8])
    gathered_two = gather_rows(normed_two.astype(jnp.bfloat16))
    hidden = jnp.dot(gathered_two, params[9], preferred_element_type=jnp.float32) + params[10]
    gelu_out, gelu_back = jax.vjp(exact_gelu, hidden)
    active = gelu_out.astype(jnp.bfloat16)
    out_low = out_grad.astype(jnp.bfloat16)
    grad_reduce_b = jnp.sum(out_low, axis=0, dtype=jnp.float32)
    out_full = gather_grads(out_low)
    grad_reduce_w = jnp.einsum("nf,nd->fd", active, out_full, preferred_element_type=jnp.float32)
    grad_active = jnp.einsum("nd,fd->nf", out_full, params[11], preferred_element_type=jnp.float32)
    grad_hidden = gelu_back(grad_active)[0].astype(jnp.bfloat16)
    grad_expand_b = jnp.sum(grad_hidden, axis=0, dtype=jnp.float32)
    grad_expand_w = jnp.einsum(
        "nd,nf->df", gathered_two, grad_hidden, preferred_element_type=jnp.float32
    )
    grad_normed_two = reduce_grads(grad_hidden, params[9], rows_here)
    norm_back_two = jax.vjp(normalize, middle, params[7], params[8])[1]
    middle_part, grad_gain_two, grad_shift_two = norm_back_two(grad_normed_two)
    grad_middle = out_grad + middle_part
    middle_low = grad_middle.astype(jnp.bfloat16)
    grad_output_b = jnp.sum(middle_low, axis=0, dtype=jnp.float32)
    middle_full = gather_grads(middle_low)
    grad_output_w = jnp.einsum(
        "nc,nd->cd", flat_context, middle_full, preferred_element_type=jnp.float32
    )
    grad_context = jnp.einsum(
        "nd,cd->nc", middle_full, params[5], preferred_element_type=jnp.float32
    )
    grad_context = grad_context.astype(jnp.bfloat16).reshape(context.shape)
    grad_context = jnp.where(switch_on, roll_forward(grad_context), grad_context)
    grad_triples, grad_attend_b, grad_table = attend_back(triples, grad_context, geometry, onehot)
    grad_attend_w = jnp.einsum(
        "riwd,riwc->dc", norm_tiles, grad_triples, preferred_element_type=jnp.float32
    )
    grad_tiles = jnp.einsum(
        "riwc,dc->riwd", grad_triples, params[2], preferred_element_type=jnp.float32
    )
    grad_tiles = jnp.where(switch_on, roll_partial(grad_tiles), grad_tiles)
    grad_normed = lax.psum_scatter(
        grad_tiles.reshape(-1, grad_tiles.shape[-1]).astype(jnp.bfloat16),
        "mp",
        scatter_dimension=0,
        tiled=True,
    ).astype(jnp.float32)
    norm_back_one = jax.vjp(normalize, layer_in, params[0], params[1])[1]
    input_part, grad_gain_one, grad_shift_one = norm_back_one(grad_normed)
    grad_in = grad_middle + input_part
    large_grads = (
        grad_attend_w,
        grad_attend_b,
        grad_table,
        grad_output_w,
        grad_expand_w,
        grad_expand_b,
        grad_reduce_w,
    )
    small_grads = (
        grad_gain_one,
        grad_shift_one,
        grad_output_b,
        grad_gain_two,
        grad_shift_two,
        grad_reduce_b,
    )
    return (grad_in, large_grads, small_grads)


def body(
    layer_input,
    out_cotangent,
    norm_one_gain,
    norm_one_bias,
    attend_weight,
    attend_bias,
    position_table,
    output_weight,
    output_bias,
    norm_two_gain,
    norm_two_bias,
    expand_weight,
    expand_bias,
    reduce_weight,
    reduce_bias,
):
    section_index = lax.axis_index("section")
    first_section = section_index == 0
    switch_on = section_index == 1
    switch = switch_on.astype(jnp.float32)
    head_count = attend_weight.shape[2]
    head_size = output_weight.shape[2]
    model_width = layer_input.shape[2]
    params = (
        norm_one_gain[0],
        norm_one_bias[0],
        attend_weight[0].reshape(model_width, -1),
        attend_bias[0],
        position_table[0],
        output_weight[0].reshape(head_count * head_size, model_width),
        output_bias[0],
        norm_two_gain[0],
        norm_two_bias[0],
        expand_weight[0],
        expand_bias[0],
        reduce_weight[0],
        reduce_bias[0],
    )
    row_count = WIN * WROWS
    image_count = IMGS
    image_width = WIN * WCOLS
    onehot = position_onehot()
    bias_terms = jnp.dot(params[4], onehot, precision=highest).reshape(
        head_count, WIN * WIN, WIN * WIN
    )
    region = region_term(row_count, image_width, switch)
    geometry = (row_count, image_count, image_width, head_count, head_size, bias_terms, region)
    batches = layer_input.shape[0]
    shard_rows = layer_input.shape[1]
    zeros_low = jnp.zeros((shard_rows, model_width), jnp.bfloat16)
    received_act = zeros_low
    received_grad = zeros_low
    kept_middles = jnp.zeros((batches, shard_rows, model_width), jnp.float32)
    outputs_low = jnp.zeros((batches, shard_rows, model_width), jnp.bfloat16)
    input_grads = jnp.zeros((batches, shard_rows, model_width), jnp.float32)
    large_total = None
    small_total = None
    for step_index in range(batches + 2):
        forward_batch = step_index - section_index
        backward_batch = step_index - 2 + section_index
        forward_valid = (forward_batch >= 0) & (forward_batch < batches)
        backward_valid = (backward_batch >= 0) & (backward_batch < batches)
        forward_slot = jnp.clip(forward_batch, 0, batches - 1)
        backward_slot = jnp.clip(backward_batch, 0, batches - 1)
        own_input = lax.dynamic_index_in_dim(layer_input, forward_slot, 0, keepdims=False).astype(
            jnp.float32
        )
        forward_in = jnp.where(first_section, own_input, received_act.astype(jnp.float32))
        forward_out, middle = layer_forward(forward_in, params, geometry, switch_on)
        forward_low = forward_out.astype(jnp.bfloat16)
        kept_old = lax.dynamic_index_in_dim(kept_middles, forward_slot, 0, keepdims=False)
        kept_middles = lax.dynamic_update_index_in_dim(
            kept_middles, jnp.where(forward_valid, middle, kept_old), forward_slot, 0
        )
        shown_old = lax.dynamic_index_in_dim(outputs_low, forward_slot, 0, keepdims=False)
        outputs_low = lax.dynamic_update_index_in_dim(
            outputs_low, jnp.where(forward_valid, forward_low, shown_old), forward_slot, 0
        )
        target = lax.dynamic_index_in_dim(out_cotangent, backward_slot, 0, keepdims=False).astype(
            jnp.float32
        )
        backward_grad = jnp.where(first_section, received_grad.astype(jnp.float32), target)
        kept_middle = lax.dynamic_index_in_dim(kept_middles, backward_slot, 0, keepdims=False)
        back_input = lax.dynamic_index_in_dim(layer_input, backward_slot, 0, keepdims=False).astype(
            jnp.float32
        )
        backward_in = jnp.where(first_section, back_input, received_act.astype(jnp.float32))
        grad_in, large_grads, small_grads = layer_backward(
            backward_in, kept_middle, backward_grad, params, geometry, switch_on, onehot
        )
        weight = backward_valid.astype(jnp.float32)
        if large_total is None:
            large_total = jax.tree.map(lambda newest: weight * newest, large_grads)
            small_total = jax.tree.map(lambda newest: weight * newest, small_grads)
        else:
            large_total = jax.tree.map(
                lambda running, newest: running + weight * newest, large_total, large_grads
            )
            small_total = jax.tree.map(
                lambda running, newest: running + weight * newest, small_total, small_grads
            )
        grad_low = grad_in.astype(jnp.bfloat16)
        stored = jnp.where(first_section, grad_in, grad_low.astype(jnp.float32))
        grad_old = lax.dynamic_index_in_dim(input_grads, backward_slot, 0, keepdims=False)
        input_grads = lax.dynamic_update_index_in_dim(
            input_grads, jnp.where(backward_valid, stored, grad_old), backward_slot, 0
        )
        received_act = from_behind(forward_low, "section", 1)
        received_grad = from_behind(grad_low, "section", -1)
    (
        attend_w_sum,
        attend_b_sum,
        table_sum,
        output_w_sum,
        expand_w_sum,
        expand_b_sum,
        reduce_w_sum,
    ) = large_total
    gain_one_sum, shift_one_sum, output_b_sum, gain_two_sum, shift_two_sum, reduce_b_sum = (
        small_total
    )
    (
        attend_w_sum,
        attend_b_sum,
        table_sum,
        output_w_sum,
        expand_w_sum,
        expand_b_sum,
        reduce_w_sum,
    ) = (
        lax.psum(attend_w_sum.astype(jnp.bfloat16), "row").astype(jnp.float32),
        lax.psum(attend_b_sum.astype(jnp.bfloat16), "row").astype(jnp.float32),
        lax.psum(table_sum.astype(jnp.bfloat16), "row").astype(jnp.float32),
        lax.psum(output_w_sum.astype(jnp.bfloat16), "row").astype(jnp.float32),
        lax.psum(expand_w_sum.astype(jnp.bfloat16), "row").astype(jnp.float32),
        lax.psum(expand_b_sum.astype(jnp.bfloat16), "row").astype(jnp.float32),
        lax.psum(reduce_w_sum.astype(jnp.bfloat16), "row").astype(jnp.float32),
    )
    gain_one_sum, shift_one_sum, output_b_sum, gain_two_sum, shift_two_sum, reduce_b_sum = lax.psum(
        (gain_one_sum, shift_one_sum, output_b_sum, gain_two_sum, shift_two_sum, reduce_b_sum),
        ("row", "mp"),
    )
    return (
        outputs_low[None],
        input_grads[None],
        gain_one_sum[None],
        shift_one_sum[None],
        attend_w_sum.reshape(attend_weight.shape),
        attend_b_sum[None],
        table_sum[None],
        output_w_sum.reshape(output_weight.shape),
        output_b_sum[None],
        gain_two_sum[None],
        shift_two_sum[None],
        expand_w_sum[None],
        expand_b_sum[None],
        reduce_w_sum[None],
        reduce_b_sum[None],
    )


def solution(mesh):
    return jax.shard_map(
        body,
        mesh=mesh,
        in_specs=(
            P(None, ("row", "mp"), None),
            P(None, ("row", "mp"), None),
            P("section", None),
            P("section", None),
            P("section", None, "mp", None),
            P("section", "mp", None),
            P("section", "mp", None),
            P("section", "mp", None, None),
            P("section", None),
            P("section", None),
            P("section", None),
            P("section", None, "mp"),
            P("section", "mp"),
            P("section", "mp", None),
            P("section", None),
        ),
        out_specs=(
            P("section", None, ("row", "mp"), None),
            P("section", None, ("row", "mp"), None),
            P("section", None),
            P("section", None),
            P("section", None, "mp", None),
            P("section", "mp", None),
            P("section", "mp", None),
            P("section", "mp", None, None),
            P("section", None),
            P("section", None),
            P("section", None),
            P("section", None, "mp"),
            P("section", "mp"),
            P("section", "mp", None),
            P("section", None),
        ),
        check_vma=False,
    )
```

profile of v0, /device:TPU:3, one launch (start us, length us, event | category | flops | bytes accessed | tf_op | source)
XLA Modules:
  0.0 2883.6 jit_solution(17666497331195931733)
XLA Ops:
  11.6 17.6 all-gather.16
  33.4 17.1 all-gather
  125.8 20.1 fusion
  189.0 19.4 fusion.14
  282.6 18.3 fusion.15
  409.4 17.1 all-gather.2
  541.9 18.5 fusion.2
  727.9 31.2 %fusion.1201 = (bf16[200,512]{1,0:T(8,128)(2,1)}, bf16[200,512]{1,0:T(8,128)(2,1)}) fusion(bf16[784,512]{1,0:T(8,128)(2,1)} %convolution_convert_fusion.17, bf16[784,512]{1,0:T(8,128)(2,1)} %bitcast.1759), kind=kCustom, calls=%all-reduce-scatter.33 | all-reduce-scatter fusion | flops 819201 | bytes 2015744
  815.5 18.8 all-gather.4
  951.7 18.3 fusion.4
  1137.5 31.2 %fusion.1200 = (bf16[200,512]{1,0:T(8,128)(2,1)}, bf16[200,512]{1,0:T(8,128)(2,1)}) fusion(bf16[784,512]{1,0:T(8,128)(2,1)} %convolution_convert_fusion.15, bf16[784,512]{1,0:T(8,128)(2,1)} %bitcast.1760), kind=kCustom, calls=%all-reduce-scatter.32 | all-reduce-scatter fusion | flops 819201 | bytes 2015744
  1224.7 18.8 all-gather.6
  1360.7 18.3 fusion.6
  1546.7 31.2 %fusion.1199 = (bf16[200,512]{1,0:T(8,128)(2,1)}, bf16[200,512]{1,0:T(8,128)(2,1)}) fusion(bf16[784,512]{1,0:T(8,128)(2,1)} %convolution_convert_fusion.13, bf16[784,512]{1,0:T(8,128)(2,1)} %bitcast.1761), kind=kCustom, calls=%all-reduce-scatter.31 | all-reduce-scatter fusion | flops 819201 | bytes 2015744
  1633.9 18.8 all-gather.8
  1770.0 18.3 fusion.8
  1955.8 31.3 %fusion.1198 = (bf16[200,512]{1,0:T(8,128)(2,1)}, bf16[200,512]{1,0:T(8,128)(2,1)}) fusion(bf16[784,512]{1,0:T(8,128)(2,1)} %convolution_convert_fusion.11, bf16[784,512]{1,0:T(8,128)(2,1)} %bitcast.1762), kind=kCustom, calls=%all-reduce-scatter.30 | all-reduce-scatter fusion | flops 819201 | bytes 2015744
  2042.9 18.8 all-gather.10
  2179.0 18.3 fusion.10
  2365.0 31.3 %fusion.1197 = (bf16[200,512]{1,0:T(8,128)(2,1)}, bf16[200,512]{1,0:T(8,128)(2,1)}) fusion(bf16[784,512]{1,0:T(8,128)(2,1)} %convolution_convert_fusion.9, bf16[784,512]{1,0:T(8,128)(2,1)} %bitcast.1763), kind=kCustom, calls=%all-reduce-scatter.29 | all-reduce-scatter fusion | flops 819201 | bytes 2015744
  2568.4 18.7 all-gather.39
  2592.2 18.4 fusion.12
  2759.7 32.8 %fusion.1196 = (bf16[200,512]{1,0:T(8,128)(2,1)S(1)}, bf16[200,512]{1,0:T(8,128)(2,1)S(1)}) fusion(bf16[784,512]{1,0:T(8,128)(2,1)} %convolution_convert_fusion.7, bf16[784,512]{1,0:T(8,128)(2,1)S(1)} %bitcast.1758), kind=kCustom, calls=%all-reduce-scatter.28 | all-reduce-scatter fusion | flops 819201 | bytes 2015744
  2809.4 57.2 %all-reduce.56 = (f32[1,512]{1,0:T(1,128)}, f32[1,512]{1,0:T(1,128)}, f32[1,512]{1,0:T(1,128)}, f32[1,512]{1,0:T(1,128)}, f32[1,512]{1,0:T(1,128)}, /*index=5*/f32[1,512]{1,0:T(1,128)}) all-reduce(f32[1,512]{1,0:T(1,128)S(1)} %bitcast.1929, f32[1,512]{1,0:T(1,128)S(1)} %bitcast.1928, ...), channel_id=1, replica_groups=mesh['section'=2,'row'=4,'mp'=4] {'row','mp'}, use_global_device_ids=true, to_apply=%region_154.155 | all-reduce | flops 3072 | bytes 24576 | tf_op jit(solution)/shard_map/psum | solution.py:469
  (1933 shorter events, 2303.6 us)
Async XLA Ops:
  7.2 2863.5 %all-reduce.67.cloned.1.call-start = ((), (), s32[]{:S(2)}) async-start(), calls=%async_computation | async-start | bytes 3145728 | tf_op jit(solution)/shard_map/psum | solution.py:461
  30.1 47.6 %collective-permute-start.20 = (bf16[3,1,56,512]{3,2,0,1:T(8,128)(2,1)}, bf16[3,1,56,512]{3,2,0,1:T(8,128)(2,1)S(1)}, u32[]{:S(2)}, u32[]{:S(2)}) collective-permute-start(bf16[3,1,56,512]{3,2,0,1:T(8,128)(2,1)} %bitcast.141), channel_id=1, source_target_pairs={{0,12},{4,0},{8,4},{12,8},{1,13},{5,1},{9,5},{13,9},{2,14},{6,2},{... | collective-permute-start | bytes 516104 | tf_op jit(solution)/shard_map/ppermute | solution.py:19
  51.3 28.8 collective-permute-start
  156.0 54.9 %collective-permute-start.47 = (bf16[3,1,56,128]{3,2,0,1:T(8,128)(2,1)}, bf16[3,1,56,128]{3,2,0,1:T(8,128)(2,1)}, u32[]{:S(2)}, u32[]{:S(2)}) collective-permute-start(bf16[3,1,56,128]{3,2,0,1:T(8,128)(2,1)} %slice.1491), channel_id=1, source_target_pairs={{0,4},{4,8},{8,12},{12,0},{1,5},{5,9},{9,13},{13,1},{2,6},{6,10},{... | collective-permute-start | bytes 129032 | tf_op jit(solution)/shard_map/ppermute | solution.py:19
  395.8 43.2 %collective-permute-start.24 = (bf16[3,1,56,512]{3,2,0,1:T(8,128)(2,1)}, bf16[3,1,56,512]{3,2,0,1:T(8,128)(2,1)}, u32[]{:S(2)}, u32[]{:S(2)}) collective-permute-start(bf16[3,1,56,512]{3,2,0,1:T(8,128)(2,1)} %bitcast.172), channel_id=1, source_target_pairs={{0,12},{4,0},{8,4},{12,8},{1,13},{5,1},{9,5},{13,9},{2,14},{6,2},{... | collective-permute-start | bytes 516104 | tf_op jit(solution)/shard_map/ppermute | solution.py:19
  434.0 86.4 %collective-permute-start.23 = (bf16[196,512]{1,0:T(8,128)(2,1)}, bf16[196,512]{1,0:T(8,128)(2,1)S(1)}, u32[]{:S(2)}, u32[]{:S(2)}) collective-permute-start(bf16[196,512]{1,0:T(8,128)(2,1)} %get-tuple-element.173), channel_id=1, source_target_pairs={{16,0},{17,1},{18,2},{19,3},{20,4},{21,5},{22,6},{23,7},{24,8},{25... | collective-permute-start | bytes 602120 | tf_op jit(solution)/shard_map/ppermute | solution.py:25
  520.0 42.2 %collective-permute-start.48 = (bf16[3,1,56,128]{3,2,0,1:T(8,128)(2,1)}, bf16[3,1,56,128]{3,2,0,1:T(8,128)(2,1)}, u32[]{:S(2)}, u32[]{:S(2)}) collective-permute-start(bf16[3,1,56,128]{3,2,0,1:T(8,128)(2,1)} %slice.1493), channel_id=1, source_target_pairs={{0,4},{4,8},{8,12},{12,0},{1,5},{5,9},{9,13},{13,1},{2,6},{6,10},{... | collective-permute-start | bytes 129032 | tf_op jit(solution)/shard_map/ppermute | solution.py:19
  810.7 37.8 %collective-permute-start.28 = (bf16[3,1,56,512]{3,2,0,1:T(8,128)(2,1)}, bf16[3,1,56,512]{3,2,0,1:T(8,128)(2,1)}, u32[]{:S(2)}, u32[]{:S(2)}) collective-permute-start(bf16[3,1,56,512]{3,2,0,1:T(8,128)(2,1)} %bitcast.204), channel_id=1, source_target_pairs={{0,12},{4,0},{8,4},{12,8},{1,13},{5,1},{9,5},{13,9},{2,14},{6,2},{... | collective-permute-start | bytes 516104 | tf_op jit(solution)/shard_map/ppermute | solution.py:19
  841.1 89.2 %collective-permute-start.27 = (bf16[196,512]{1,0:T(8,128)(2,1)}, bf16[196,512]{1,0:T(8,128)(2,1)S(1)}, u32[]{:S(2)}, u32[]{:S(2)}) collective-permute-start(bf16[196,512]{1,0:T(8,128)(2,1)} %fusion.878), channel_id=1, source_target_pairs={{16,0},{17,1},{18,2},{19,3},{20,4},{21,5},{22,6},{23,7},{24,8},{25... | collective-permute-start | bytes 602120 | tf_op jit(solution)/shard_map/ppermute | solution.py:25
  927.9 22.4 collective-permute-start.7
  929.8 42.2 %collective-permute-start.49 = (bf16[3,1,56,128]{3,2,0,1:T(8,128)(2,1)}, bf16[3,1,56,128]{3,2,0,1:T(8,128)(2,1)}, u32[]{:S(2)}, u32[]{:S(2)}) collective-permute-start(bf16[3,1,56,128]{3,2,0,1:T(8,128)(2,1)} %slice.1495), channel_id=1, source_target_pairs={{0,4},{4,8},{8,12},{12,0},{1,5},{5,9},{9,13},{13,1},{2,6},{6,10},{... | collective-permute-start | bytes 129032 | tf_op jit(solution)/shard_map/ppermute | solution.py:19
  1219.8 38.0 %collective-permute-start.32 = (bf16[3,1,56,512]{3,2,0,1:T(8,128)(2,1)}, bf16[3,1,56,512]{3,2,0,1:T(8,128)(2,1)}, u32[]{:S(2)}, u32[]{:S(2)}) collective-permute-start(bf16[3,1,56,512]{3,2,0,1:T(8,128)(2,1)} %bitcast.236), channel_id=1, source_target_pairs={{0,12},{4,0},{8,4},{12,8},{1,13},{5,1},{9,5},{13,9},{2,14},{6,2},{... | collective-permute-start | bytes 516104 | tf_op jit(solution)/shard_map/ppermute | solution.py:19
  1250.3 89.1 %collective-permute-start.31 = (bf16[196,512]{1,0:T(8,128)(2,1)}, bf16[196,512]{1,0:T(8,128)(2,1)S(1)}, u32[]{:S(2)}, u32[]{:S(2)}) collective-permute-start(bf16[196,512]{1,0:T(8,128)(2,1)} %fusion.879), channel_id=1, source_target_pairs={{16,0},{17,1},{18,2},{19,3},{20,4},{21,5},{22,6},{23,7},{24,8},{25... | collective-permute-start | bytes 602120 | tf_op jit(solution)/shard_map/ppermute | solution.py:25
  1338.9 42.1 %collective-permute-start.50 = (bf16[3,1,56,128]{3,2,0,1:T(8,128)(2,1)}, bf16[3,1,56,128]{3,2,0,1:T(8,128)(2,1)}, u32[]{:S(2)}, u32[]{:S(2)}) collective-permute-start(bf16[3,1,56,128]{3,2,0,1:T(8,128)(2,1)} %slice.1497), channel_id=1, source_target_pairs={{0,4},{4,8},{8,12},{12,0},{1,5},{5,9},{9,13},{13,1},{2,6},{6,10},{... | collective-permute-start | bytes 129032 | tf_op jit(solution)/shard_map/ppermute | solution.py:19
  1629.0 38.0 %collective-permute-start.36 = (bf16[3,1,56,512]{3,2,0,1:T(8,128)(2,1)}, bf16[3,1,56,512]{3,2,0,1:T(8,128)(2,1)}, u32[]{:S(2)}, u32[]{:S(2)}) collective-permute-start(bf16[3,1,56,512]{3,2,0,1:T(8,128)(2,1)} %bitcast.268), channel_id=1, source_target_pairs={{0,12},{4,0},{8,4},{12,8},{1,13},{5,1},{9,5},{13,9},{2,14},{6,2},{... | collective-permute-start | bytes 516104 | tf_op jit(solution)/shard_map/ppermute | solution.py:19
  1659.5 89.2 %collective-permute-start.35 = (bf16[196,512]{1,0:T(8,128)(2,1)}, bf16[196,512]{1,0:T(8,128)(2,1)S(1)}, u32[]{:S(2)}, u32[]{:S(2)}) collective-permute-start(bf16[196,512]{1,0:T(8,128)(2,1)} %fusion.880), channel_id=1, source_target_pairs={{16,0},{17,1},{18,2},{19,3},{20,4},{21,5},{22,6},{23,7},{24,8},{25... | collective-permute-start | bytes 602120 | tf_op jit(solution)/shard_map/ppermute | solution.py:25
  1746.5 22.2 collective-permute-start.13
  1748.2 42.1 %collective-permute-start.51 = (bf16[3,1,56,128]{3,2,0,1:T(8,128)(2,1)}, bf16[3,1,56,128]{3,2,0,1:T(8,128)(2,1)}, u32[]{:S(2)}, u32[]{:S(2)}) collective-permute-start(bf16[3,1,56,128]{3,2,0,1:T(8,128)(2,1)} %slice.1499), channel_id=1, source_target_pairs={{0,4},{4,8},{8,12},{12,0},{1,5},{5,9},{9,13},{13,1},{2,6},{6,10},{... | collective-permute-start | bytes 129032 | tf_op jit(solution)/shard_map/ppermute | solution.py:19
  2038.0 38.0 %collective-permute-start.40 = (bf16[3,1,56,512]{3,2,0,1:T(8,128)(2,1)}, bf16[3,1,56,512]{3,2,0,1:T(8,128)(2,1)}, u32[]{:S(2)}, u32[]{:S(2)}) collective-permute-start(bf16[3,1,56,512]{3,2,0,1:T(8,128)(2,1)} %bitcast.300), channel_id=1, source_target_pairs={{0,12},{4,0},{8,4},{12,8},{1,13},{5,1},{9,5},{13,9},{2,14},{6,2},{... | collective-permute-start | bytes 516104 | tf_op jit(solution)/shard_map/ppermute | solution.py:19
  2068.5 89.1 %collective-permute-start.39 = (bf16[196,512]{1,0:T(8,128)(2,1)}, bf16[196,512]{1,0:T(8,128)(2,1)S(1)}, u32[]{:S(2)}, u32[]{:S(2)}) collective-permute-start(bf16[196,512]{1,0:T(8,128)(2,1)} %fusion.881), channel_id=1, source_target_pairs={{16,0},{17,1},{18,2},{19,3},{20,4},{21,5},{22,6},{23,7},{24,8},{25... | collective-permute-start | bytes 602120 | tf_op jit(solution)/shard_map/ppermute | solution.py:25
  2157.1 42.2 %collective-permute-start.52 = (bf16[3,1,56,128]{3,2,0,1:T(8,128)(2,1)}, bf16[3,1,56,128]{3,2,0,1:T(8,128)(2,1)}, u32[]{:S(2)}, u32[]{:S(2)}) collective-permute-start(bf16[3,1,56,128]{3,2,0,1:T(8,128)(2,1)} %slice.1501), channel_id=1, source_target_pairs={{0,4},{4,8},{8,12},{12,0},{1,5},{5,9},{9,13},{13,1},{2,6},{6,10},{... | collective-permute-start | bytes 129032 | tf_op jit(solution)/shard_map/ppermute | solution.py:19
  2470.6 95.7 %collective-permute-start.43 = (bf16[196,512]{1,0:T(8,128)(2,1)}, bf16[196,512]{1,0:T(8,128)(2,1)}, u32[]{:S(2)}, u32[]{:S(2)}) collective-permute-start(bf16[196,512]{1,0:T(8,128)(2,1)} %fusion.882), channel_id=1, source_target_pairs={{16,0},{17,1},{18,2},{19,3},{20,4},{21,5},{22,6},{23,7},{24,8},{25... | collective-permute-start | bytes 602120 | tf_op jit(solution)/shard_map/ppermute | solution.py:25
  2564.2 25.8 collective-permute-start.19
  2565.9 46.6 %collective-permute-start.53 = (bf16[3,1,56,128]{3,2,0,1:T(8,128)(2,1)}, bf16[3,1,56,128]{3,2,0,1:T(8,128)(2,1)}, u32[]{:S(2)}, u32[]{:S(2)}) collective-permute-start(bf16[3,1,56,128]{3,2,0,1:T(8,128)(2,1)} %slice.1503), channel_id=1, source_target_pairs={{0,4},{4,8},{8,12},{12,0},{1,5},{5,9},{9,13},{13,1},{2,6},{6,10},{... | collective-permute-start | bytes 129032 | tf_op jit(solution)/shard_map/ppermute | solution.py:19
  (436 other events, 4938.4 us)
Sparse Core Ops, SparseCore 0:
  2804.3 41.0 all-reduce.66
where the time goes:
time: 2910 us; the launch traced here: 2880 us
  blocking collectives  1200 us (41%)
  local copies, waits for them, and re-layouts  751 us (26%)
  matrix products  360 us (12%)
  starting transfers between devices  266 us (9%)
  other arithmetic  263 us (9%)
    unnamed x22, blocking collectives  468 us
    all_gather x28, blocking collectives, gather_rows(): return lax.all_gather(shard, 'mp', axis=0, tiled=True)  457 us
    unnamed x851, local copies, waits for them, and re-layouts  255 us
    all_gather x14, blocking collectives, gather_grads(): return lax.all_gather(shard, 'mp', axis=0, tiled=True)  216 us
    ppermute x42, starting transfers between devices, passed_along(): lax.ppermute(shard, axis, [(i, (i + by) % count) for i in range(count)])  177 us
    unnamed x28, starting transfers between devices  58.6 us
  transfers between devices with their start and end apart: 83, of which 8 were waited for; matrix products, arithmetic and copies ran while one was open for 31% of the time, Pallas kernels for 0%

commit v1 on v0

v1 whole, which is shorter than its diff:
```python
import functools

import jax
import jax.numpy as jnp
import numpy as np
from jax import lax
from jax.experimental import pallas as pl
from jax.experimental.pallas import tpu as pltpu
from jax.sharding import PartitionSpec as P

WIN = 7
SHIFT = 3
WCOLS = 8
WROWS = 2
TOKENS = WIN * WIN
SLOT = 64
GROUP = 4
AXES = ("section", "row", "mp")
EPS = 1e-05
BF = jnp.bfloat16
F32 = jnp.float32
NN = (((1,), (0,)), ((), ()))
NT = (((1,), (1,)), ((), ()))
TN = (((0,), (0,)), ((), ()))
VMEM_LIMIT = 56 * 1024 * 1024
highest = lax.Precision.HIGHEST


def mm(left, right, dims=NN):
    return lax.dot_general(left, right, dims, preferred_element_type=F32)


def up16(count):
    return -(-count // 16) * 16


def patch_place(row, col):
    return (col // WIN) * SLOT + row * WIN + col % WIN


class Tables:
    def __init__(self, wins):
        self.wins = wins
        self.rows = wins * SLOT
        cols = wins * WIN
        wide = range(SHIFT, cols)
        thin = range(SHIFT)
        low, high = range(SHIFT, WIN), range(SHIFT)
        pieces = [(low, wide), (high, wide), (low, thin), (high, thin)]
        self.sizes = [up16(len(a) * len(b)) for a, b in pieces]
        self.total = sum(self.sizes)
        pick = np.zeros((self.total, self.rows), np.float32)
        put = np.zeros((self.rows, self.total), np.float32)
        at = 0
        for (rows, columns), size in zip(pieces, self.sizes):
            spot = at
            for row in rows:
                for col in columns:
                    pick[spot, patch_place(row, col)] = 1
                    put[patch_place((row - SHIFT) % WIN, (col - SHIFT) % cols), spot] = 1
                    spot += 1
            at += size
        self.pick, self.put = pick, put


def pair_tables(wins):
    cols = wins * WIN
    tokens = WIN * cols
    keep = np.zeros((2, wins * SLOT, tokens), np.float32)
    take = np.zeros((2, wins * SLOT, up16(SHIFT * cols)), np.float32)
    send = np.zeros((up16(SHIFT * cols), tokens), np.float32)
    for seg in range(SHIFT):
        for col in range(cols):
            send[seg * cols + col, (2 * seg + 1) * cols + col] = 1
    for side in range(2):
        for row in range(WIN):
            for col in range(cols):
                place = patch_place(row, col)
                own = row <= SHIFT if side == 0 else row >= SHIFT
                if own:
                    seg = row if side == 0 else row - SHIFT
                    keep[side, place, 2 * seg * cols + col] = 1
                else:
                    seg = row - SHIFT - 1 if side == 0 else row
                    take[side, place, seg * cols + col] = 1
    return keep, take, send


class Layout:
    def __init__(self, row_count, mp_count):
        self.row_count, self.mp_count = row_count, mp_count
        self.across = mp_count // WROWS
        self.wins = WCOLS // self.across
        self.high = row_count * WROWS

    def device(self, section, window_row, place):
        window_row, place = window_row % self.high, place % self.across
        row = window_row // WROWS
        return (section * self.row_count + row) * self.mp_count + (window_row % WROWS) * self.across + place

    def route(self, source, target, up, back):
        return [
            (self.device(source, window_row, place), self.device(target, window_row - up, place - back))
            for window_row in range(self.high)
            for place in range(self.across)
        ]


HALO = ((0, 0), (1, 0), (0, 1), (1, 1))


def forward_halo(layout, parts, source):
    return [lax.ppermute(part, AXES, layout.route(source, 1, *by)) if (source, by) != (1, (0, 0)) else part for part, by in zip(parts, HALO)]


def backward_halo(layout, parts, target):
    result = []
    for part, by in zip(parts, HALO):
        if (target, by) == (1, (0, 0)):
            result.append(part)
        else:
            result.append(lax.ppermute(part, AXES, [(b, a) for a, b in layout.route(target, 1, *by)]))
    return result


def head_masks(dtype):
    lane = lax.broadcasted_iota(jnp.int32, (1, GROUP * 32), 1)
    return [jnp.where(lane // 32 == h, 1.0, 0.0).astype(dtype) for h in range(GROUP)]


def spread_heads(block, masks):
    return jnp.concatenate([block * mask for mask in masks], axis=0)


def fold_heads(tall, masks):
    total = tall[:SLOT] * masks[0]
    for h in range(1, GROUP):
        total = total + tall[h * SLOT : (h + 1) * SLOT] * masks[h]
    return total


def centre(values):
    middle = jnp.mean(values, axis=-1, keepdims=True)
    centred = values - middle
    scale = lax.rsqrt(jnp.mean(centred * centred, axis=-1, keepdims=True) + EPS)
    return centred * scale, scale


def forward_kernel(
    wins, sec, pin, p_main, p_row, p_col, p_cor, put, pick, wq_h, wo_h, w1_h, w2_h, vec, bq, b1, bias, region,
    y, s_main, s_row, s_col, s_cor, x_o, a_o, qkv_o, prob_o, ctx_o, mid_o, n2_o, act_o, gp_o,
    wq, wo, w1, w2, sems,
):
    copies = [pltpu.make_async_copy(src, dst, sems.at[i]) for i, (src, dst) in enumerate(((wq_h, wq), (wo_h, wo), (w1_h, w1), (w2_h, w2)))]
    for copy in copies:
        copy.start()

    @pl.when(sec[0] == 0)
    def _():
        x_o[...] = pin[0]

    @pl.when(sec[0] == 1)
    def _():
        joined = jnp.concatenate([p_main[...], p_row[...], p_col[...], p_cor[...]], axis=0)
        x_o[...] = mm(put[...], joined).astype(BF)

    def norm_one(w, carry):
        rows = pl.ds(pl.multiple_of(w * SLOT, SLOT), SLOT)
        hat, _ = centre(x_o[rows, :].astype(F32))
        a_o[rows, :] = (hat * vec[0:1, :] + vec[1:2, :]).astype(BF)
        return carry

    lax.fori_loop(0, wins, norm_one, 0)
    copies[0].wait()
    lane = lax.broadcasted_iota(jnp.int32, (1, 3 * GROUP * 32), 1)
    factor = jnp.where(lane < GROUP * 32, 32 ** (-0.5), 1.0)
    for g in range(4):
        cols = slice(g * 384, (g + 1) * 384)
        pr = mm(a_o[...], wq[g]) + bq[g : g + 1, :]
        qkv_o[:, cols] = (pr * factor).astype(BF)

    masks, masks_f = head_masks(BF), head_masks(F32)

    def attend(w, carry):
        rows = pl.ds(pl.multiple_of(w * SLOT, SLOT), SLOT)
        for g in range(4):
            q = qkv_o[rows, g * 384 : g * 384 + 128]
            k = qkv_o[rows, g * 384 + 128 : g * 384 + 256]
            v = qkv_o[rows, g * 384 + 256 : g * 384 + 384]
            scores = mm(k, spread_heads(q, masks), NT) + bias[g] + region[w]
            top = jnp.max(scores, axis=0, keepdims=True)
            e = jnp.exp(scores - top)
            prob = (e * (1.0 / jnp.sum(e, axis=0, keepdims=True))).astype(BF)
            prob_o[rows, g * 256 : (g + 1) * 256] = prob
            ctx_o[rows, g * 128 : (g + 1) * 128] = fold_heads(mm(prob, v, TN), masks_f).astype(BF)
        return carry

    lax.fori_loop(0, wins, attend, 0)
    copies[1].wait()
    mid_o[...] = x_o[...].astype(F32) + (mm(ctx_o[...], wo[...]) + vec[2:3, :])

    def norm_two(w, carry):
        rows = pl.ds(pl.multiple_of(w * SLOT, SLOT), SLOT)
        hat, _ = centre(mid_o[rows, :])
        n2_o[rows, :] = (hat * vec[3:4, :] + vec[4:5, :]).astype(BF)
        return carry

    lax.fori_loop(0, wins, norm_two, 0)
    copies[2].wait()
    copies[3].wait()
    parts, _, width = w1.shape
    total = mid_o[...] + vec[5:6, :]
    for j in range(parts):
        cols = slice(j * width, (j + 1) * width)
        hidden = mm(n2_o[...], w1[j]) + b1[j : j + 1, :]
        phi = 0.5 + 0.5 * lax.erf(hidden * 0.7071067811865476)
        act = (hidden * phi).astype(BF)
        act_o[:, cols] = act
        gp_o[:, cols] = (phi + hidden * (jnp.exp(hidden * hidden * -0.5) * 0.3989422804014327)).astype(BF)
        total = total + mm(act, w2[j])
    out = total.astype(BF)
    y[...] = out
    picked = mm(pick[...], out).astype(BF)
    at = 0
    for ref in (s_main, s_row, s_col, s_cor):
        ref[...] = picked[at : at + ref.shape[0]]
        at += ref.shape[0]


def norm_back(grad, hat, scale, gain):
    inner = grad * gain
    return scale * (inner - jnp.mean(inner, axis=-1, keepdims=True) - hat * jnp.mean(inner * hat, axis=-1, keepdims=True))


def backward_kernel(
    wins, sec, g_main, g_row, g_col, g_cor, c_main, c_row, c_col, c_cor, put, pick, wq_h, wo_h, w1_h, w2_h, vec,
    x0, qkv0, prob0, mid0, gp0, x1, qkv1, prob1, mid1, gp1,
    dx_o, s_main, s_row, s_col, s_cor, g_o, dh_o, gm_o, dqkv_o, small, dbias,
    wq, wo, w1, w2, x, qkv, prob, mid, gp, dmid, dn, dctx, sems,
):
    weights = [pltpu.make_async_copy(src, dst, sems.at[i]) for i, (src, dst) in enumerate(((w2_h, w2), (w1_h, w1), (wo_h, wo), (wq_h, wq)))]
    for copy in weights:
        copy.start()
    kept = (gp, mid, qkv, prob, x)
    olds = [pltpu.make_async_copy(src, dst, sems.at[4 + i]) for i, (src, dst) in enumerate(zip((gp0, mid0, qkv0, prob0, x0), kept))]
    news = [pltpu.make_async_copy(src, dst, sems.at[4 + i]) for i, (src, dst) in enumerate(zip((gp1, mid1, qkv1, prob1, x1), kept))]

    @pl.when(sec[0] == 0)
    def _():
        for copy in olds:
            copy.start()
        joined = jnp.concatenate([g_main[...], g_row[...], g_col[...], g_cor[...]], axis=0)
        g_o[...] = mm(pick[...], joined, TN).astype(BF)

    @pl.when(sec[0] == 1)
    def _():
        for copy in news:
            copy.start()
        joined = jnp.concatenate([c_main[0], c_row[0], c_col[0], c_cor[0]], axis=0)
        g_o[...] = mm(put[...], joined).astype(BF)

    small[...] = jnp.zeros_like(small)
    parts, _, width = w1.shape
    weights[0].wait()
    weights[1].wait()
    olds[0].wait()
    for j in range(parts):
        cols = slice(j * width, (j + 1) * width)
        dh = (mm(g_o[...], w2[j], NT) * gp[:, cols].astype(F32)).astype(BF)
        dh_o[:, cols] = dh
        small[0:1, cols] = jnp.sum(dh.astype(F32), axis=0, keepdims=True)
        part = mm(dh, w1[j], NT)
        if j == 0:
            dn[...] = part
        else:
            dn[...] += part
    olds[1].wait()

    def middle(w, carry):
        rows = pl.ds(pl.multiple_of(w * SLOT, SLOT), SLOT)
        grad = dn[rows, :]
        out = g_o[rows, :].astype(F32)
        hat, scale = centre(mid[rows, :])
        result = out + norm_back(grad, hat, scale, vec[3:4, :])
        dmid[rows, :] = result
        low = result.astype(BF)
        gm_o[rows, :] = low
        small[1:2, 0:512] += jnp.sum(out, axis=0, keepdims=True)
        small[1:2, 512:1024] += jnp.sum(low.astype(F32), axis=0, keepdims=True)
        small[2:3, 0:512] += jnp.sum(grad * hat, axis=0, keepdims=True)
        small[2:3, 512:1024] += jnp.sum(grad, axis=0, keepdims=True)
        return carry

    lax.fori_loop(0, wins, middle, 0)
    weights[2].wait()
    dctx[...] = mm(gm_o[...], wo[...], NT).astype(BF)
    olds[2].wait()
    olds[3].wait()
    dbias[...] = jnp.zeros_like(dbias)
    masks, masks_f = head_masks(BF), head_masks(F32)

    def attend(w, carry):
        rows = pl.ds(pl.multiple_of(w * SLOT, SLOT), SLOT)
        for g in range(4):
            q = qkv[rows, g * 384 : g * 384 + 128]
            k = qkv[rows, g * 384 + 128 : g * 384 + 256]
            v = qkv[rows, g * 384 + 256 : g * 384 + 384]
            do = spread_heads(dctx[rows, g * 128 : (g + 1) * 128], masks)
            low = prob[rows, g * 256 : (g + 1) * 256]
            p = low.astype(F32)
            dp = mm(v, do, NT)
            ds = (p * (dp - jnp.sum(p * dp, axis=0, keepdims=True))).astype(BF)
            dbias[:, g * 256 : (g + 1) * 256] += ds.astype(F32)
            dv = mm(low, do).astype(BF)
            dk = mm(ds, spread_heads(q, masks)).astype(BF)
            dq = (fold_heads(mm(ds, k, TN), masks_f) * 32 ** (-0.5)).astype(BF)
            dqkv_o[rows, g * 384 : g * 384 + 128] = dq
            dqkv_o[rows, g * 384 + 128 : g * 384 + 256] = dk
            dqkv_o[rows, g * 384 + 256 : g * 384 + 384] = dv
            small[3:4, g * 384 : g * 384 + 128] += jnp.sum(dq.astype(F32), axis=0, keepdims=True)
            small[3:4, g * 384 + 256 : g * 384 + 384] += jnp.sum(dv.astype(F32), axis=0, keepdims=True)
        return carry

    lax.fori_loop(0, wins, attend, 0)
    weights[3].wait()
    for g in range(4):
        part = mm(dqkv_o[:, g * 384 : (g + 1) * 384], wq[g], NT)
        if g == 0:
            dn[...] = part
        else:
            dn[...] += part
    olds[4].wait()

    def first(w, carry):
        rows = pl.ds(pl.multiple_of(w * SLOT, SLOT), SLOT)
        grad = dn[rows, :]
        hat, scale = centre(x[rows, :].astype(F32))
        dx_o[rows, :] = (dmid[rows, :] + norm_back(grad, hat, scale, vec[0:1, :])).astype(BF)
        small[1:2, 1024:1536] += jnp.sum(grad * hat, axis=0, keepdims=True)
        small[1:2, 1536:2048] += jnp.sum(grad, axis=0, keepdims=True)
        return carry

    lax.fori_loop(0, wins, first, 0)
    picked = mm(put[...], dx_o[...], TN).astype(BF)
    at = 0
    for ref in (s_main, s_row, s_col, s_cor):
        ref[...] = picked[at : at + ref.shape[0]]
        at += ref.shape[0]


def weight_grad_kernel(slots, batches, cut, sec, *refs):
    lists = [refs[i * slots : (i + 1) * slots] for i in range(4)]
    out1, out2, l1, r1, l2, r2, sems = refs[4 * slots :]
    rows = lists[0][0].shape[0]

    def copies(shift):
        result = []
        for kind, (slot_list, target) in enumerate(zip(lists, (l1, r1, l2, r2))):
            for batch in range(batches):
                result.append(
                    pltpu.make_async_copy(slot_list[batch + shift[kind % 2]], target.at[pl.ds(batch * rows, rows), :], sems.at[kind])
                )
        return result

    first, second = copies((0, 1)), copies((1, 0))

    @pl.when(sec[0] == 0)
    def _():
        for copy in first:
            copy.start()

    @pl.when(sec[0] == 1)
    def _():
        for copy in second:
            copy.start()

    for copy in first[: 2 * batches]:
        copy.wait()
    for part in range(out1.shape[0]):
        if cut[0] == "left":
            width = out1.shape[1]
            out1[part] = mm(l1[:, part * width : (part + 1) * width], r1[...], TN).astype(BF)
        else:
            width = out1.shape[2]
            out1[part] = mm(l1[...], r1[:, part * width : (part + 1) * width], TN).astype(BF)
    for copy in first[2 * batches :]:
        copy.wait()
    for part in range(out2.shape[0]):
        if cut[1] == "left":
            width = out2.shape[1]
            out2[part] = mm(l2[:, part * width : (part + 1) * width], r2[...], TN).astype(BF)
        else:
            width = out2.shape[2]
            out2[part] = mm(l2[...], r2[:, part * width : (part + 1) * width], TN).astype(BF)


SMEM_SPEC = pl.BlockSpec(memory_space=pltpu.SMEM)
HBM_SPEC = pl.BlockSpec(memory_space=pl.ANY)
VMEM_SPEC = pl.BlockSpec(memory_space=pltpu.VMEM)


def batch_spec(array, index):
    return pl.BlockSpec((1,) + array.shape[1:], lambda i: (index, 0, 0))


def shape_of(rows, cols, dtype=BF):
    return jax.ShapeDtypeStruct((rows, cols), dtype)


def run_forward(tables, sec, pin, index, pieces, put, pick, weights, vec, bq, b1, bias, region):
    rows = tables.rows
    wide = weights[2].shape[0] * weights[2].shape[2]
    outs = (
        [shape_of(rows, 512)]
        + [shape_of(size, 512) for size in tables.sizes]
        + [shape_of(rows, 512), shape_of(rows, 512), shape_of(rows, 1536), shape_of(rows, 1024), shape_of(rows, 512)]
        + [shape_of(rows, 512, F32), shape_of(rows, 512), shape_of(rows, wide), shape_of(rows, wide)]
    )
    flops = 2 * rows * 3145728 * 2
    result = pl.pallas_call(
        functools.partial(forward_kernel, tables.wins),
        grid=(1,),
        out_shape=outs,
        in_specs=[SMEM_SPEC, batch_spec(pin, index)] + [VMEM_SPEC] * 6 + [HBM_SPEC] * 4 + [VMEM_SPEC] * 5,
        out_specs=[VMEM_SPEC] * len(outs),
        scratch_shapes=[pltpu.VMEM(w.shape, BF) for w in weights] + [pltpu.SemaphoreType.DMA((4,))],
        compiler_params=pltpu.CompilerParams(vmem_limit_bytes=VMEM_LIMIT),
        cost_estimate=pl.CostEstimate(flops=flops, bytes_accessed=12_000_000, transcendentals=0),
        name="layer_forward",
    )(sec, pin, *pieces, put, pick, *weights, vec, bq, b1, bias, region)
    return result[0], result[1:5], result[5:]


def run_backward(tables, sec, pieces, targets, index, put, pick, weights, vec, old, new):
    rows = tables.rows
    wide = weights[2].shape[0] * weights[2].shape[2]
    outs = (
        [shape_of(rows, 512)]
        + [shape_of(size, 512) for size in tables.sizes]
        + [shape_of(rows, 512), shape_of(rows, wide), shape_of(rows, 512), shape_of(rows, 1536)]
        + [shape_of(8, 2048, F32), shape_of(SLOT, 1024, F32)]
    )
    kept = [pltpu.VMEM(a.shape, a.dtype) for a in old]
    result = pl.pallas_call(
        functools.partial(backward_kernel, tables.wins),
        grid=(1,),
        out_shape=outs,
        in_specs=[SMEM_SPEC] + [VMEM_SPEC] * 4 + [batch_spec(t, index) for t in targets] + [VMEM_SPEC] * 2
        + [HBM_SPEC] * 4 + [VMEM_SPEC] + [HBM_SPEC] * 10,
        out_specs=[VMEM_SPEC] * len(outs),
        scratch_shapes=[pltpu.VMEM(w.shape, BF) for w in weights]
        + kept
        + [pltpu.VMEM((rows, 512), F32), pltpu.VMEM((rows, 512), F32), pltpu.VMEM((rows, 512), BF)]
        + [pltpu.SemaphoreType.DMA((9,))],
        compiler_params=pltpu.CompilerParams(vmem_limit_bytes=VMEM_LIMIT),
        cost_estimate=pl.CostEstimate(flops=2 * rows * 3145728 * 2, bytes_accessed=16_000_000, transcendentals=0),
        name="layer_backward",
    )(sec, *pieces, *targets, put, pick, *weights, vec, *old, *new)
    return result[0], result[1:5], result[5:9], result[9], result[10]


def run_weight_grad(sec, batches, lists, outs, cut):
    slots = len(lists[0])
    rows = lists[0][0].shape[0]
    scratch = [pltpu.VMEM((batches * rows, members[0].shape[1]), BF) for members in lists]
    flops = sum(2 * batches * rows * int(np.prod(out)) for out in outs)
    return pl.pallas_call(
        functools.partial(weight_grad_kernel, slots, batches, cut),
        out_shape=[jax.ShapeDtypeStruct(out, BF) for out in outs],
        in_specs=[SMEM_SPEC] + [HBM_SPEC] * (4 * slots),
        out_specs=[VMEM_SPEC] * 2,
        scratch_shapes=scratch + [pltpu.SemaphoreType.DMA((4,))],
        compiler_params=pltpu.CompilerParams(vmem_limit_bytes=VMEM_LIMIT),
        cost_estimate=pl.CostEstimate(flops=flops, bytes_accessed=20_000_000, transcendentals=0),
        name="weight_grad",
    )(sec, *[member for members in lists for member in members])


def table_onehot():
    code = np.full((SLOT, SLOT), -1, np.int32)
    for u in range(TOKENS):
        for t in range(TOKENS):
            code[u, t] = (t // WIN - u // WIN + WIN - 1) * (2 * WIN - 1) + t % WIN - u % WIN + WIN - 1
    side = (2 * WIN - 1) ** 2
    return (jnp.arange(side, dtype=jnp.int32)[:, None] == jnp.asarray(code.reshape(1, -1))).astype(F32)


def region_mask(layout, section):
    row, mp = lax.axis_index("row"), lax.axis_index("mp")
    window_row = row * WROWS + mp // layout.across
    window_col = (mp % layout.across) * layout.wins + jnp.arange(layout.wins)
    place = jnp.arange(SLOT)
    row_label = jnp.where(window_row == layout.high - 1, 1 + (place // WIN >= WIN - SHIFT).astype(jnp.int32), 0)
    col_label = jnp.where(
        (window_col == WCOLS - 1)[:, None], 1 + (place % WIN >= WIN - SHIFT).astype(jnp.int32)[None], 0
    )
    labels = 3 * row_label[None] + col_label
    differs = labels[:, :, None] != labels[:, None, :]
    term = jnp.where(differs & (section == 1), -100.0, 0.0).astype(F32)
    return jnp.tile(term, (1, 1, GROUP))


def full_patches(layout, mp, tokens):
    wins = layout.wins
    place = jnp.arange(wins * SLOT)
    window, inner = place // SLOT, place % SLOT
    row = (mp // layout.across) * WIN + inner // WIN
    col = ((mp % layout.across) * wins + window) * WIN + inner % WIN
    token = jnp.where(inner < TOKENS, row * (WCOLS * WIN) + col, -1)
    return (token[:, None] == jnp.arange(tokens)[None]).astype(BF)


def whole_patches(layout, mp, tokens_here):
    token = mp * tokens_here + jnp.arange(tokens_here)
    row, col = token // (WCOLS * WIN), token % (WCOLS * WIN)
    window = col // WIN
    owner = (row // WIN) * layout.across + window // layout.wins
    place = owner * layout.wins * SLOT + (window % layout.wins) * SLOT + (row % WIN) * WIN + col % WIN
    return (place[:, None] == jnp.arange(layout.mp_count * layout.wins * SLOT)[None]).astype(BF)


def low_dot(matrix, stack):
    return jnp.einsum("pr,nrd->npd", matrix, stack, preferred_element_type=F32).astype(BF)


def body(
    layer_input,
    out_cotangent,
    norm_one_gain,
    norm_one_bias,
    attend_weight,
    attend_bias,
    position_table,
    output_weight,
    output_bias,
    norm_two_gain,
    norm_two_bias,
    expand_weight,
    expand_bias,
    reduce_weight,
    reduce_bias,
):
    row_count, mp_count = lax.axis_size("row"), lax.axis_size("mp")
    section, mp = lax.axis_index("section"), lax.axis_index("mp")
    layout = Layout(row_count, mp_count)
    tables = Tables(layout.wins)
    put = jnp.asarray(tables.put, BF)
    pick = jnp.asarray(tables.pick, BF)
    batches, tokens_here, width = layer_input.shape
    heads_here = attend_weight.shape[2]
    hidden_here = expand_weight.shape[2]
    sec = section.astype(jnp.int32).reshape(1)
    paired = layout.across == 2
    first = section == 0

    wq_here = attend_weight[0]
    if mp_count == 4:
        wq_here = wq_here.reshape(width, GROUP, 3, 32).transpose(0, 2, 1, 3).reshape(width, GROUP * 96)
    wq_all = lax.all_gather(wq_here, "mp", axis=0)
    if mp_count != 4:
        wq_all = wq_all.transpose(1, 0, 2, 3).reshape(width, 4, GROUP, 3, 32).transpose(1, 0, 3, 2, 4).reshape(4, width, GROUP * 96)
    wo_all = lax.all_gather(output_weight[0], "mp", axis=0).reshape(-1, width)
    w1_all = lax.all_gather(expand_weight[0], "mp", axis=0)
    w2_all = lax.all_gather(reduce_weight[0], "mp", axis=0)
    weights = (wq_all, wo_all, w1_all, w2_all)
    flat = jnp.concatenate([attend_bias[0].reshape(-1), position_table[0].reshape(-1), expand_bias[0].reshape(-1)])
    flat_all = lax.all_gather(flat, "mp", axis=0)
    cut_one = heads_here * 64
    cut_two = cut_one + heads_here * position_table.shape[2]
    bias_all = flat_all[:, :cut_one].reshape(4, GROUP, 2, 32)
    table_all = flat_all[:, cut_one:cut_two].reshape(-1, position_table.shape[2])
    b1 = flat_all[:, cut_two:]
    bq = jnp.stack([bias_all[:, :, 0], jnp.zeros_like(bias_all[:, :, 0]), bias_all[:, :, 1]], axis=1).reshape(4, -1)
    onehot = table_onehot()
    bias = jnp.dot(table_all, onehot, precision=highest).reshape(4, GROUP, SLOT, SLOT).transpose(0, 2, 1, 3)
    bias = bias.reshape(4, SLOT, GROUP * SLOT) + jnp.where(jnp.arange(SLOT) < TOKENS, 0.0, -1e30)[None, :, None]
    vec = jnp.concatenate(
        [norm_one_gain, norm_one_bias, output_bias, norm_two_gain, norm_two_bias, reduce_bias, jnp.zeros((2, width), F32)]
    )
    region = region_mask(layout, section)

    taken = jnp.where(first, layer_input, out_cotangent)
    if paired:
        keep, take, send = pair_tables(layout.wins)
        side = mp % 2
        keep = lax.dynamic_index_in_dim(jnp.asarray(keep, BF), side, 0, keepdims=False)
        take = lax.dynamic_index_in_dim(jnp.asarray(take, BF), side, 0, keepdims=False)
        send = jnp.asarray(send, BF)
        swap = [(i, i ^ 1) for i in range(mp_count)]
        arrived = lax.ppermute(low_dot(send, taken), "mp", swap)
        pin = low_dot(jnp.concatenate([keep, take], axis=1), jnp.concatenate([taken, arrived], axis=1))
    else:
        everything = lax.all_gather(taken, "mp", axis=1, tiled=True)
        pin = low_dot(full_patches(layout, mp, everything.shape[1]), everything)
    cuts = np.cumsum(tables.sizes)[:-1].tolist()
    targets = forward_halo(layout, jnp.split(low_dot(pick, pin), cuts, axis=1), 1)

    zero_pieces = [jnp.zeros((size, width), BF) for size in tables.sizes]
    forward_pieces, backward_pieces = zero_pieces, zero_pieces
    kept, outputs, grads, back_kept, smalls, biases = [], [], [], [], [], []
    for step in range(batches + 2):
        if step <= batches:
            out, sends, saved = run_forward(
                tables, sec, pin, min(step, batches - 1), forward_pieces, put, pick, weights, vec, bq, b1, bias, region
            )
            outputs.append(out)
            kept.append(saved)
            forward_pieces = forward_halo(layout, sends, 0)
        if step >= 1:
            chosen = [[kept[min(max(at, 0), batches)][i] for i in (0, 2, 3, 5, 8)] for at in (step - 2, step)]
            grad, sends, saved, small, table = run_backward(
                tables, sec, backward_pieces, targets, min(step - 1, batches - 1), put, pick, weights, vec, *chosen
            )
            grads.append(grad)
            back_kept.append(saved)
            smalls.append(small)
            biases.append(table)
            backward_pieces = backward_halo(layout, sends, 0)

    column = lambda rows, i: [row[i] for row in rows]
    d2, d1 = run_weight_grad(
        sec,
        batches,
        (column(kept, 7), column(back_kept, 0), column(kept, 6), column(back_kept, 1)),
        ((mp_count, hidden_here, width), (mp_count, width, hidden_here)),
        ("left", "right"),
    )
    do, dq = run_weight_grad(
        sec,
        batches,
        (column(kept, 4), column(back_kept, 2), column(kept, 1), column(back_kept, 3)),
        ((4, GROUP * 32, width), (4, width, GROUP * 96)),
        ("left", "right"),
    )
    do = do.reshape(mp_count, -1, width)
    if mp_count != 4:
        dq = dq.reshape(4, width, 3, GROUP, 32).transpose(0, 3, 1, 2, 4).reshape(mp_count, heads_here, width, 96)

    def shared(parts):
        part = lax.psum_scatter(parts, "mp", scatter_dimension=0, tiled=False)
        return lax.psum(part, "row").astype(F32)

    d2, d1, do, dq = shared(d2), shared(d1), shared(do), shared(dq)
    if mp_count == 4:
        dq = dq.reshape(width, 3, GROUP, 32).transpose(0, 2, 1, 3).reshape(width, GROUP, 96)
    else:
        dq = dq.transpose(1, 0, 2)
    pick_slots = lambda values: sum(jnp.where(first, values[i + 1], values[i]) for i in range(batches))
    small = pick_slots(smalls)
    table = pick_slots(biases).reshape(SLOT, 4 * GROUP, SLOT).transpose(1, 0, 2).reshape(4 * GROUP, -1)
    table = jnp.dot(table, onehot.T, precision=highest)
    small, table = lax.psum((small, table), ("row", "mp"))
    shift = small[3, :1536].reshape(4, 3, GROUP, 32)
    shift = jnp.concatenate([shift[:, 0], shift[:, 2]], axis=-1).reshape(4 * GROUP, 64)
    mine = lambda array: lax.dynamic_index_in_dim(array.reshape((mp_count, -1) + array.shape[1:]), mp, 0, keepdims=False)

    stack = jnp.stack(
        [jnp.where(first, outputs[i], outputs[i + 1]) for i in range(batches)]
        + [jnp.where(first, grads[i + 1], grads[i]) for i in range(batches)]
    )
    parts = jnp.split(low_dot(put.T, stack), cuts, axis=1)
    unrolled = low_dot(pick.T, jnp.concatenate(backward_halo(layout, parts, 1), axis=1))
    patches = jnp.where(first, stack, unrolled)
    if paired:
        arrived = lax.ppermute(low_dot(take.T, patches), "mp", swap)
        placed = low_dot(jnp.concatenate([keep.T, send.T], axis=1), jnp.concatenate([patches, arrived], axis=1))
    else:
        everything = lax.all_gather(patches, "mp", axis=1, tiled=True)
        placed = low_dot(whole_patches(layout, mp, tokens_here), everything)

    return (
        placed[:batches][None],
        placed[batches:].astype(F32)[None],
        small[1, 1024:1536][None],
        small[1, 1536:2048][None],
        dq[None],
        mine(shift)[None],
        mine(table)[None],
        do.reshape(output_weight.shape),
        small[1, 512:1024][None],
        small[2, 0:512][None],
        small[2, 512:1024][None],
        d1[None],
        mine(small[0])[None],
        d2[None],
        small[1, 0:512][None],
    )


def solution(mesh):
    return jax.shard_map(
        body,
        mesh=mesh,
        in_specs=(
            P(None, ("row", "mp"), None),
            P(None, ("row", "mp"), None),
            P("section", None),
            P("section", None),
            P("section", None, "mp", None),
            P("section", "mp", None),
            P("section", "mp", None),
            P("section", "mp", None, None),
            P("section", None),
            P("section", None),
            P("section", None),
            P("section", None, "mp"),
            P("section", "mp"),
            P("section", "mp", None),
            P("section", None),
        ),
        out_specs=(
            P("section", None, ("row", "mp"), None),
            P("section", None, ("row", "mp"), None),
            P("section", None),
            P("section", None),
            P("section", None, "mp", None),
            P("section", "mp", None),
            P("section", "mp", None),
            P("section", "mp", None, None),
            P("section", None),
            P("section", None),
            P("section", None),
            P("section", None, "mp"),
            P("section", "mp"),
            P("section", "mp", None),
            P("section", None),
        ),
        check_vma=False,
    )
```

time: 2910 us -> 759 us (0.26)
  blocking collectives: 1200 us -> 123 us
  local copies, waits for them, and re-layouts: 751 us -> 31.4 us
  matrix products: 360 us -> 16.3 us
  other arithmetic: 263 us -> 19.5 us
  waiting for transfers between devices: 18.3 us -> 252 us
  Pallas kernels: 0 us -> 172 us
  starting transfers between devices: 266 us -> 116 us
    all_gather x42 -> x1, blocking collectives: 673 us -> 12.7 us  [body(): wo_all = lax.all_gather(output_weight[0], 'mp', axis=0).reshape(-1, width)]
    unnamed x22 -> x1, blocking collectives: 468 us -> 27.6 us
    dot_general x141 -> x9, matrix products: 306 us -> 16.3 us  [the longest x7 11.6 us: low_dot(): jnp.einsum('pr,nrd->npd', matrix, stack, preferred_element_type=F32)]
    unnamed x851 -> x178, local copies, waits for them, and re-layouts: 255 us -> 12.8 us
    pallas_call x0 -> x14, Pallas kernels: none -> 172 us  [the longest x6 89 us: run_backward(): pl.pallas_call(functools.partial(backward_kernel, tables.wins), grid=(1,)...]
    reduce_scatter x0 -> x4, waiting for transfers between devices: none -> 130 us  [shared(): part = lax.psum_scatter(parts, 'mp', scatter_dimension=0, tiled=False)]
    another operation x58 -> x10, local copies, waits for them, and re-layouts: 123 us -> 2.99 us  [the longest x2 1.14 us: region_mask(): return jnp.tile(term, (1, 1, GROUP))]
    slice x118 -> x7, local copies, waits for them, and re-layouts: 120 us -> 3.84 us  [the longest x1 1.47 us: body(): small[1, 0:512][None]]
  transfers between devices with their start and end apart: 83 -> 57, of which waited for: 8 -> 9; matrix products, arithmetic and copies ran while one was open for 31% -> 7% of each run, Pallas kernels for 0% -> 19%
where the time goes in v1:
time: 759 us; the launch traced here: 747 us
  waiting for transfers between devices  252 us (33%)
  Pallas kernels  172 us (23%)
  blocking collectives  123 us (16%)
  starting transfers between devices  116 us (15%)
  local copies, waits for them, and re-layouts  31.4 us (4%)
  other arithmetic  19.5 us (3%)
  between operations  17 us (2%)
  matrix products  16.3 us (2%)
    reduce_scatter x4, waiting for transfers between devices, shared(): part = lax.psum_scatter(parts, 'mp', scatter_dimension=0, tiled=False)  130 us
    pallas_call x6, Pallas kernels, run_backward(): pl.pallas_call(functools.partial(backward_kernel, tables.wins), grid=(1,)...  89 us
    psum x1, blocking collectives, body(): small, table = lax.psum((small, table), ('row', 'mp'))  82.6 us
    pallas_call x6, Pallas kernels, run_forward(): pl.pallas_call(functools.partial(forward_kernel, tables.wins), grid=(1,),...  65.7 us
    ppermute x23, starting transfers between devices, backward_halo(): lax.ppermute(part, AXES, [(b, a) for a, b in layout.route(target, 1, *by)])  60.4 us
    ppermute x23, starting transfers between devices, forward_halo(): lax.ppermute(part, AXES, layout.route(source, 1, *by))  53.2 us
    all_gather x1, waiting for transfers between devices, body(): w2_all = lax.all_gather(reduce_weight[0], 'mp', axis=0)  45.5 us
    psum x1, waiting for transfers between devices, shared(): return lax.psum(part, 'row').astype(F32)  36.8 us
  transfers between devices with their start and end apart: 57, of which 9 were waited for; matrix products, arithmetic and copies ran while one was open for 7% of the time, Pallas kernels for 19%

profile of v1, /device:TPU:3, one launch (start us, length us, event | category | flops | bytes accessed | tf_op | source)
XLA Modules:
  0.0 747.3 jit_solution(8933869907845511857)
XLA Ops:
  14.1 27.6 %all-reduce = f32[5776]{0:T(1024)S(1)} all-reduce(f32[5776]{0:T(1024)S(1)} %dynamic-update-slice), channel_id=2, replica_groups=mesh['section'=2,'row'=4,'mp'=4] {'mp'}, use_global_device_ids=true, to_apply=%add | all-reduce | flops 5776 | bytes 46208
  49.8 12.7 %all_gather.19 = bf16[4,4,32,512]{3,2,1,0:T(8,128)(2,1)} all-gather(bf16[1,4,32,512]{3,2,1,0:T(8,128)(2,1)S(1)} %copy-done.22), channel_id=1, replica_groups=mesh['section'=2,'row'=4,'mp'=4] {'mp'}, dimensions={0}, use_global_device_ids=true | all-gather | bytes 655360 | tf_op jit(solution)/shard_map/all_gather | solution.py:562
  65.7 19.7 %collective-permute-start.21 = (bf16[5,80,512]{2,1,0:T(8,128)(2,1)S(1)}, bf16[5,80,512]{2,1,0:T(8,128)(2,1)S(1)}, u32[]{:S(2)}, u32[]{:S(2)}) collective-permute-start(bf16[5,80,512]{2,1,0:T(8,128)(2,1)S(1)} %split.33), channel_id=1, source_target_pairs={{16,30},{17,31},{18,16},{19,17},{20,18},{21,19},{22,20},{23,21},{2... | collective-permute-start | bytes 1228808 | tf_op jit(solution)/shard_map/ppermute | solution.py:113
  85.4 34.8 %all-gather.7.cloned.1.call-done.w1_h = bf16[4,512,512]{2,1,0:T(8,128)(2,1)} async-done(((bf16[1,512,512]{2,1,0:T(8,128)(2,1)}), bf16[4,512,512]{2,1,0:T(8,128)(2,1)}) %all-gather.7.cloned.1.call-update) | async-done | bytes 2097168 | tf_op jit(solution)/shard_map/all_gather | solution.py:563
  120.2 45.5 %all-gather.9.cloned.1.call-done.w2_h = bf16[4,512,512]{2,1,0:T(8,128)(2,1)} async-done(((bf16[1,512,512]{2,1,0:T(8,128)(2,1)}), bf16[4,512,512]{2,1,0:T(8,128)(2,1)}) %all-gather.9.cloned.1.call-update) | async-done | bytes 2097168 | tf_op jit(solution)/shard_map/all_gather | solution.py:564
  167.6 10.9 %layer_forward.6 = (bf16[256,512]{1,0:T(8,128)(2,1)}, bf16[112,512]{1,0:T(8,128)(2,1)}, bf16[80,512]{1,0:T(8,128)(2,1)}, bf16[16,512]{1,0:T(8,128)(2,1)}, bf16[1...) custom-call(s32[1]{0:T(128)} %bitcast.sec, ...), custom_call_target="tpu_custom_call" | custom-call | flops 3221225472 | bytes 12000000 | tf_op jit(solution)/shard_map/layer_forward/pallas_call | solution.py:420
  196.0 10.9 %layer_forward.7 = (bf16[256,512]{1,0:T(8,128)(2,1)}, bf16[112,512]{1,0:T(8,128)(2,1)}, bf16[80,512]{1,0:T(8,128)(2,1)}, bf16[16,512]{1,0:T(8,128)(2,1)}, bf16[1...) custom-call(s32[1]{0:T(128)} %bitcast.sec, ...), custom_call_target="tpu_custom_call" | custom-call | flops 3221225472 | bytes 12000000 | tf_op jit(solution)/shard_map/layer_forward/pallas_call | solution.py:420
  213.0 14.8 %layer_backward.6 = (bf16[256,512]{1,0:T(8,128)(2,1)}, bf16[112,512]{1,0:T(8,128)(2,1)}, bf16[80,512]{1,0:T(8,128)(2,1)}, bf16[16,512]{1,0:T(8,128)(2,1)}, bf16[...) custom-call(s32[1]{0:T(128)} %bitcast.sec, ...), custom_call_target="tpu_custom_call" | custom-call | flops 3221225472 | bytes 16000000 | tf_op jit(solution)/shard_map/layer_backward/pallas_call | solution.py:444
  239.2 11.0 %layer_forward.8 = (bf16[256,512]{1,0:T(8,128)(2,1)}, bf16[112,512]{1,0:T(8,128)(2,1)}, bf16[80,512]{1,0:T(8,128)(2,1)}, bf16[16,512]{1,0:T(8,128)(2,1)}, bf16[1...) custom-call(s32[1]{0:T(128)} %bitcast.sec, ...), custom_call_target="tpu_custom_call" | custom-call | flops 3221225472 | bytes 12000000 | tf_op jit(solution)/shard_map/layer_forward/pallas_call | solution.py:420
  256.1 14.9 %layer_backward.7 = (bf16[256,512]{1,0:T(8,128)(2,1)}, bf16[112,512]{1,0:T(8,128)(2,1)}, bf16[80,512]{1,0:T(8,128)(2,1)}, bf16[16,512]{1,0:T(8,128)(2,1)}, bf16[...) custom-call(s32[1]{0:T(128)} %bitcast.sec, ...), custom_call_target="tpu_custom_call" | custom-call | flops 3221225472 | bytes 16000000 | tf_op jit(solution)/shard_map/layer_backward/pallas_call | solution.py:444
  282.3 10.9 %layer_forward.9 = (bf16[256,512]{1,0:T(8,128)(2,1)}, bf16[112,512]{1,0:T(8,128)(2,1)}, bf16[80,512]{1,0:T(8,128)(2,1)}, bf16[16,512]{1,0:T(8,128)(2,1)}, bf16[1...) custom-call(s32[1]{0:T(128)} %bitcast.sec, ...), custom_call_target="tpu_custom_call" | custom-call | flops 3221225472 | bytes 12000000 | tf_op jit(solution)/shard_map/layer_forward/pallas_call | solution.py:420
  299.2 14.8 %layer_backward.8 = (bf16[256,512]{1,0:T(8,128)(2,1)}, bf16[112,512]{1,0:T(8,128)(2,1)}, bf16[80,512]{1,0:T(8,128)(2,1)}, bf16[16,512]{1,0:T(8,128)(2,1)}, bf16[...) custom-call(s32[1]{0:T(128)} %bitcast.sec, ...), custom_call_target="tpu_custom_call" | custom-call | flops 3221225472 | bytes 16000000 | tf_op jit(solution)/shard_map/layer_backward/pallas_call | solution.py:444
  325.4 11.0 %layer_forward.10 = (bf16[256,512]{1,0:T(8,128)(2,1)}, bf16[112,512]{1,0:T(8,128)(2,1)}, bf16[80,512]{1,0:T(8,128)(2,1)}, bf16[16,512]{1,0:T(8,128)(2,1)}, bf16[...) custom-call(s32[1]{0:T(128)} %bitcast.sec, ...), custom_call_target="tpu_custom_call" | custom-call | flops 3221225472 | bytes 12000000 | tf_op jit(solution)/shard_map/layer_forward/pallas_call | solution.py:420
  342.4 14.8 %layer_backward.9 = (bf16[256,512]{1,0:T(8,128)(2,1)}, bf16[112,512]{1,0:T(8,128)(2,1)}, bf16[80,512]{1,0:T(8,128)(2,1)}, bf16[16,512]{1,0:T(8,128)(2,1)}, bf16[...) custom-call(s32[1]{0:T(128)} %bitcast.sec, ...), custom_call_target="tpu_custom_call" | custom-call | flops 3221225472 | bytes 16000000 | tf_op jit(solution)/shard_map/layer_backward/pallas_call | solution.py:444
  369.6 10.9 %layer_forward.11 = (bf16[256,512]{1,0:T(8,128)(2,1)}, bf16[112,512]{1,0:T(8,128)(2,1)}, bf16[80,512]{1,0:T(8,128)(2,1)}, bf16[16,512]{1,0:T(8,128)(2,1)}, bf16[...) custom-call(s32[1]{0:T(128)} %bitcast.sec, ...), custom_call_target="tpu_custom_call" | custom-call | flops 3221225472 | bytes 12000000 | tf_op jit(solution)/shard_map/layer_forward/pallas_call | solution.py:420
  381.3 14.8 %layer_backward.10 = (bf16[256,512]{1,0:T(8,128)(2,1)}, bf16[112,512]{1,0:T(8,128)(2,1)}, bf16[80,512]{1,0:T(8,128)(2,1)}, bf16[16,512]{1,0:T(8,128)(2,1)}, bf16...) custom-call(s32[1]{0:T(128)} %bitcast.sec, ...), custom_call_target="tpu_custom_call" | custom-call | flops 3221225472 | bytes 16000000 | tf_op jit(solution)/shard_map/layer_backward/pallas_call | solution.py:444
  403.9 14.8 %layer_backward.11 = (bf16[256,512]{1,0:T(8,128)(2,1)}, bf16[112,512]{1,0:T(8,128)(2,1)}, bf16[80,512]{1,0:T(8,128)(2,1)}, bf16[16,512]{1,0:T(8,128)(2,1)}, bf16...) custom-call(s32[1]{0:T(128)} %bitcast.sec, ...), custom_call_target="tpu_custom_call" | custom-call | flops 3221225472 | bytes 16000000 | tf_op jit(solution)/shard_map/layer_backward/pallas_call | solution.py:444
  427.8 10.2 %weight_grad.3 = (bf16[4,512,512]{2,1,0:T(8,128)(2,1)}, bf16[4,512,512]{2,1,0:T(8,128)(2,1)}) custom-call(s32[1]{0:T(128)} %bitcast.sec, bf16[256,2048]{1,0:T(8,128)(2,1)} %get-tuple-element.281.refs_0_, bf16[256,2048]{1,0:T(8,128)(2,1)} %get-tuple-element.282.refs_1_, bf16[256,2048]{1,0:T(8,128)(2,1)} %get-tuple-element.283.refs_2_, ...), custom_call_target="tpu_custom_call" | custom-call | flops 5368709120 | bytes 20000000 | tf_op jit(solution)/shard_map/weight_grad/pallas_call | solution.py:467
  466.2 82.6 %psum.44 = f32[4,4,169]{2,1,0:T(4,128)S(1)} all-reduce(f32[4,4,169]{2,1,0:T(4,128)S(1)} %reshape.224), channel_id=1, replica_groups=mesh['section'=2,'row'=4,'mp'=4] {'row','mp'}, use_global_device_ids=true, to_apply=%region_3.4 | all-reduce | flops 2704 | bytes 21632 | tf_op jit(solution)/shard_map/psum | solution.py:652
  555.8 16.9 %reduce-scatter.5.cloned.1.call-done = bf16[1,512,384]{2,1,0:T(8,128)(2,1)} async-done(((bf16[4,512,384]{2,1,0:T(8,128)(2,1)}), bf16[1,512,384]{2,1,0:T(8,128)(2,1)}) %reduce-scatter.5.cloned.1.call-update) | async-done | bytes 393232 | tf_op jit(solution)/shard_map/reduce_scatter | solution.py:640
  574.6 22.7 %reduce-scatter.7.cloned.1.call-done = bf16[1,128,512]{2,1,0:T(8,128)(2,1)} async-done(((bf16[4,128,512]{2,1,0:T(8,128)(2,1)}), bf16[1,128,512]{2,1,0:T(8,128)(2,1)}) %reduce-scatter.7.cloned.1.call-update) | async-done | bytes 131088 | tf_op jit(solution)/shard_map/reduce_scatter | solution.py:640
  597.3 45.3 %reduce-scatter.11.cloned.1.call-done = bf16[1,512,512]{2,1,0:T(8,128)(2,1)} async-done(((bf16[4,512,512]{2,1,0:T(8,128)(2,1)}), bf16[1,512,512]{2,1,0:T(8,128)(2,1)}) %reduce-scatter.11.cloned.1.call-update) | async-done | bytes 524304 | tf_op jit(solution)/shard_map/reduce_scatter | solution.py:640
  642.6 45.5 %reduce-scatter.9.cloned.1.call-done = bf16[1,512,512]{2,1,0:T(8,128)(2,1)} async-done(((bf16[4,512,512]{2,1,0:T(8,128)(2,1)}), bf16[1,512,512]{2,1,0:T(8,128)(2,1)}) %reduce-scatter.9.cloned.1.call-update) | async-done | bytes 524304 | tf_op jit(solution)/shard_map/reduce_scatter | solution.py:640
  697.4 36.8 %all-reduce.7.cloned.1.call-done = (bf16[1,512,4,96]{1,3,2,0:T(8,128)(2,1)}, bf16[1,4,32,512]{3,2,1,0:T(8,128)(2,1)}, bf16[1,512,512]{2,1,0:T(8,128)(2,1)}, bf16[1,512,512]{2,1,0:T(8,128)(2,1)}) async-done(((bf16[1,512,4,96]{1,3,2,0:T(8,128)(2,1)}, bf16[1,4,32,512]{3,2,1,0:T(8,128)(2,1)}, bf16[1,512,512]{2,1,0:T(8,128)(2,1)}, bf16[1,512,512]{2,1,0:T(8,128)(2,1)}), (bf16[1,512,4,96]{1,3,2,0:T(8,128)(2,1)}, ...) | async-done | bytes 1572880 | tf_op jit(solution)/shard_map/psum | solution.py:641
  (375 shorter events, 175.4 us)
Async XLA Ops:
  7.2 78.2 %all-gather.5.cloned.1.call-start = ((), (), s32[]{:S(2)}) async-start(), calls=%async_computation.4 | async-start | bytes 1966080 | tf_op jit(solution)/shard_map/all_gather | solution.py:559
  9.4 110.8 %all-gather.7.cloned.1.call-start = ((), (), s32[]{:S(2)}) async-start(), calls=%async_computation.5 | async-start | bytes 2621440 | tf_op jit(solution)/shard_map/all_gather | solution.py:563
  10.1 155.6 %all-gather.9.cloned.1.call-start = ((), (), s32[]{:S(2)}) async-start(), calls=%async_computation.6 | async-start | bytes 2621440 | tf_op jit(solution)/shard_map/all_gather | solution.py:564
  10.7 52.6 %collective-permute-start = (bf16[5,96,512]{2,1,0:T(8,128)(2,1)S(1)}, bf16[5,96,512]{2,1,0:T(8,128)(2,1)}, u32[]{:S(2)}, u32[]{:S(2)}) collective-permute-start(bf16[5,96,512]{2,1,0:T(8,128)(2,1)S(1)} %fusion.26), channel_id=1, source_target_pairs={{0,1},{1,0},{2,3},{3,2},{4,5},{5,4},{6,7},{7,6},{8,9},{9,8},{10,11... | collective-permute-start | bytes 1474568 | tf_op jit(solution)/shard_map/ppermute | solution.py:590
  12.1 541.3 %all-reduce.5.cloned.1.call-start = ((), (), s32[]{:S(2)}) async-start(), calls=%async_computation.7 | async-start | bytes 131072 | tf_op jit(solution)/shard_map/psum | solution.py:652
  65.7 146.5 %collective-permute-start.21 = (bf16[5,80,512]{2,1,0:T(8,128)(2,1)S(1)}, bf16[5,80,512]{2,1,0:T(8,128)(2,1)S(1)}, u32[]{:S(2)}, u32[]{:S(2)}) collective-permute-start(bf16[5,80,512]{2,1,0:T(8,128)(2,1)S(1)} %split.33), channel_id=1, source_target_pairs={{16,30},{17,31},{18,16},{19,17},{20,18},{21,19},{22,20},{23,21},{2... | collective-permute-start | bytes 1228808 | tf_op jit(solution)/shard_map/ppermute | solution.py:113
  207.0 31.6 %collective-permute-start.5 = (bf16[112,512]{1,0:T(8,128)(2,1)}, bf16[112,512]{1,0:T(8,128)(2,1)S(1)}, u32[]{:S(2)}, u32[]{:S(2)}) collective-permute-start(bf16[112,512]{1,0:T(8,128)(2,1)} %get-tuple-element.167), channel_id=1, source_target_pairs={{0,16},{1,17},{2,18},{3,19},{4,20},{5,21},{6,22},{7,23},{8,24},{9,... | collective-permute-start | bytes 344072 | tf_op jit(solution)/shard_map/ppermute | solution.py:113
  208.3 28.5 %collective-permute-start.6 = (bf16[80,512]{1,0:T(8,128)(2,1)}, bf16[80,512]{1,0:T(8,128)(2,1)S(1)}, u32[]{:S(2)}, u32[]{:S(2)}) collective-permute-start(bf16[80,512]{1,0:T(8,128)(2,1)} %get-tuple-element.168), channel_id=1, source_target_pairs={{0,30},{1,31},{2,16},{3,17},{4,18},{5,19},{6,20},{7,21},{8,22},{9,... | collective-permute-start | bytes 245768 | tf_op jit(solution)/shard_map/ppermute | solution.py:113
  250.2 31.4 %collective-permute-start.9 = (bf16[112,512]{1,0:T(8,128)(2,1)}, bf16[112,512]{1,0:T(8,128)(2,1)S(1)}, u32[]{:S(2)}, u32[]{:S(2)}) collective-permute-start(bf16[112,512]{1,0:T(8,128)(2,1)} %get-tuple-element.172), channel_id=1, source_target_pairs={{0,16},{1,17},{2,18},{3,19},{4,20},{5,21},{6,22},{7,23},{8,24},{9,... | collective-permute-start | bytes 344072 | tf_op jit(solution)/shard_map/ppermute | solution.py:113
  251.5 28.6 %collective-permute-start.10 = (bf16[80,512]{1,0:T(8,128)(2,1)}, bf16[80,512]{1,0:T(8,128)(2,1)S(1)}, u32[]{:S(2)}, u32[]{:S(2)}) collective-permute-start(bf16[80,512]{1,0:T(8,128)(2,1)} %get-tuple-element.173), channel_id=1, source_target_pairs={{0,30},{1,31},{2,16},{3,17},{4,18},{5,19},{6,20},{7,21},{8,22},{9,... | collective-permute-start | bytes 245768 | tf_op jit(solution)/shard_map/ppermute | solution.py:113
  293.2 31.5 %collective-permute-start.13 = (bf16[112,512]{1,0:T(8,128)(2,1)}, bf16[112,512]{1,0:T(8,128)(2,1)S(1)}, u32[]{:S(2)}, u32[]{:S(2)}) collective-permute-start(bf16[112,512]{1,0:T(8,128)(2,1)} %get-tuple-element.177), channel_id=1, source_target_pairs={{0,16},{1,17},{2,18},{3,19},{4,20},{5,21},{6,22},{7,23},{8,24},{9,... | collective-permute-start | bytes 344072 | tf_op jit(solution)/shard_map/ppermute | solution.py:113
  294.6 28.9 %collective-permute-start.14 = (bf16[80,512]{1,0:T(8,128)(2,1)}, bf16[80,512]{1,0:T(8,128)(2,1)S(1)}, u32[]{:S(2)}, u32[]{:S(2)}) collective-permute-start(bf16[80,512]{1,0:T(8,128)(2,1)} %get-tuple-element.178), channel_id=1, source_target_pairs={{0,30},{1,31},{2,16},{3,17},{4,18},{5,19},{6,20},{7,21},{8,22},{9,... | collective-permute-start | bytes 245768 | tf_op jit(solution)/shard_map/ppermute | solution.py:113
  314.0 27.7 %collective-permute-start.32 = (bf16[112,512]{1,0:T(8,128)(2,1)}, bf16[112,512]{1,0:T(8,128)(2,1)S(1)}, u32[]{:S(2)}, u32[]{:S(2)}) collective-permute-start(bf16[112,512]{1,0:T(8,128)(2,1)} %get-tuple-element.218), channel_id=1, source_target_pairs={{16,0},{17,1},{18,2},{19,3},{20,4},{21,5},{22,6},{23,7},{24,8},{25... | collective-permute-start | bytes 344072 | tf_op jit(solution)/shard_map/ppermute | solution.py:122
  336.5 32.5 %collective-permute-start.17 = (bf16[112,512]{1,0:T(8,128)(2,1)}, bf16[112,512]{1,0:T(8,128)(2,1)S(1)}, u32[]{:S(2)}, u32[]{:S(2)}) collective-permute-start(bf16[112,512]{1,0:T(8,128)(2,1)} %get-tuple-element.182), channel_id=1, source_target_pairs={{0,16},{1,17},{2,18},{3,19},{4,20},{5,21},{6,22},{7,23},{8,24},{9,... | collective-permute-start | bytes 344072 | tf_op jit(solution)/shard_map/ppermute | solution.py:113
  337.8 29.8 %collective-permute-start.18 = (bf16[80,512]{1,0:T(8,128)(2,1)}, bf16[80,512]{1,0:T(8,128)(2,1)S(1)}, u32[]{:S(2)}, u32[]{:S(2)}) collective-permute-start(bf16[80,512]{1,0:T(8,128)(2,1)} %get-tuple-element.183), channel_id=1, source_target_pairs={{0,30},{1,31},{2,16},{3,17},{4,18},{5,19},{6,20},{7,21},{8,22},{9,... | collective-permute-start | bytes 245768 | tf_op jit(solution)/shard_map/ppermute | solution.py:113
  419.4 153.2 %reduce-scatter.5.cloned.1.call-start = ((), (), s32[]{:S(2)}) async-start(), calls=%async_computation.8 | async-start | bytes 1966080 | tf_op jit(solution)/shard_map/reduce_scatter | solution.py:640
  426.9 170.4 %reduce-scatter.7.cloned.1.call-start = ((), (), s32[]{:S(2)}) async-start(), calls=%async_computation.9 | async-start | bytes 655360 | tf_op jit(solution)/shard_map/reduce_scatter | solution.py:640
  427.4 215.1 %reduce-scatter.11.cloned.1.call-start = ((), (), s32[]{:S(2)}) async-start(), calls=%async_computation.11 | async-start | bytes 2621440 | tf_op jit(solution)/shard_map/reduce_scatter | solution.py:640
  438.0 250.1 %reduce-scatter.9.cloned.1.call-start = ((), (), s32[]{:S(2)}) async-start(), calls=%async_computation.10 | async-start | bytes 2621440 | tf_op jit(solution)/shard_map/reduce_scatter | solution.py:640
  440.5 293.7 %all-reduce.7.cloned.1.call-start = ((), (), s32[]{:S(2)}) async-start(), calls=%async_computation.12 | async-start | bytes 3145728 | tf_op jit(solution)/shard_map/psum | solution.py:641
  449.6 99.2 %collective-permute-start.44 = (bf16[10,80,512]{2,1,0:T(8,128)(2,1)}, bf16[10,80,512]{2,1,0:T(8,128)(2,1)}, u32[]{:S(2)}, u32[]{:S(2)}) collective-permute-start(bf16[10,80,512]{2,1,0:T(8,128)(2,1)} %split.37), channel_id=1, source_target_pairs={{30,16},{31,17},{16,18},{17,19},{18,20},{19,21},{20,22},{21,23},{2... | collective-permute-start | bytes 2457608 | tf_op jit(solution)/shard_map/ppermute | solution.py:122
  457.6 91.2 %collective-permute-start.45 = (bf16[10,16,512]{2,1,0:T(8,128)(2,1)S(1)}, bf16[10,16,512]{2,1,0:T(8,128)(2,1)S(1)}, u32[]{:S(2)}, u32[]{:S(2)}) collective-permute-start(bf16[10,16,512]{2,1,0:T(8,128)(2,1)S(1)} %get-tuple-element.371), channel_id=1, source_target_pairs={{17,16},{16,17},{19,18},{18,19},{21,20},{20,21},{23,22},{22,23},{2... | collective-permute-start | bytes 491528 | tf_op jit(solution)/shard_map/ppermute | solution.py:122
  460.6 88.2 %collective-permute-start.46 = (bf16[10,16,512]{2,1,0:T(8,128)(2,1)S(1)}, bf16[10,16,512]{2,1,0:T(8,128)(2,1)S(1)}, u32[]{:S(2)}, u32[]{:S(2)}) collective-permute-start(bf16[10,16,512]{2,1,0:T(8,128)(2,1)S(1)} %get-tuple-element.372), channel_id=1, source_target_pairs={{31,16},{30,17},{17,18},{16,19},{19,20},{18,21},{21,22},{20,23},{2... | collective-permute-start | bytes 491528 | tf_op jit(solution)/shard_map/ppermute | solution.py:122
  552.8 137.5 %collective-permute-start.47 = (bf16[10,96,512]{2,1,0:T(8,128)(2,1)}, bf16[10,96,512]{2,1,0:T(8,128)(2,1)}, u32[]{:S(2)}, u32[]{:S(2)}) collective-permute-start(bf16[10,96,512]{2,1,0:T(8,128)(2,1)} %fusion.25), channel_id=1, source_target_pairs={{0,1},{1,0},{2,3},{3,2},{4,5},{5,4},{6,7},{7,6},{8,9},{9,8},{10,11... | collective-permute-start | bytes 2949128 | tf_op jit(solution)/shard_map/ppermute | solution.py:665
  (120 other events, 1354.2 us)
Sparse Core Ops, SparseCore 0:
  10.2 40.3 all-gather.4
  52.2 68.0 all-gather.6
  121.8 43.9 all-gather.8
  419.5 106.4 all-reduce.4
  528.9 43.7 reduce-scatter.4
  574.9 22.3 reduce-scatter.6
  599.7 42.8 reduce-scatter.10
  644.9 43.1 reduce-scatter.8
  691.5 42.7 all-reduce.6

commit v2 on v1

v2 whole, which is shorter than its diff:
```python
import functools

import jax
import jax.numpy as jnp
import numpy as np
from jax import lax
from jax.experimental import pallas as pl
from jax.experimental.pallas import tpu as pltpu
from jax.sharding import PartitionSpec as P

WIN = 7
SHIFT = 3
WCOLS = 8
WROWS = 2
TOKENS = WIN * WIN
SLOT = 64
GROUP = 4
AXES = ("section", "row", "mp")
EPS = 1e-05
BF = jnp.bfloat16
F32 = jnp.float32
NN = (((1,), (0,)), ((), ()))
NT = (((1,), (1,)), ((), ()))
TN = (((0,), (0,)), ((), ()))
VMEM_LIMIT = 56 * 1024 * 1024
highest = lax.Precision.HIGHEST


def mm(left, right, dims=NN):
    return lax.dot_general(left, right, dims, preferred_element_type=F32)


def up16(count):
    return -(-count // 16) * 16


def patch_place(row, col):
    return (col // WIN) * SLOT + row * WIN + col % WIN


class Tables:
    def __init__(self, wins):
        self.wins = wins
        self.rows = wins * SLOT
        cols = wins * WIN
        wide = range(SHIFT, cols)
        thin = range(SHIFT)
        low, high = range(SHIFT, WIN), range(SHIFT)
        pieces = [(low, wide), (high, wide), (low, thin), (high, thin)]
        self.sizes = [up16(len(a) * len(b)) for a, b in pieces]
        self.total = sum(self.sizes)
        pick = np.zeros((self.total, self.rows), np.float32)
        put = np.zeros((self.rows, self.total), np.float32)
        at = 0
        for (rows, columns), size in zip(pieces, self.sizes):
            spot = at
            for row in rows:
                for col in columns:
                    pick[spot, patch_place(row, col)] = 1
                    put[patch_place((row - SHIFT) % WIN, (col - SHIFT) % cols), spot] = 1
                    spot += 1
            at += size
        self.pick, self.put = pick, put


def pair_tables(wins):
    cols = wins * WIN
    tokens = WIN * cols
    keep = np.zeros((2, wins * SLOT, tokens), np.float32)
    take = np.zeros((2, wins * SLOT, up16(SHIFT * cols)), np.float32)
    send = np.zeros((up16(SHIFT * cols), tokens), np.float32)
    for seg in range(SHIFT):
        for col in range(cols):
            send[seg * cols + col, (2 * seg + 1) * cols + col] = 1
    for side in range(2):
        for row in range(WIN):
            for col in range(cols):
                place = patch_place(row, col)
                own = row <= SHIFT if side == 0 else row >= SHIFT
                if own:
                    seg = row if side == 0 else row - SHIFT
                    keep[side, place, 2 * seg * cols + col] = 1
                else:
                    seg = row - SHIFT - 1 if side == 0 else row
                    take[side, place, seg * cols + col] = 1
    return keep, take, send


class Layout:
    def __init__(self, row_count, mp_count):
        self.row_count, self.mp_count = row_count, mp_count
        self.across = mp_count // WROWS
        self.wins = WCOLS // self.across
        self.high = row_count * WROWS

    def device(self, section, window_row, place):
        window_row, place = window_row % self.high, place % self.across
        row = window_row // WROWS
        return (section * self.row_count + row) * self.mp_count + (window_row % WROWS) * self.across + place

    def route(self, source, target, up, back):
        return [
            (self.device(source, window_row, place), self.device(target, window_row - up, place - back))
            for window_row in range(self.high)
            for place in range(self.across)
        ]


HALO = ((0, 0), (1, 0), (0, 1), (1, 1))


def halo_swap(layout, parts):
    result = []
    for part, by in zip(parts, HALO):
        there = layout.route(0, 1, *by)
        result.append(lax.ppermute(part, AXES, there + [(b, a) for a, b in there]))
    return result


def halo_inside(layout, parts, back):
    result = [parts[0]]
    for part, by in zip(parts[1:], HALO[1:]):
        there = layout.route(1, 1, *by)
        result.append(lax.ppermute(part, AXES, [(b, a) for a, b in there] if back else there))
    return result


def ring(shard, axis, by=1):
    count = lax.axis_size(axis)
    return lax.ppermute(shard, axis, [(i, (i + by) % count) for i in range(count)])


def swap(shard, axis, bit):
    return lax.ppermute(shard, axis, [(i, i ^ bit) for i in range(lax.axis_size(axis))])


def natural_ring(shards, mp):
    stacked, count = jnp.stack(shards), len(shards)
    return jnp.stack([lax.dynamic_index_in_dim(stacked, (mp - j) % count, 0, keepdims=False) for j in range(count)])


def gather_quarter(quarter):
    held, crossed = [quarter], [swap(quarter, "row", 2)]
    for _ in range(lax.axis_size("mp") - 1):
        held.append(ring(held[-1], "mp"))
        crossed.append(swap(held[-1], "row", 2))
    mine = jnp.stack(held + crossed)
    return mine, swap(mine, "row", 1)


def take_at(array, index, axis=0):
    return lax.dynamic_index_in_dim(array, index, axis, keepdims=False)


def reduce_quarters(keep, send, row, mp):
    count = keep.shape[0]
    core, high = row % 2, row // 2
    part = keep + swap(send, "row", 1)
    part = take_at(part, high, 1) + swap(take_at(part, 1 - high, 1), "row", 2)
    total = take_at(part, (mp - 1) % count)
    for step in range(count - 1):
        total = ring(total, "mp") + take_at(part, (mp - 2 - step) % count)
    other = swap(total, "row", 2)
    pair = jnp.stack([jnp.where(high == 0, total, other), jnp.where(high == 0, other, total)])
    crossed = swap(pair, "row", 1)
    whole = jnp.stack([jnp.where(core == 0, pair, crossed), jnp.where(core == 0, crossed, pair)], axis=1)
    return whole.astype(F32).reshape((4,) + keep.shape[2:])


def sum_everywhere(array):
    for axis, bit in (("row", 1), ("row", 2), ("mp", 1), ("mp", 2)):
        array = array + swap(array, axis, bit)
    return array


def head_masks(dtype):
    lane = lax.broadcasted_iota(jnp.int32, (1, GROUP * 32), 1)
    return [jnp.where(lane // 32 == h, 1.0, 0.0).astype(dtype) for h in range(GROUP)]


def spread_heads(block, masks):
    return jnp.concatenate([block * mask for mask in masks], axis=0)


def fold_heads(tall, masks):
    total = tall[:SLOT] * masks[0]
    for h in range(1, GROUP):
        total = total + tall[h * SLOT : (h + 1) * SLOT] * masks[h]
    return total


def centre(values):
    middle = jnp.mean(values, axis=-1, keepdims=True)
    centred = values - middle
    scale = lax.rsqrt(jnp.mean(centred * centred, axis=-1, keepdims=True) + EPS)
    return centred * scale, scale


KEPT = ("gp", "mid", "qkv", "prob", "x")
WEIGHTS = ("wq", "wo", "w1", "w2")


class Refs:
    pass


class Copies:
    def __init__(self, sems):
        self.sems, self.used, self.sent = sems, 0, []

    def sem(self):
        self.used += 1
        return self.sems.at[self.used - 1]

    def ship(self, src, dst):
        copy = pltpu.make_async_copy(src, dst, self.sem())
        copy.start()
        self.sent.append(copy)

    def finish(self):
        for copy in self.sent:
            copy.wait()


def arrival(target, sem):
    return pltpu.make_async_copy(target, target, sem)


def load_weights(k, kinds, held, offsets):
    waits = {}
    shards = k.w1.shape[0]
    for name in kinds:
        kind, target, sem = WEIGHTS.index(name), getattr(k, name), k.copies.sem()
        waits[name] = arrival(target, sem)
        if held == 1:
            pltpu.make_async_copy(getattr(k, name + "_0"), target, sem).start()
            continue
        flat = len(target.shape) == 2
        high = target.shape[-2] // (4 * shards if flat else 4)
        for core in range(2):
            source = getattr(k, f"{name}_{core}")
            for piece in range(2 * shards):
                quarter = k.sec[1] ^ (core + 2 * (piece // shards))
                shard = lax.rem(k.sec[2] + (shards - piece % shards), shards)
                start = quarter * high
                if flat:
                    start = start + shard * (4 * high)
                rows = pl.ds(pl.multiple_of(start, high), high)
                place = target.at[rows, :] if flat else target.at[shard, rows, :]
                pltpu.make_async_copy(source.at[piece, pl.ds(offsets[kind], high), :], place, sem).start()
    return waits


def window_rows(w):
    return slice(w * SLOT, (w + 1) * SLOT)


def forward_part(k, wins, waits):
    x, qkv, prob, mid, gp = (k.x.at[0], k.qkv.at[0], k.prob.at[0], k.mid.at[0], k.gp.at[0])
    ship = k.copies.ship
    tables = []
    for name in ("bias", "region"):
        copy = pltpu.make_async_copy(getattr(k, name + "_h"), getattr(k, name), k.copies.sem())
        copy.start()
        tables.append(copy)

    @pl.when(k.sec[0] == 0)
    def _():
        x[...] = k.pin[0]

    @pl.when(k.sec[0] == 1)
    def _():
        joined = jnp.concatenate([k.p_main[...], k.p_row[...], k.p_col[...], k.p_cor[...]], axis=0)
        x[...] = mm(k.put[...], joined).astype(BF)

    for w in range(wins):
        rows = window_rows(w)
        hat, _ = centre(x[rows, :].astype(F32))
        k.a[rows, :] = (hat * k.vec[0:1, :] + k.vec[1:2, :]).astype(BF)
    ship(x, k.x_o)
    ship(k.a, k.a_o)
    waits["wq"].wait()
    lane = lax.broadcasted_iota(jnp.int32, (1, 3 * GROUP * 32), 1)
    factor = jnp.where(lane < GROUP * 32, 32 ** (-0.5), 1.0)
    for g in range(4):
        pr = mm(k.a[...], k.wq[g]) + k.bq[g : g + 1, :]
        qkv[:, g * 384 : (g + 1) * 384] = (pr * factor).astype(BF)
    ship(qkv, k.qkv_o)
    for copy in tables:
        copy.wait()
    masks, masks_f = head_masks(BF), head_masks(F32)
    for w in range(wins):
        rows = window_rows(w)
        for g in range(4):
            query = qkv[rows, g * 384 : g * 384 + 128]
            key = qkv[rows, g * 384 + 128 : g * 384 + 256]
            value = qkv[rows, g * 384 + 256 : g * 384 + 384]
            scores = mm(key, spread_heads(query, masks), NT) + k.bias[g] + k.region[w]
            top = jnp.max(scores, axis=0, keepdims=True)
            e = jnp.exp(scores - top)
            low = (e * (1.0 / jnp.sum(e, axis=0, keepdims=True))).astype(BF)
            prob[rows, g * 256 : (g + 1) * 256] = low
            k.ctx[rows, g * 128 : (g + 1) * 128] = fold_heads(mm(low, value, TN), masks_f).astype(BF)
    ship(prob, k.prob_o)
    ship(k.ctx, k.ctx_o)
    waits["wo"].wait()
    mid[...] = x[...].astype(F32) + (mm(k.ctx[...], k.wo[...]) + k.vec[2:3, :])
    ship(mid, k.mid_o)
    for w in range(wins):
        rows = window_rows(w)
        hat, _ = centre(mid[rows, :])
        k.n2[rows, :] = (hat * k.vec[3:4, :] + k.vec[4:5, :]).astype(BF)
    ship(k.n2, k.n2_o)
    waits["w1"].wait()
    waits["w2"].wait()
    parts, _, width = k.w1.shape
    total = mid[...] + k.vec[5:6, :]
    for j in range(parts):
        cols = slice(j * width, (j + 1) * width)
        hidden = mm(k.n2[...], k.w1[j]) + k.b1[j : j + 1, :]
        phi = 0.5 + 0.5 * lax.erf(hidden * 0.7071067811865476)
        act = (hidden * phi).astype(BF)
        k.act[:, cols] = act
        gp[:, cols] = (phi + hidden * (jnp.exp(hidden * hidden * -0.5) * 0.3989422804014327)).astype(BF)
        ship(k.act.at[:, cols], k.act_o.at[:, cols])
        ship(gp.at[:, cols], k.gp_o.at[:, cols])
        total = total + mm(act, k.w2[j])
    k.y[...] = total.astype(BF)
    ship(k.y, k.y_o)


def put_pieces(refs, joined):
    at = 0
    for ref in refs:
        ref[...] = joined[at : at + ref.shape[0]]
        at += ref.shape[0]


def norm_back(grad, hat, scale, gain):
    inner = grad * gain
    return scale * (inner - jnp.mean(inner, axis=-1, keepdims=True) - hat * jnp.mean(inner * hat, axis=-1, keepdims=True))


def column_sum(values):
    return jnp.sum(values, axis=0, keepdims=True)


def backward_start(k, names):
    waits = {}
    for name in names:
        copy = pltpu.make_async_copy(getattr(k, "old_" + name), getattr(k, name).at[1], k.copies.sem())
        pl.when(k.sec[0] == 0)(copy.start)
        waits[name] = lambda copy=copy: pl.when(k.sec[0] == 0)(copy.wait)
    return waits


def backward_mlp(k, wins, waits, olds):
    slot = 1 - k.sec[0]
    gp, mid = k.gp.at[slot], k.mid.at[slot]
    ship = k.copies.ship

    @pl.when(k.sec[0] == 0)
    def _():
        joined = jnp.concatenate([k.p_main[...], k.p_row[...], k.p_col[...], k.p_cor[...]], axis=0)
        k.g[...] = mm(k.pick[...], joined, TN).astype(BF)

    @pl.when(k.sec[0] == 1)
    def _():
        joined = jnp.concatenate([k.c_main[0], k.c_row[0], k.c_col[0], k.c_cor[0]], axis=0)
        k.g[...] = mm(k.put[...], joined).astype(BF)

    ship(k.g, k.g_o)
    parts, _, width = k.w1.shape
    waits["w2"].wait()
    waits["w1"].wait()
    olds["gp"]()
    total = None
    for j in range(parts):
        cols = slice(j * width, (j + 1) * width)
        dh = (mm(k.g[...], k.w2[j], NT) * gp[:, cols].astype(F32)).astype(BF)
        k.dh[:, cols] = dh
        k.small[0:1, cols] = column_sum(dh.astype(F32))
        ship(k.dh.at[:, cols], k.dh_o.at[:, cols])
        part = mm(dh, k.w1[j], NT)
        total = part if total is None else total + part
    k.dn[...] = total
    olds["mid"]()
    sums = [0.0] * 4
    for w in range(wins):
        rows = window_rows(w)
        grad = k.dn[rows, :]
        out = k.g[rows, :].astype(F32)
        hat, scale = centre(mid[rows, :])
        result = out + norm_back(grad, hat, scale, k.vec[3:4, :])
        k.dmid[rows, :] = result
        low = result.astype(BF)
        k.gm[rows, :] = low
        for i, term in enumerate((out, low.astype(F32), grad * hat, grad)):
            sums[i] = sums[i] + column_sum(term)
    ship(k.gm, k.gm_o)
    k.small[1:2, 0:512], k.small[1:2, 512:1024] = sums[0], sums[1]
    k.small[2:3, 0:512], k.small[2:3, 512:1024] = sums[2], sums[3]


def backward_attention(k, wins, waits, olds):
    slot = 1 - k.sec[0]
    qkv, prob, x = k.qkv.at[slot], k.prob.at[slot], k.x.at[slot]
    ship = k.copies.ship
    waits["wo"].wait()
    k.dctx[...] = mm(k.gm[...], k.wo[...], NT).astype(BF)
    olds["qkv"]()
    olds["prob"]()
    masks, masks_f = head_masks(BF), head_masks(F32)
    for w in range(wins):
        rows = window_rows(w)
        for g in range(4):
            at = g * 384
            query = qkv[rows, at : at + 128]
            key = qkv[rows, at + 128 : at + 256]
            value = qkv[rows, at + 256 : at + 384]
            do = spread_heads(k.dctx[rows, g * 128 : (g + 1) * 128], masks)
            low = prob[rows, g * 256 : (g + 1) * 256]
            p = low.astype(F32)
            dp = mm(value, do, NT)
            ds = (p * (dp - column_sum(p * dp))).astype(BF)
            if w == 0:
                k.dbias[:, g * 256 : (g + 1) * 256] = ds.astype(F32)
            else:
                k.dbias[:, g * 256 : (g + 1) * 256] += ds.astype(F32)
            dv = mm(low, do).astype(BF)
            dk = mm(ds, spread_heads(query, masks)).astype(BF)
            dq = (fold_heads(mm(ds, key, TN), masks_f) * 32 ** (-0.5)).astype(BF)
            k.dqkv[rows, at : at + 128] = dq
            k.dqkv[rows, at + 128 : at + 256] = dk
            k.dqkv[rows, at + 256 : at + 384] = dv
    ship(k.dqkv, k.dqkv_o)
    ship(k.dbias, k.dbias_o)
    waits["wq"].wait()
    total = None
    for g in range(4):
        part = k.dqkv[:, g * 384 : (g + 1) * 384]
        k.small[3:4, g * 384 : (g + 1) * 384] = column_sum(part.astype(F32))
        part = mm(part, k.wq[g], NT)
        total = part if total is None else total + part
    k.dn[...] = total
    olds["x"]()
    sums = [0.0] * 2
    for w in range(wins):
        rows = window_rows(w)
        grad = k.dn[rows, :]
        hat, scale = centre(x[rows, :].astype(F32))
        k.dx[rows, :] = (k.dmid[rows, :] + norm_back(grad, hat, scale, k.vec[0:1, :])).astype(BF)
        sums[0] = sums[0] + column_sum(grad * hat)
        sums[1] = sums[1] + column_sum(grad)
    ship(k.dx, k.dx_o)
    k.small[1:2, 1024:1536], k.small[1:2, 1536:2048] = sums


def step_kernel(wins, held, offsets, ahead, back, k):
    k.copies = Copies(k.sems)
    waits = load_weights(k, WEIGHTS if ahead else WEIGHTS[::-1], held, offsets)
    if back:
        olds = backward_start(k, KEPT)
    sends = [k.s_main, k.s_row, k.s_col, k.s_cor] if ahead else []
    if ahead:
        forward_part(k, wins, waits)

        @pl.when(k.sec[0] == 0)
        def _():
            put_pieces(sends, mm(k.pick[...], k.y[...]).astype(BF))

        @pl.when(k.sec[0] == 1)
        def _():
            k.unroll[...] = mm(k.put[...], k.y[...], TN).astype(BF)
            if not back:
                for ref in sends:
                    ref[...] = jnp.zeros_like(ref)

    if back:
        if ahead:
            waits = {name: Done() for name in WEIGHTS}
        k.small[...] = jnp.zeros_like(k.small)
        backward_mlp(k, wins, waits, olds)
        backward_attention(k, wins, waits, olds)
        if ahead:

            @pl.when(k.sec[0] == 1)
            def _():
                put_pieces(sends, mm(k.put[...], k.dx[...], TN).astype(BF))

    k.copies.finish()


class Done:
    def wait(self):
        pass


SMEM_SPEC = pl.BlockSpec(memory_space=pltpu.SMEM)
HBM_SPEC = pl.BlockSpec(memory_space=pl.ANY)
VMEM_SPEC = pl.BlockSpec(memory_space=pltpu.VMEM)


def shape_of(rows, cols, dtype=BF):
    return jax.ShapeDtypeStruct((rows, cols), dtype)


def call(kernel, name, ins, outs, scratch, flops, moved):
    names = list(ins) + list(outs) + list(scratch)

    def wrapped(*refs):
        k = Refs()
        for key, ref in zip(names, refs):
            setattr(k, key, ref)
        kernel(k)

    results = pl.pallas_call(
        wrapped,
        grid=(1,),
        out_shape=[shape for shape, _ in outs.values()],
        in_specs=[spec for _, spec in ins.values()],
        out_specs=[spec for _, spec in outs.values()],
        scratch_shapes=list(scratch.values()),
        compiler_params=pltpu.CompilerParams(vmem_limit_bytes=VMEM_LIMIT),
        cost_estimate=pl.CostEstimate(flops=flops, bytes_accessed=moved, transcendentals=0),
        name=name,
    )(*[array for array, _ in ins.values()])
    return dict(zip(outs, results))


PIECES = ("main", "row", "col", "cor")


def run_step(tables, static, landed, ahead=None, back=None):
    sources, offsets, shapes = static["weights"]
    rows, wide = tables.rows, shapes[2][0] * shapes[2][2]
    vmem = lambda array: (array, VMEM_SPEC)
    hbm = lambda array: (array, HBM_SPEC)
    one = lambda array, index: (array, pl.BlockSpec((1,) + array.shape[1:], lambda i: (index, 0, 0)))
    ins = {"sec": (static["sec"], SMEM_SPEC), "put": vmem(static["put"]), "pick": vmem(static["pick"]), "vec": vmem(static["vec"])}
    for name, piece in zip(PIECES, landed):
        ins["p_" + name] = vmem(piece)
    for core, source in enumerate(sources):
        for name, array in zip(WEIGHTS, source):
            ins[f"{name}_{core}"] = hbm(array)
    outs = {}
    scratch = {name: pltpu.VMEM(shape, BF) for name, shape in zip(WEIGHTS, shapes)}
    widths = {"gp": (wide, BF), "mid": (512, F32), "qkv": (1536, BF), "prob": (1024, BF), "x": (512, BF)}
    for name, (cols, dtype) in widths.items():
        scratch[name] = pltpu.VMEM((2, rows, cols), dtype)
    local = {}
    if ahead is not None:
        ins["pin"] = one(static["pin"], ahead)
        ins["bq"], ins["b1"] = vmem(static["bq"]), vmem(static["b1"])
        for name in ("bias", "region"):
            ins[name + "_h"] = hbm(static[name])
            scratch[name] = pltpu.VMEM(static[name].shape, F32)
        for name, size in zip(PIECES, tables.sizes):
            outs["s_" + name] = (shape_of(size, 512), VMEM_SPEC)
        outs["unroll"] = (shape_of(tables.total, 512), VMEM_SPEC)
        for name, (cols, dtype) in widths.items():
            outs[name + "_o"] = (shape_of(rows, cols, dtype), HBM_SPEC)
        local |= {"a": (512, BF), "ctx": (512, BF), "n2": (512, BF), "act": (wide, BF), "y": (512, BF)}
    if back is not None:
        index, old = back
        for name, target in zip(PIECES, static["targets"]):
            ins["c_" + name] = one(target, index)
        for name in KEPT:
            ins["old_" + name] = hbm(old[name + "_o"])
        outs["small"] = (shape_of(8, 2048, F32), VMEM_SPEC)
        local |= {"g": (512, BF), "dh": (wide, BF), "gm": (512, BF), "dqkv": (1536, BF), "dx": (512, BF)}
        for name, cols, dtype in (("dmid", 512, F32), ("dn", 512, F32), ("dctx", 512, BF)):
            scratch[name] = pltpu.VMEM((rows, cols), dtype)
        outs["dbias_o"] = (shape_of(SLOT, 1024, F32), HBM_SPEC)
        scratch["dbias"] = pltpu.VMEM((SLOT, 1024), F32)
    for name, (cols, dtype) in local.items():
        outs[name + "_o"] = (shape_of(rows, cols, dtype), HBM_SPEC)
        scratch[name] = pltpu.VMEM((rows, cols), dtype)
    scratch["sems"] = pltpu.SemaphoreType.DMA((96,))
    passes = 2 * (ahead is not None) + 4 * (back is not None)
    kernel = functools.partial(step_kernel, tables.wins, len(sources), offsets, ahead is not None, back is not None)
    return call(kernel, "layer_step", ins, outs, scratch, passes * rows * 3145728, 12_000_000)


def weight_grad_kernel(batches, first_slots, terms, quartered, k):
    k.copies = Copies(k.sems)
    waits = []
    for name in dict.fromkeys(name for term in terms for name in term[:2]):
        target, sem = getattr(k, name), k.copies.sem()
        rows = target.shape[0] // batches
        shift = first_slots[name]
        for section in range(2):
            for batch in range(batches):
                source = getattr(k, f"{name}_{batch + shift[section]}")
                copy = pltpu.make_async_copy(source, target.at[pl.ds(batch * rows, rows), :], sem)
                pl.when(k.sec[0] == section)(copy.start)
        waits.append((name, arrival(target, sem)))
    waits = dict(waits)
    for left, right, side, target, first, rows in terms:
        for name in (left, right):
            waits.pop(name, Done()).wait()
        l, r, t = getattr(k, left), getattr(k, right), getattr(k, target)
        parts = t.shape[0]
        for part in range(parts):
            if side == "left":
                width = l.shape[1] // parts
                value = mm(l[:, part * width : (part + 1) * width], r[...], TN)
            else:
                width = r.shape[1] // parts
                value = mm(l[...], r[:, part * width : (part + 1) * width], TN)
            t[part, first : first + rows, :] = value.astype(BF)
    targets = list(dict.fromkeys(term[3] for term in terms))
    if not quartered:
        for name in targets:
            k.copies.ship(getattr(k, name), getattr(k, name + "_o"))
        k.copies.finish()
        return
    sem = k.copies.sem()
    at = 0
    for name in targets:
        target = getattr(k, name)
        high = target.shape[1] // 4
        for quarter in range(4):
            source = target.at[:, pl.ds(quarter * high, high), :]
            for core in range(2):
                result = k.keep if quarter % 2 == core else k.send
                copy = pltpu.make_async_copy(source, result.at[:, quarter // 2, pl.ds(at, high), :], sem)
                pl.when(lax.rem(k.sec[1], 2) == core)(copy.start)
        at += high
    for result in (k.keep, k.send):
        arrival(result, sem).wait()


def run_weight_grad(static, batches, slots, first_slots, terms, shapes, quartered):
    ins = {"sec": (static["sec"], SMEM_SPEC)}
    scratch = {}
    for name, members in slots.items():
        for i, member in enumerate(members):
            ins[f"{name}_{i}"] = (member, HBM_SPEC)
        scratch[name] = pltpu.VMEM((batches * members[0].shape[0], members[0].shape[1]), BF)
    for name, shape in shapes.items():
        scratch[name] = pltpu.VMEM(shape, BF)
    if quartered:
        parts, cols = next(iter(shapes.values()))[::2]
        shape = jax.ShapeDtypeStruct((parts, 2, sum(shape[1] for shape in shapes.values()) // 4, cols), BF)
        outs = {"keep": (shape, HBM_SPEC), "send": (shape, HBM_SPEC)}
    else:
        outs = {name + "_o": (jax.ShapeDtypeStruct(shape, BF), HBM_SPEC) for name, shape in shapes.items()}
    scratch["sems"] = pltpu.SemaphoreType.DMA((16,))
    rows = batches * next(iter(slots.values()))[0].shape[0]
    flops = 2 * rows * sum(int(np.prod(shape)) for shape in shapes.values())
    kernel = functools.partial(weight_grad_kernel, batches, first_slots, terms, quartered)
    return call(kernel, "weight_grad", ins, outs, scratch, flops, 20_000_000)


def table_onehot():
    code = np.full((SLOT, SLOT), -1, np.int32)
    for u in range(TOKENS):
        for t in range(TOKENS):
            code[u, t] = (t // WIN - u // WIN + WIN - 1) * (2 * WIN - 1) + t % WIN - u % WIN + WIN - 1
    side = (2 * WIN - 1) ** 2
    return (jnp.arange(side, dtype=jnp.int32)[:, None] == jnp.asarray(code.reshape(1, -1))).astype(F32)


def region_mask(layout, section):
    row, mp = lax.axis_index("row"), lax.axis_index("mp")
    window_row = row * WROWS + mp // layout.across
    window_col = (mp % layout.across) * layout.wins + jnp.arange(layout.wins)
    place = jnp.arange(SLOT)
    row_label = jnp.where(window_row == layout.high - 1, 1 + (place // WIN >= WIN - SHIFT).astype(jnp.int32), 0)
    col_label = jnp.where(
        (window_col == WCOLS - 1)[:, None], 1 + (place % WIN >= WIN - SHIFT).astype(jnp.int32)[None], 0
    )
    labels = 3 * row_label[None] + col_label
    differs = labels[:, :, None] != labels[:, None, :]
    term = jnp.where(differs & (section == 1), -100.0, 0.0).astype(F32)
    return jnp.tile(term, (1, 1, GROUP))


def full_patches(layout, mp, tokens):
    wins = layout.wins
    place = jnp.arange(wins * SLOT)
    window, inner = place // SLOT, place % SLOT
    row = (mp // layout.across) * WIN + inner // WIN
    col = ((mp % layout.across) * wins + window) * WIN + inner % WIN
    token = jnp.where(inner < TOKENS, row * (WCOLS * WIN) + col, -1)
    return (token[:, None] == jnp.arange(tokens)[None]).astype(BF)


def whole_patches(layout, mp, tokens_here):
    token = mp * tokens_here + jnp.arange(tokens_here)
    row, col = token // (WCOLS * WIN), token % (WCOLS * WIN)
    window = col // WIN
    owner = (row // WIN) * layout.across + window // layout.wins
    place = owner * layout.wins * SLOT + (window % layout.wins) * SLOT + (row % WIN) * WIN + col % WIN
    return (place[:, None] == jnp.arange(layout.mp_count * layout.wins * SLOT)[None]).astype(BF)


def low_dot(matrix, stack):
    return jnp.einsum("pr,nrd->npd", matrix, stack, preferred_element_type=F32).astype(BF)


def body(
    layer_input,
    out_cotangent,
    norm_one_gain,
    norm_one_bias,
    attend_weight,
    attend_bias,
    position_table,
    output_weight,
    output_bias,
    norm_two_gain,
    norm_two_bias,
    expand_weight,
    expand_bias,
    reduce_weight,
    reduce_bias,
):
    row_count, mp_count = lax.axis_size("row"), lax.axis_size("mp")
    section, mp = lax.axis_index("section"), lax.axis_index("mp")
    layout = Layout(row_count, mp_count)
    tables = Tables(layout.wins)
    put = jnp.asarray(tables.put, BF)
    pick = jnp.asarray(tables.pick, BF)
    batches, tokens_here, width = layer_input.shape
    heads_here = attend_weight.shape[2]
    hidden_here = expand_weight.shape[2]
    row = lax.axis_index("row")
    sec = jnp.stack([section, row, mp]).astype(jnp.int32)
    paired = layout.across == 2 and row_count == 4
    first = section == 0

    flat = jnp.concatenate([attend_bias[0].reshape(-1), position_table[0].reshape(-1), expand_bias[0].reshape(-1)])
    if paired:
        quarter = lambda array: take_at(array.reshape((4, -1) + array.shape[1:]), row)
        one = quarter(attend_weight[0]).reshape(-1, GROUP, 3, 32).transpose(0, 2, 1, 3).reshape(-1, GROUP * 96)
        two = jnp.concatenate([quarter(output_weight[0].reshape(-1, width)), quarter(expand_weight[0]), quarter(reduce_weight[0])])
        held = [flat]
        for _ in range(mp_count - 1):
            held.append(ring(held[-1], "mp"))
        flat_all = natural_ring(held, mp)
        one, two = gather_quarter(one), gather_quarter(two)
        high_o, high_1 = heads_here * 8, width // 4
        weights = (
            [(one[i], two[i], two[i], two[i]) for i in range(2)],
            (0, 0, high_o, high_o + high_1),
            ((4, width, GROUP * 96), (4 * GROUP * 32, width), (mp_count, width, hidden_here), (mp_count, hidden_here, width)),
        )
    else:
        wq_all = lax.all_gather(attend_weight[0], "mp", axis=0)
        wq_all = wq_all.transpose(1, 0, 2, 3).reshape(width, 4, GROUP, 3, 32).transpose(1, 0, 3, 2, 4).reshape(4, width, GROUP * 96)
        wo_all = lax.all_gather(output_weight[0], "mp", axis=0).reshape(-1, width)
        w1_all = lax.all_gather(expand_weight[0], "mp", axis=0)
        w2_all = lax.all_gather(reduce_weight[0], "mp", axis=0)
        flat_all = lax.all_gather(flat, "mp", axis=0)
        whole = (wq_all, wo_all, w1_all, w2_all)
        weights = ([whole], (0, 0, 0, 0), tuple(array.shape for array in whole))
    cut_one = heads_here * 64
    cut_two = cut_one + heads_here * position_table.shape[2]
    bias_all = flat_all[:, :cut_one].reshape(4, GROUP, 2, 32)
    table_all = flat_all[:, cut_one:cut_two].reshape(-1, position_table.shape[2])
    b1 = flat_all[:, cut_two:]
    bq = jnp.stack([bias_all[:, :, 0], jnp.zeros_like(bias_all[:, :, 0]), bias_all[:, :, 1]], axis=1).reshape(4, -1)
    onehot = table_onehot()
    bias = jnp.dot(table_all, onehot, precision=highest).reshape(4, GROUP, SLOT, SLOT).transpose(0, 2, 1, 3)
    bias = bias.reshape(4, SLOT, GROUP * SLOT) + jnp.where(jnp.arange(SLOT) < TOKENS, 0.0, -1e30)[None, :, None]
    vec = jnp.concatenate(
        [norm_one_gain, norm_one_bias, output_bias, norm_two_gain, norm_two_bias, reduce_bias, jnp.zeros((2, width), F32)]
    )
    region = region_mask(layout, section)

    taken = jnp.where(first, layer_input, out_cotangent)
    if paired:
        keep, take, send = pair_tables(layout.wins)
        side = mp % 2
        keep = lax.dynamic_index_in_dim(jnp.asarray(keep, BF), side, 0, keepdims=False)
        take = lax.dynamic_index_in_dim(jnp.asarray(take, BF), side, 0, keepdims=False)
        send = jnp.asarray(send, BF)
        arrived = swap(low_dot(send, taken), "mp", 1)
        pin = low_dot(jnp.concatenate([keep, take], axis=1), jnp.concatenate([taken, arrived], axis=1))
    else:
        everything = lax.all_gather(taken, "mp", axis=1, tiled=True)
        pin = low_dot(full_patches(layout, mp, everything.shape[1]), everything)
    cuts = np.cumsum(tables.sizes)[:-1].tolist()
    targets = halo_inside(layout, jnp.split(low_dot(pick, pin), cuts, axis=1), False)

    static = dict(
        sec=sec, weights=weights, pin=pin, targets=targets, put=put, pick=pick, vec=vec, bq=bq, b1=b1, bias=bias, region=region
    )
    landed = [jnp.zeros((size, width), BF) for size in tables.sizes]
    steps = []
    for step in range(batches + 2):
        ahead = min(step, batches - 1) if step <= batches else None
        back = (min(step - 1, batches - 1), steps[max(step - 2, 0)]) if step else None
        done = run_step(tables, static, landed, ahead, back)
        steps.append(done)
        if step <= batches:
            landed = halo_swap(layout, [done["s_" + name] for name in PIECES])

    ahead_slots, back_slots = (0, 1), (1, 0)
    column = lambda name: [done[name + "_o"] for done in (steps[:-1] if name in ("act", "n2", "a", "ctx") else steps[1:])]
    where = {name: ahead_slots if name in ("act", "n2", "a", "ctx") else back_slots for name in ("act", "n2", "a", "ctx", "g", "dh", "gm", "dqkv")}
    gradient = lambda names, terms, shapes: run_weight_grad(
        static, batches, {name: column(name) for name in names}, where, terms, shapes, paired
    )
    mlp = gradient(
        ("act", "g", "n2", "dh"),
        (("act", "g", "left", "d2", 0, hidden_here), ("n2", "dh", "right", "d1", 0, width)),
        {"d2": (mp_count, hidden_here, width), "d1": (mp_count, width, hidden_here)},
    )
    heads = gradient(
        ("dqkv", "a", "ctx", "gm"),
        (("dqkv", "a", "left", "da", 0, GROUP * 96), ("ctx", "gm", "left", "da", GROUP * 96, GROUP * 32)),
        {"da": (4, GROUP * 128, width)},
    )
    if paired:
        both = reduce_quarters(mlp["keep"], mlp["send"], row, mp)
        d2 = both[:, : hidden_here // 4].reshape(hidden_here, width)
        d1 = both[:, hidden_here // 4 :].reshape(width, hidden_here)
        da = reduce_quarters(heads["keep"], heads["send"], row, mp).reshape(GROUP * 128, width)
        dq, do = da[: GROUP * 96].reshape(3, GROUP, 32, width), da[GROUP * 96 :]
        dq = dq.transpose(3, 1, 0, 2).reshape(attend_weight.shape[1:])
    else:

        def shared(parts):
            part = lax.psum_scatter(parts, "mp", scatter_dimension=0, tiled=False)
            return lax.psum(part, "row").astype(F32)

        da = heads["da_o"]
        dq = da[:, : GROUP * 96].reshape(4, 3, GROUP, 32, width).transpose(0, 2, 1, 3, 4).reshape(mp_count, heads_here * 96, width)
        d2, d1, do = shared(mlp["d2_o"]), shared(mlp["d1_o"]), shared(da[:, GROUP * 96 :].reshape(mp_count, heads_here * 32, width))
        dq = shared(dq).T.reshape(attend_weight.shape[1:])
    pick_slots = lambda values: sum(jnp.where(first, values[i + 1], values[i]) for i in range(batches))
    small = pick_slots([done["small"] for done in steps[1:]])
    table = pick_slots([done["dbias_o"] for done in steps[1:]]).reshape(SLOT, 4 * GROUP, SLOT).transpose(1, 0, 2).reshape(4 * GROUP, -1)
    table = jnp.dot(table, onehot.T, precision=highest)
    if paired:
        count = table.size
        table = jnp.pad(table.reshape(-1), (0, -count % 2048)).reshape(-1, 2048)
        both = sum_everywhere(jnp.concatenate([small, table]))
        small, table = both[: small.shape[0]], both[small.shape[0] :].reshape(-1)[:count].reshape(4 * GROUP, -1)
    else:
        small, table = lax.psum((small, table), ("row", "mp"))
    shift = small[3, :1536].reshape(4, 3, GROUP, 32)
    shift = jnp.concatenate([shift[:, 0], shift[:, 2]], axis=-1).reshape(4 * GROUP, 64)
    mine = lambda array: lax.dynamic_index_in_dim(array.reshape((mp_count, -1) + array.shape[1:]), mp, 0, keepdims=False)

    stack = jnp.stack([done["y_o"] for done in steps[:batches]] + [done["dx_o"] for done in steps[2:]])
    mine_y = [jnp.split(done["unroll"], cuts) for done in steps[1 : batches + 1]]
    mine_dx = [[done["s_" + name] for name in PIECES] for done in steps[1 : batches + 1]]
    parts = [jnp.stack([member[i] for member in mine_y + mine_dx]) for i in range(4)]
    unrolled = low_dot(pick.T, jnp.concatenate(halo_inside(layout, parts, True), axis=1))
    patches = jnp.where(first, stack, unrolled)
    if paired:
        arrived = swap(low_dot(take.T, patches), "mp", 1)
        placed = low_dot(jnp.concatenate([keep.T, send.T], axis=1), jnp.concatenate([patches, arrived], axis=1))
    else:
        everything = lax.all_gather(patches, "mp", axis=1, tiled=True)
        placed = low_dot(whole_patches(layout, mp, tokens_here), everything)

    return (
        placed[:batches][None],
        placed[batches:].astype(F32)[None],
        small[1, 1024:1536][None],
        small[1, 1536:2048][None],
        dq[None],
        mine(shift)[None],
        mine(table)[None],
        do.reshape(output_weight.shape),
        small[1, 512:1024][None],
        small[2, 0:512][None],
        small[2, 512:1024][None],
        d1[None],
        mine(small[0])[None],
        d2[None],
        small[1, 0:512][None],
    )


def solution(mesh):
    return jax.shard_map(
        body,
        mesh=mesh,
        in_specs=(
            P(None, ("row", "mp"), None),
            P(None, ("row", "mp"), None),
            P("section", None),
            P("section", None),
            P("section", None, "mp", None),
            P("section", "mp", None),
            P("section", "mp", None),
            P("section", "mp", None, None),
            P("section", None),
            P("section", None),
            P("section", None),
            P("section", None, "mp"),
            P("section", "mp"),
            P("section", "mp", None),
            P("section", None),
        ),
        out_specs=(
            P("section", None, ("row", "mp"), None),
            P("section", None, ("row", "mp"), None),
            P("section", None),
            P("section", None),
            P("section", None, "mp", None),
            P("section", "mp", None),
            P("section", "mp", None),
            P("section", "mp", None, None),
            P("section", None),
            P("section", None),
            P("section", None),
            P("section", None, "mp"),
            P("section", "mp"),
            P("section", "mp", None),
            P("section", None),
        ),
        check_vma=False,
    )
```

time: 759 us -> 439 us (0.58)
  waiting for transfers between devices: 252 us -> 91.2 us
  blocking collectives: 123 us -> 0 us
  Pallas kernels: 172 us -> 130 us
  local copies, waits for them, and re-layouts: 31.4 us -> 71.3 us
  between operations: 17 us -> 2.81 us
  starting transfers between devices: 116 us -> 108 us
    reduce_scatter x4 -> x0, waiting for transfers between devices: 130 us -> none  [shared(): part = lax.psum_scatter(parts, 'mp', scatter_dimension=0, tiled=False)]
    ppermute x48 -> x69, waiting for transfers between devices: 3.51 us -> 91.2 us  [the longest x24 54.1 us: swap(): lax.ppermute(shard, axis, [(i, i ^ bit) for i in range(lax.axis_size(axis...]
    psum x1 -> x0, blocking collectives: 82.6 us -> none  [body(): small, table = lax.psum((small, table), ('row', 'mp'))]
    all_gather x3 -> x0, waiting for transfers between devices: 80.3 us -> none  [the longest x1 45.5 us: body(): w2_all = lax.all_gather(reduce_weight[0], 'mp', axis=0)]
    pallas_call x14 -> x9, Pallas kernels: 172 us -> 130 us  [call(): pl.pallas_call(wrapped, grid=(1,), out_shape=[shape for shape, _ in outs....]
    psum x2 -> x0, waiting for transfers between devices: 36.8 us -> none  [the longest x1 36.8 us: shared(): return lax.psum(part, 'row').astype(F32)]
    unnamed x178 -> x239, local copies, waits for them, and re-layouts: 12.8 us -> 47.2 us
    unnamed x1 -> x0, blocking collectives: 27.6 us -> none
  transfers between devices with their start and end apart: 57 -> 69, of which waited for: 9 -> 20; matrix products, arithmetic and copies ran while one was open for 7% -> 20% of each run, Pallas kernels for 19% -> 10%
where the time goes in v2:
time: 439 us; the launch traced here: 430 us
  Pallas kernels  130 us (30%)
  starting transfers between devices  108 us (25%)
  waiting for transfers between devices  91.2 us (21%)
  local copies, waits for them, and re-layouts  71.3 us (16%)
  matrix products  13.9 us (3%)
  other arithmetic  13.3 us (3%)
    pallas_call x9, Pallas kernels, call(): pl.pallas_call(wrapped, grid=(1,), out_shape=[shape for shape, _ in outs....  130 us
    ppermute x24, waiting for transfers between devices, swap(): lax.ppermute(shard, axis, [(i, i ^ bit) for i in range(lax.axis_size(axis...  54.1 us
    unnamed x239, local copies, waits for them, and re-layouts  47.2 us
    ppermute x24, starting transfers between devices, halo_swap(): result.append(lax.ppermute(part, AXES, there + [(b, a) for a, b in there]))  44.5 us
    ppermute x24, starting transfers between devices, swap(): lax.ppermute(shard, axis, [(i, i ^ bit) for i in range(lax.axis_size(axis...  34.5 us
    ppermute x15, waiting for transfers between devices, ring(): lax.ppermute(shard, axis, [(i, (i + by) % count) for i in range(count)])  34 us
    ppermute x6, starting transfers between devices, halo_inside(): lax.ppermute(part, AXES, [(b, a) for a, b in there] if back else there)  21 us
  transfers between devices with their start and end apart: 69, of which 20 were waited for; matrix products, arithmetic and copies ran while one was open for 20% of the time, Pallas kernels for 10%

profile of v2, /device:TPU:3, one launch (start us, length us, event | category | flops | bytes accessed | tf_op | source)
XLA Modules:
  0.0 430.4 jit_solution(14199569186973546211)
XLA Ops:
  26.6 4.6 %convolution_bitcast_fusion = f32[4,64,4,64]{3,2,1,0:T(4,128)} fusion(pred[64,64,169,1]{2,1,0,3:T(32,128)(4,1)} %bitcast.280, f32[4,4,169,1]{2,1,0,3:T(4,128)S(1)} %reshape.245), kind=kOutput, calls=%fused_computation.28 | convolution fusion | flops 132907008 | bytes 965184 | tf_op jit(solution)/shard_map/dot_general | solution.py:766
  37.9 6.7 %collective-permute-done.8 = bf16[288,512]{1,0:T(8,128)(2,1)S(1)} collective-permute-done((bf16[288,512]{1,0:T(8,128)(2,1)}, bf16[288,512]{1,0:T(8,128)(2,1)S(1)}, u32[]{:S(2)}, u32[]{:S(2)}) %collective-permute-start.8) | collective-permute-done | bytes 294944 | tf_op jit(solution)/shard_map/ppermute | solution.py:130
  45.6 6.9 %collective-permute-done.9 = bf16[288,512]{1,0:T(8,128)(2,1)S(1)} collective-permute-done((bf16[288,512]{1,0:T(8,128)(2,1)S(1)}, bf16[288,512]{1,0:T(8,128)(2,1)S(1)}, u32[]{:S(2)}, u32[]{:S(2)}) %collective-permute-start.9) | collective-permute-done | bytes 294944 | tf_op jit(solution)/shard_map/ppermute | solution.py:130
  62.6 6.3 %collective-permute-done.13 = bf16[288,512]{1,0:T(8,128)(2,1)S(1)} collective-permute-done((bf16[288,512]{1,0:T(8,128)(2,1)S(1)}, bf16[288,512]{1,0:T(8,128)(2,1)S(1)}, u32[]{:S(2)}, u32[]{:S(2)}) %collective-permute-start.13) | collective-permute-done | bytes 294944 | tf_op jit(solution)/shard_map/ppermute | solution.py:134
  68.9 7.0 %collective-permute-start.15 = (bf16[8,288,512]{2,1,0:T(8,128)(2,1)S(1)}, bf16[8,288,512]{2,1,0:T(8,128)(2,1)}, u32[]{:S(2)}, u32[]{:S(2)}) collective-permute-start(bf16[8,288,512]{2,1,0:T(8,128)(2,1)S(1)} %bitcast_dynamic-update-slice_fusion.refs_9_.refs_10_.refs_11_), channel_id=1, source_target_pairs={{0,4},{4,0},{8,12},{12,8},{1,5},{5,1},{9,13},{13,9},{2,6},{6,2},{1... | collective-permute-start | bytes 7077896 | tf_op jit(solution)/shard_map/ppermute | solution.py:134
  80.9 4.6 %collective-permute-start.14 = (bf16[8,128,384]{2,1,0:T(8,128)(2,1)S(1)}, bf16[8,128,384]{2,1,0:T(8,128)(2,1)}, u32[]{:S(2)}, u32[]{:S(2)}) collective-permute-start(bf16[8,128,384]{2,1,0:T(8,128)(2,1)S(1)} %constant_dynamic-update-slice_fusion.refs_8_), channel_id=1, source_target_pairs={{0,4},{4,0},{8,12},{12,8},{1,5},{5,1},{9,13},{13,9},{2,6},{6,2},{1... | collective-permute-start | bytes 2359304 | tf_op jit(solution)/shard_map/ppermute | solution.py:134
  94.5 5.9 %collective-permute-start.26 = (bf16[5,16,512]{2,1,0:T(8,128)(2,1)S(1)}, bf16[5,16,512]{2,1,0:T(8,128)(2,1)S(1)}, u32[]{:S(2)}, u32[]{:S(2)}) collective-permute-start(bf16[5,16,512]{2,1,0:T(8,128)(2,1)S(1)} %get-tuple-element.320), channel_id=1, source_target_pairs={{16,31},{17,30},{18,17},{19,16},{20,19},{21,18},{22,21},{23,20},{2... | collective-permute-start | bytes 245768 | tf_op jit(solution)/shard_map/ppermute | solution.py:124
  102.3 10.7 %layer_step.7 = (bf16[112,512]{1,0:T(8,128)(2,1)}, bf16[80,512]{1,0:T(8,128)(2,1)}, bf16[16,512]{1,0:T(8,128)(2,1)}, bf16[16,512]{1,0:T(8,128)(2,1)}, bf16[224,5...) custom-call(s32[3]{0:T(128)} %pad_add_fusion.refs_0_, ...), custom_call_target="tpu_custom_call" | custom-call | flops 1610612736 | bytes 12000000 | tf_op jit(solution)/shard_map/layer_step/pallas_call | solution.py:517
  115.1 4.5 %collective-permute-start.23 = (bf16[16,512]{1,0:T(8,128)(2,1)}, bf16[16,512]{1,0:T(8,128)(2,1)S(1)}, u32[]{:S(2)}, u32[]{:S(2)}) collective-permute-start(bf16[16,512]{1,0:T(8,128)(2,1)} %get-tuple-element.147), channel_id=1, source_target_pairs={{0,31},{1,30},{2,17},{3,16},{4,19},{5,18},{6,21},{7,20},{8,23},{9,... | collective-permute-start | bytes 49160 | tf_op jit(solution)/shard_map/ppermute | solution.py:116
  122.2 17.6 %layer_step.8 = (bf16[112,512]{1,0:T(8,128)(2,1)}, bf16[80,512]{1,0:T(8,128)(2,1)}, bf16[16,512]{1,0:T(8,128)(2,1)}, bf16[16,512]{1,0:T(8,128)(2,1)}, bf16[224,5...) custom-call(s32[3]{0:T(128)} %pad_add_fusion.refs_0_, ...), custom_call_target="tpu_custom_call" | custom-call | flops 4831838208 | bytes 12000000 | tf_op jit(solution)/shard_map/layer_step/pallas_call | solution.py:517
  144.7 4.8 %collective-permute-start.29 = (bf16[16,512]{1,0:T(8,128)(2,1)}, bf16[16,512]{1,0:T(8,128)(2,1)S(1)}, u32[]{:S(2)}, u32[]{:S(2)}) collective-permute-start(bf16[16,512]{1,0:T(8,128)(2,1)} %get-tuple-element.156), channel_id=1, source_target_pairs={{0,17},{1,16},{2,19},{3,18},{4,21},{5,20},{6,23},{7,22},{8,25},{9,... | collective-permute-start | bytes 49160 | tf_op jit(solution)/shard_map/ppermute | solution.py:116
  156.3 17.7 %layer_step.9 = (bf16[112,512]{1,0:T(8,128)(2,1)}, bf16[80,512]{1,0:T(8,128)(2,1)}, bf16[16,512]{1,0:T(8,128)(2,1)}, bf16[16,512]{1,0:T(8,128)(2,1)}, bf16[224,5...) custom-call(s32[3]{0:T(128)} %pad_add_fusion.refs_0_, ...), custom_call_target="tpu_custom_call" | custom-call | flops 4831838208 | bytes 12000000 | tf_op jit(solution)/shard_map/layer_step/pallas_call | solution.py:517
  187.5 17.5 %layer_step.10 = (bf16[112,512]{1,0:T(8,128)(2,1)}, bf16[80,512]{1,0:T(8,128)(2,1)}, bf16[16,512]{1,0:T(8,128)(2,1)}, bf16[16,512]{1,0:T(8,128)(2,1)}, bf16[224,...) custom-call(s32[3]{0:T(128)} %pad_add_fusion.refs_0_, ...), custom_call_target="tpu_custom_call" | custom-call | flops 4831838208 | bytes 12000000 | tf_op jit(solution)/shard_map/layer_step/pallas_call | solution.py:517
  216.6 17.8 %layer_step.11 = (bf16[112,512]{1,0:T(8,128)(2,1)}, bf16[80,512]{1,0:T(8,128)(2,1)}, bf16[16,512]{1,0:T(8,128)(2,1)}, bf16[16,512]{1,0:T(8,128)(2,1)}, bf16[224,...) custom-call(s32[3]{0:T(128)} %pad_add_fusion.refs_0_, ...), custom_call_target="tpu_custom_call" | custom-call | flops 4831838208 | bytes 12000000 | tf_op jit(solution)/shard_map/layer_step/pallas_call | solution.py:517
  250.1 17.5 %layer_step.12 = (bf16[112,512]{1,0:T(8,128)(2,1)}, bf16[80,512]{1,0:T(8,128)(2,1)}, bf16[16,512]{1,0:T(8,128)(2,1)}, bf16[16,512]{1,0:T(8,128)(2,1)}, bf16[224,...) custom-call(s32[3]{0:T(128)} %pad_add_fusion.refs_0_, ...), custom_call_target="tpu_custom_call" | custom-call | flops 4831838208 | bytes 12000000 | tf_op jit(solution)/shard_map/layer_step/pallas_call | solution.py:517
  295.5 5.2 %collective-permute-start.49 = (bf16[10,16,512]{2,1,0:T(8,128)(2,1)}, bf16[10,16,512]{2,1,0:T(8,128)(2,1)}, u32[]{:S(2)}, u32[]{:S(2)}) collective-permute-start(bf16[10,16,512]{2,1,0:T(8,128)(2,1)} %constant_dynamic-update-slice_fusion.38), channel_id=1, source_target_pairs={{31,16},{30,17},{17,18},{16,19},{19,20},{18,21},{21,22},{20,23},{2... | collective-permute-start | bytes 491528 | tf_op jit(solution)/shard_map/ppermute | solution.py:124
  301.4 12.4 %layer_step.13 = (f32[8,2048]{1,0:T(8,128)}, f32[64,1024]{1,0:T(8,128)}, bf16[256,512]{1,0:T(8,128)(2,1)}, bf16[256,2048]{1,0:T(8,128)(2,1)}, bf16[256,512]{1,0:...) custom-call(s32[3]{0:T(128)} %pad_add_fusion.refs_0_, bf16[256,224]{1,0:T(8,128)(2,1)} %constant.234.clone.refs_1_, ...), custom_call_target="tpu_custom_call" | custom-call | flops 3221225472 | bytes 12000000 | tf_op jit(solution)/shard_map/layer_step/pallas_call | solution.py:517
  316.3 10.9 %weight_grad.3 = (bf16[4,2,256,512]{3,2,1,0:T(8,128)(2,1)}, bf16[4,2,256,512]{3,2,1,0:T(8,128)(2,1)}) custom-call(s32[3]{0:T(128)} %pad_add_fusion.refs_0_, bf16[256,2048]{1,0:T(8,128)(2,1)} %get-tuple-element.245.refs_1_, bf16[256,2048]{1,0:T(8,128)(2,1)} %get-tuple-element.246.refs_2_, bf16[256,2048]{1,0:T(8,128)(2,1)} %get-tuple-element.247.refs_3_, ...), custom_call_target="tpu_custom_call" | custom-call | flops 5368709120 | bytes 20000000 | tf_op jit(solution)/shard_map/weight_grad/pallas_call | solution.py:517
  333.0 8.1 %weight_grad.2 = (bf16[4,2,128,512]{3,2,1,0:T(8,128)(2,1)}, bf16[4,2,128,512]{3,2,1,0:T(8,128)(2,1)}) custom-call(s32[3]{0:T(128)} %pad_add_fusion.refs_0_, bf16[256,1536]{1,0:T(8,128)(2,1)} %get-tuple-element.219.refs_1_, bf16[256,1536]{1,0:T(8,128)(2,1)} %get-tuple-element.220.refs_2_, bf16[256,1536]{1,0:T(8,128)(2,1)} %get-tuple-element.221.refs_3_, ...), custom_call_target="tpu_custom_call" | custom-call | flops 2684354560 | bytes 20000000 | tf_op jit(solution)/shard_map/weight_grad/pallas_call | solution.py:517
  342.0 7.2 %collective-permute-done.54 = f32[10,2048]{1,0:T(8,128)S(1)} collective-permute-done((f32[10,2048]{1,0:T(8,128)S(1)}, f32[10,2048]{1,0:T(8,128)S(1)}, u32[]{:S(2)}, u32[]{:S(2)}) %collective-permute-start.54) | collective-permute-done | bytes 81952 | tf_op jit(solution)/shard_map/ppermute | solution.py:134
  362.0 6.1 %collective-permute-done.56 = bf16[4,128,512]{2,1,0:T(8,128)(2,1)S(1)} collective-permute-done((bf16[4,128,512]{2,1,0:T(8,128)(2,1)S(1)}, bf16[4,128,512]{2,1,0:T(8,128)(2,1)S(1)}, u32[]{:S(2)}, u32[]{:S(2)}) %collective-permute-start.56) | collective-permute-done | bytes 524320 | tf_op jit(solution)/shard_map/ppermute | solution.py:134
  368.3 22.3 %collective-permute-done.63 = bf16[4,256,512]{2,1,0:T(8,128)(2,1)S(1)} collective-permute-done((bf16[4,256,512]{2,1,0:T(8,128)(2,1)S(1)}, bf16[4,256,512]{2,1,0:T(8,128)(2,1)S(1)}, u32[]{:S(2)}, u32[]{:S(2)}) %collective-permute-start.63) | collective-permute-done | bytes 1048608 | tf_op jit(solution)/shard_map/ppermute | solution.py:134
  391.5 7.6 %collective-permute-done.64 = bf16[256,512]{1,0:T(8,128)(2,1)S(1)} collective-permute-done((bf16[256,512]{1,0:T(8,128)(2,1)S(1)}, bf16[256,512]{1,0:T(8,128)(2,1)S(1)}, u32[]{:S(2)}, u32[]{:S(2)}) %collective-permute-start.64) | collective-permute-done | bytes 262176 | tf_op jit(solution)/shard_map/ppermute | solution.py:130
  415.6 6.7 %collective-permute-start.61 = (bf16[2,128,512]{2,1,0:T(8,128)(2,1)S(1)}, bf16[2,128,512]{2,1,0:T(8,128)(2,1)S(1)}, u32[]{:S(2)}, u32[]{:S(2)}) collective-permute-start(bf16[2,128,512]{2,1,0:T(8,128)(2,1)S(1)} %pad_maximum_fusion.4), channel_id=1, source_target_pairs={{0,4},{4,0},{8,12},{12,8},{1,5},{5,1},{9,13},{13,9},{2,6},{6,2},{1... | collective-permute-start | bytes 786440 | tf_op jit(solution)/shard_map/ppermute | solution.py:134
  (480 shorter events, 191.0 us)
Async XLA Ops:
  3.4 30.1 %collective-permute-start.7 = (bf16[288,512]{1,0:T(8,128)(2,1)}, bf16[288,512]{1,0:T(8,128)(2,1)}, u32[]{:S(2)}, u32[]{:S(2)}) collective-permute-start(bf16[288,512]{1,0:T(8,128)(2,1)} %pad_maximum_fusion.3), channel_id=1, source_target_pairs={{0,1},{1,2},{2,3},{3,0},{4,5},{5,6},{6,7},{7,4},{8,9},{9,10},{10,1... | collective-permute-start | bytes 884744 | tf_op jit(solution)/shard_map/ppermute | solution.py:130
  4.7 49.1 %collective-permute-start.10 = (bf16[288,512]{1,0:T(8,128)(2,1)}, bf16[288,512]{1,0:T(8,128)(2,1)}, u32[]{:S(2)}, u32[]{:S(2)}) collective-permute-start(bf16[288,512]{1,0:T(8,128)(2,1)} %pad_maximum_fusion.3), channel_id=1, source_target_pairs={{0,8},{4,12},{8,0},{12,4},{1,9},{5,13},{9,1},{13,5},{2,10},{6,14},... | collective-permute-start | bytes 884744 | tf_op jit(solution)/shard_map/ppermute | solution.py:134
  8.0 27.0 %collective-permute-start = (bf16[128,384]{1,0:T(8,128)(2,1)}, bf16[128,384]{1,0:T(8,128)(2,1)}, u32[]{:S(2)}, u32[]{:S(2)}) collective-permute-start(bf16[128,384]{1,0:T(8,128)(2,1)} %copy.62), channel_id=1, source_target_pairs={{0,1},{1,2},{2,3},{3,0},{4,5},{5,6},{6,7},{7,4},{8,9},{9,10},{10,1... | collective-permute-start | bytes 294920 | tf_op jit(solution)/shard_map/ppermute | solution.py:130
  9.3 68.0 %collective-permute-start.3 = (bf16[128,384]{1,0:T(8,128)(2,1)}, bf16[128,384]{1,0:T(8,128)(2,1)}, u32[]{:S(2)}, u32[]{:S(2)}) collective-permute-start(bf16[128,384]{1,0:T(8,128)(2,1)} %copy.62), channel_id=1, source_target_pairs={{0,8},{4,12},{8,0},{12,4},{1,9},{5,13},{9,1},{13,5},{2,10},{6,14},... | collective-permute-start | bytes 294920 | tf_op jit(solution)/shard_map/ppermute | solution.py:134
  26.4 60.5 %collective-permute-start.16 = (bf16[5,96,512]{2,1,0:T(8,128)(2,1)}, bf16[5,96,512]{2,1,0:T(8,128)(2,1)}, u32[]{:S(2)}, u32[]{:S(2)}) collective-permute-start(bf16[5,96,512]{2,1,0:T(8,128)(2,1)} %fusion.26), channel_id=1, source_target_pairs={{0,1},{1,0},{2,3},{3,2},{4,5},{5,4},{6,7},{7,6},{8,9},{9,8},{10,11... | collective-permute-start | bytes 1474568 | tf_op jit(solution)/shard_map/ppermute | solution.py:134
  35.0 24.6 %collective-permute-start.1 = (bf16[128,384]{1,0:T(8,128)(2,1)}, bf16[128,384]{1,0:T(8,128)(2,1)S(1)}, u32[]{:S(2)}, u32[]{:S(2)}) collective-permute-start(bf16[128,384]{1,0:T(8,128)(2,1)} %collective-permute-done), channel_id=1, source_target_pairs={{0,1},{1,2},{2,3},{3,0},{4,5},{5,6},{6,7},{7,4},{8,9},{9,10},{10,1... | collective-permute-start | bytes 294920 | tf_op jit(solution)/shard_map/ppermute | solution.py:130
  59.6 18.9 %collective-permute-start.4 = (bf16[128,384]{1,0:T(8,128)(2,1)}, bf16[128,384]{1,0:T(8,128)(2,1)S(1)}, u32[]{:S(2)}, u32[]{:S(2)}) collective-permute-start(bf16[128,384]{1,0:T(8,128)(2,1)} %collective-permute-done), channel_id=1, source_target_pairs={{0,8},{4,12},{8,0},{12,4},{1,9},{5,13},{9,1},{13,5},{2,10},{6,14},... | collective-permute-start | bytes 294920 | tf_op jit(solution)/shard_map/ppermute | solution.py:134
  68.9 31.5 %collective-permute-start.15 = (bf16[8,288,512]{2,1,0:T(8,128)(2,1)S(1)}, bf16[8,288,512]{2,1,0:T(8,128)(2,1)}, u32[]{:S(2)}, u32[]{:S(2)}) collective-permute-start(bf16[8,288,512]{2,1,0:T(8,128)(2,1)S(1)} %bitcast_dynamic-update-slice_fusion.refs_9_.refs_10_.refs_11_), channel_id=1, source_target_pairs={{0,4},{4,0},{8,12},{12,8},{1,5},{5,1},{9,13},{13,9},{2,6},{6,2},{1... | collective-permute-start | bytes 7077896 | tf_op jit(solution)/shard_map/ppermute | solution.py:134
  80.9 19.5 %collective-permute-start.14 = (bf16[8,128,384]{2,1,0:T(8,128)(2,1)S(1)}, bf16[8,128,384]{2,1,0:T(8,128)(2,1)}, u32[]{:S(2)}, u32[]{:S(2)}) collective-permute-start(bf16[8,128,384]{2,1,0:T(8,128)(2,1)S(1)} %constant_dynamic-update-slice_fusion.refs_8_), channel_id=1, source_target_pairs={{0,4},{4,0},{8,12},{12,8},{1,5},{5,1},{9,13},{13,9},{2,6},{6,2},{1... | collective-permute-start | bytes 2359304 | tf_op jit(solution)/shard_map/ppermute | solution.py:134
  89.7 30.9 %collective-permute-start.24 = (bf16[5,80,512]{2,1,0:T(8,128)(2,1)S(1)}, bf16[5,80,512]{2,1,0:T(8,128)(2,1)S(1)}, u32[]{:S(2)}, u32[]{:S(2)}) collective-permute-start(bf16[5,80,512]{2,1,0:T(8,128)(2,1)S(1)} %split.97), channel_id=1, source_target_pairs={{16,30},{17,31},{18,16},{19,17},{20,18},{21,19},{22,20},{23,21},{2... | collective-permute-start | bytes 1228808 | tf_op jit(solution)/shard_map/ppermute | solution.py:124
  92.5 20.6 %collective-permute-start.25 = (bf16[5,16,512]{2,1,0:T(8,128)(2,1)S(1)}, bf16[5,16,512]{2,1,0:T(8,128)(2,1)S(1)}, u32[]{:S(2)}, u32[]{:S(2)}) collective-permute-start(bf16[5,16,512]{2,1,0:T(8,128)(2,1)S(1)} %get-tuple-element.321), channel_id=1, source_target_pairs={{16,17},{17,16},{18,19},{19,18},{20,21},{21,20},{22,23},{23,22},{2... | collective-permute-start | bytes 245768 | tf_op jit(solution)/shard_map/ppermute | solution.py:124
  94.5 20.7 %collective-permute-start.26 = (bf16[5,16,512]{2,1,0:T(8,128)(2,1)S(1)}, bf16[5,16,512]{2,1,0:T(8,128)(2,1)S(1)}, u32[]{:S(2)}, u32[]{:S(2)}) collective-permute-start(bf16[5,16,512]{2,1,0:T(8,128)(2,1)S(1)} %get-tuple-element.320), channel_id=1, source_target_pairs={{16,31},{17,30},{18,17},{19,16},{20,19},{21,18},{22,21},{23,20},{2... | collective-permute-start | bytes 245768 | tf_op jit(solution)/shard_map/ppermute | solution.py:124
  234.4 15.0 %collective-permute-start.39 = (bf16[112,512]{1,0:T(8,128)(2,1)}, bf16[112,512]{1,0:T(8,128)(2,1)S(1)}, u32[]{:S(2)}, u32[]{:S(2)}) collective-permute-start(bf16[112,512]{1,0:T(8,128)(2,1)} %get-tuple-element.182), channel_id=1, source_target_pairs={{0,16},{1,17},{2,18},{3,19},{4,20},{5,21},{6,22},{7,23},{8,24},{9,... | collective-permute-start | bytes 344072 | tf_op jit(solution)/shard_map/ppermute | solution.py:116
  267.7 32.9 %collective-permute-start.43 = (bf16[112,512]{1,0:T(8,128)(2,1)}, bf16[112,512]{1,0:T(8,128)(2,1)S(1)}, u32[]{:S(2)}, u32[]{:S(2)}) collective-permute-start(bf16[112,512]{1,0:T(8,128)(2,1)} %get-tuple-element.192), channel_id=1, source_target_pairs={{0,16},{1,17},{2,18},{3,19},{4,20},{5,21},{6,22},{7,23},{8,24},{9,... | collective-permute-start | bytes 344072 | tf_op jit(solution)/shard_map/ppermute | solution.py:116
  270.7 29.9 %collective-permute-start.44 = (bf16[80,512]{1,0:T(8,128)(2,1)}, bf16[80,512]{1,0:T(8,128)(2,1)S(1)}, u32[]{:S(2)}, u32[]{:S(2)}) collective-permute-start(bf16[80,512]{1,0:T(8,128)(2,1)} %get-tuple-element.193), channel_id=1, source_target_pairs={{0,30},{1,31},{2,16},{3,17},{4,18},{5,19},{6,20},{7,21},{8,22},{9,... | collective-permute-start | bytes 245768 | tf_op jit(solution)/shard_map/ppermute | solution.py:116
  270.7 20.6 %collective-permute-start.45 = (bf16[16,512]{1,0:T(8,128)(2,1)}, bf16[16,512]{1,0:T(8,128)(2,1)S(1)}, u32[]{:S(2)}, u32[]{:S(2)}) collective-permute-start(bf16[16,512]{1,0:T(8,128)(2,1)} %get-tuple-element.194), channel_id=1, source_target_pairs={{0,17},{1,16},{2,19},{3,18},{4,21},{5,20},{6,23},{7,22},{8,25},{9,... | collective-permute-start | bytes 49160 | tf_op jit(solution)/shard_map/ppermute | solution.py:116
  272.3 23.2 %collective-permute-start.46 = (bf16[16,512]{1,0:T(8,128)(2,1)}, bf16[16,512]{1,0:T(8,128)(2,1)S(1)}, u32[]{:S(2)}, u32[]{:S(2)}) collective-permute-start(bf16[16,512]{1,0:T(8,128)(2,1)} %get-tuple-element.195), channel_id=1, source_target_pairs={{0,31},{1,30},{2,17},{3,16},{4,19},{5,18},{6,21},{7,20},{8,23},{9,... | collective-permute-start | bytes 49160 | tf_op jit(solution)/shard_map/ppermute | solution.py:116
  282.0 77.0 %collective-permute-start.47 = (bf16[10,80,512]{2,1,0:T(8,128)(2,1)}, bf16[10,80,512]{2,1,0:T(8,128)(2,1)}, u32[]{:S(2)}, u32[]{:S(2)}) collective-permute-start(bf16[10,80,512]{2,1,0:T(8,128)(2,1)} %constant_dynamic-update-slice_fusion.18), channel_id=1, source_target_pairs={{30,16},{31,17},{16,18},{17,19},{18,20},{19,21},{20,22},{21,23},{2... | collective-permute-start | bytes 2457608 | tf_op jit(solution)/shard_map/ppermute | solution.py:124
  291.3 67.7 %collective-permute-start.48 = (bf16[10,16,512]{2,1,0:T(8,128)(2,1)}, bf16[10,16,512]{2,1,0:T(8,128)(2,1)}, u32[]{:S(2)}, u32[]{:S(2)}) collective-permute-start(bf16[10,16,512]{2,1,0:T(8,128)(2,1)} %constant_dynamic-update-slice_fusion.28), channel_id=1, source_target_pairs={{17,16},{16,17},{19,18},{18,19},{21,20},{20,21},{23,22},{22,23},{2... | collective-permute-start | bytes 491528 | tf_op jit(solution)/shard_map/ppermute | solution.py:124
  295.5 63.5 %collective-permute-start.49 = (bf16[10,16,512]{2,1,0:T(8,128)(2,1)}, bf16[10,16,512]{2,1,0:T(8,128)(2,1)}, u32[]{:S(2)}, u32[]{:S(2)}) collective-permute-start(bf16[10,16,512]{2,1,0:T(8,128)(2,1)} %constant_dynamic-update-slice_fusion.38), channel_id=1, source_target_pairs={{31,16},{30,17},{17,18},{16,19},{19,20},{18,21},{21,22},{20,23},{2... | collective-permute-start | bytes 491528 | tf_op jit(solution)/shard_map/ppermute | solution.py:124
  327.3 28.4 %collective-permute-start.62 = (bf16[4,2,256,512]{3,2,1,0:T(8,128)(2,1)}, bf16[4,2,256,512]{3,2,1,0:T(8,128)(2,1)}, u32[]{:S(2)}, u32[]{:S(2)}) collective-permute-start(bf16[4,2,256,512]{3,2,1,0:T(8,128)(2,1)} %get-tuple-element.270), channel_id=1, source_target_pairs={{0,4},{4,0},{8,12},{12,8},{1,5},{5,1},{9,13},{13,9},{2,6},{6,2},{1... | collective-permute-start | bytes 6291464 | tf_op jit(solution)/shard_map/ppermute | solution.py:134
  358.1 32.5 %collective-permute-start.63 = (bf16[4,256,512]{2,1,0:T(8,128)(2,1)S(1)}, bf16[4,256,512]{2,1,0:T(8,128)(2,1)S(1)}, u32[]{:S(2)}, u32[]{:S(2)}) collective-permute-start(bf16[4,256,512]{2,1,0:T(8,128)(2,1)S(1)} %dynamic-slice_bitcast_fusion), channel_id=1, source_target_pairs={{0,8},{4,12},{8,0},{12,4},{1,9},{5,13},{9,1},{13,5},{2,10},{6,14},... | collective-permute-start | bytes 3145736 | tf_op jit(solution)/shard_map/ppermute | solution.py:134
  361.9 37.4 %collective-permute-start.50 = (bf16[10,96,512]{2,1,0:T(8,128)(2,1)S(1)}, bf16[10,96,512]{2,1,0:T(8,128)(2,1)S(1)}, u32[]{:S(2)}, u32[]{:S(2)}) collective-permute-start(bf16[10,96,512]{2,1,0:T(8,128)(2,1)S(1)} %fusion.25), channel_id=1, source_target_pairs={{0,1},{1,0},{2,3},{3,2},{4,5},{5,4},{6,7},{7,6},{8,9},{9,8},{10,11... | collective-permute-start | bytes 2949128 | tf_op jit(solution)/shard_map/ppermute | solution.py:134
  368.2 23.2 %collective-permute-start.57 = (bf16[128,512]{1,0:T(8,128)(2,1)S(1)}, bf16[128,512]{1,0:T(8,128)(2,1)S(1)}, u32[]{:S(2)}, u32[]{:S(2)}) collective-permute-start(bf16[128,512]{1,0:T(8,128)(2,1)S(1)} %dynamic-slice_bitcast_fusion.5), channel_id=1, source_target_pairs={{0,1},{1,2},{2,3},{3,0},{4,5},{5,6},{6,7},{7,4},{8,9},{9,10},{10,1... | collective-permute-start | bytes 393224 | tf_op jit(solution)/shard_map/ppermute | solution.py:130
  (136 other events, 1385.5 us)

commit v3 on v2

v3 whole, which is shorter than its diff:
```python
import functools

import jax
import jax.numpy as jnp
import numpy as np
from jax import lax
from jax.experimental import pallas as pl
from jax.experimental.pallas import tpu as pltpu
from jax.sharding import PartitionSpec as P

WIN = 7
SHIFT = 3
WCOLS = 8
WROWS = 2
TOKENS = WIN * WIN
SLOT = 64
GROUP = 4
AXES = ("section", "row", "mp")
EPS = 1e-05
BF = jnp.bfloat16
F32 = jnp.float32
NN = (((1,), (0,)), ((), ()))
NT = (((1,), (1,)), ((), ()))
TN = (((0,), (0,)), ((), ()))
VMEM_LIMIT = 56 * 1024 * 1024
highest = lax.Precision.HIGHEST


def mm(left, right, dims=NN):
    return lax.dot_general(left, right, dims, preferred_element_type=F32)


def up16(count):
    return -(-count // 16) * 16


def patch_place(row, col):
    return (col // WIN) * SLOT + row * WIN + col % WIN


class Tables:
    def __init__(self, wins):
        self.wins = wins
        self.rows = wins * SLOT
        cols = wins * WIN
        wide = range(SHIFT, cols)
        thin = range(SHIFT)
        low, high = range(SHIFT, WIN), range(SHIFT)
        pieces = [(low, wide), (high, wide), (low, thin), (high, thin)]
        self.sizes = [up16(len(a) * len(b)) for a, b in pieces]
        self.total = sum(self.sizes)
        pick = np.zeros((self.total, self.rows), np.float32)
        put = np.zeros((self.rows, self.total), np.float32)
        at = 0
        for (rows, columns), size in zip(pieces, self.sizes):
            spot = at
            for row in rows:
                for col in columns:
                    pick[spot, patch_place(row, col)] = 1
                    put[patch_place((row - SHIFT) % WIN, (col - SHIFT) % cols), spot] = 1
                    spot += 1
            at += size
        self.pick, self.put = pick, put


def pair_tables(wins):
    cols = wins * WIN
    tokens = WIN * cols
    keep = np.zeros((2, wins * SLOT, tokens), np.float32)
    take = np.zeros((2, wins * SLOT, up16(SHIFT * cols)), np.float32)
    send = np.zeros((up16(SHIFT * cols), tokens), np.float32)
    for seg in range(SHIFT):
        for col in range(cols):
            send[seg * cols + col, (2 * seg + 1) * cols + col] = 1
    for side in range(2):
        for row in range(WIN):
            for col in range(cols):
                place = patch_place(row, col)
                own = row <= SHIFT if side == 0 else row >= SHIFT
                if own:
                    seg = row if side == 0 else row - SHIFT
                    keep[side, place, 2 * seg * cols + col] = 1
                else:
                    seg = row - SHIFT - 1 if side == 0 else row
                    take[side, place, seg * cols + col] = 1
    return keep, take, send


def placing_tables(wins):
    cols, tokens, most = wins * WIN, WIN * wins * WIN, up16(SHIFT * (wins * WIN + 1))
    own = np.zeros((2, 2, wins * SLOT, tokens), np.float32)
    give = np.zeros((2, 2, wins * SLOT, most), np.float32)
    take = np.zeros((2, 2, most, tokens), np.float32)
    up = np.zeros((wins * SLOT, most), np.float32)
    land = np.zeros((2, most, tokens), np.float32)
    half = SHIFT * 2 * cols + cols

    def holder(row, col):
        token = row * 2 * cols + col
        return (0, token) if token < half else (1, token - half)

    for section in range(2):
        for side in range(2):
            given, raised = 0, 0
            for row in range(WIN):
                for col in range(cols):
                    place = patch_place(row, col)
                    real_row = row + SHIFT * section
                    real_col = (side * cols + col + SHIFT * section) % (2 * cols)
                    if real_row >= WIN:
                        up[place, raised] = 1
                        land[side, raised, holder(real_row - WIN, real_col)[1]] = 1
                        raised += 1
                        continue
                    keeper, token = holder(real_row, real_col)
                    if keeper == side:
                        own[section, side, place, token] = 1
                    else:
                        give[section, side, place, given] = 1
                        take[section, keeper, given, token] = 1
                        given += 1
    return own, give, take, up, land


class Layout:
    def __init__(self, row_count, mp_count):
        self.row_count, self.mp_count = row_count, mp_count
        self.across = mp_count // WROWS
        self.wins = WCOLS // self.across
        self.high = row_count * WROWS

    def device(self, section, window_row, place):
        window_row, place = window_row % self.high, place % self.across
        row = window_row // WROWS
        return (section * self.row_count + row) * self.mp_count + (window_row % WROWS) * self.across + place

    def route(self, source, target, up, back):
        return [
            (self.device(source, window_row, place), self.device(target, window_row - up, place - back))
            for window_row in range(self.high)
            for place in range(self.across)
        ]


    def up_routes(self):
        return [
            [(self.device(1, window_row, side), self.device(1, window_row + 1, 0)) for window_row in range(self.high)] for side in range(2)
        ]


HALO = ((0, 0), (1, 0), (0, 1), (1, 1))


def halo_swap(layout, parts, back_only):
    result = []
    for part, by in zip(parts, HALO):
        there = layout.route(0, 1, *by)
        result.append(lax.ppermute(part, AXES, [(b, a) for a, b in there] + ([] if back_only else there)))
    return result


def halo_inside(layout, parts, back):
    result = [parts[0]]
    for part, by in zip(parts[1:], HALO[1:]):
        there = layout.route(1, 1, *by)
        result.append(lax.ppermute(part, AXES, [(b, a) for a, b in there] if back else there))
    return result


def ring(shard, axis, by=1):
    count = lax.axis_size(axis)
    return lax.ppermute(shard, axis, [(i, (i + by) % count) for i in range(count)])


def swap(shard, axis, bit):
    return lax.ppermute(shard, axis, [(i, i ^ bit) for i in range(lax.axis_size(axis))])


def natural_ring(shards, mp):
    stacked, count = jnp.stack(shards), len(shards)
    return jnp.stack([lax.dynamic_index_in_dim(stacked, (mp - j) % count, 0, keepdims=False) for j in range(count)])


def gather_quarter(quarter):
    near, far = ring(quarter, "mp"), ring(quarter, "mp", -1)
    further = ring(near, "mp")
    across = lambda piece: swap(piece, "row", 2)
    return (
        [(jnp.stack([quarter, near, across(quarter), across(near)]), ((0, 0), (0, 1), (2, 0), (2, 1)))]
        + [(jnp.stack([far, further, across(far), across(further)]), ((0, 3), (0, 2), (2, 3), (2, 2)))]
    ), further


def take_at(array, index, axis=0):
    return lax.dynamic_index_in_dim(array, index, axis, keepdims=False)


def head_masks(dtype):
    lane = lax.broadcasted_iota(jnp.int32, (1, GROUP * 32), 1)
    return [jnp.where(lane // 32 == h, 1.0, 0.0).astype(dtype) for h in range(GROUP)]


def spread_heads(block, masks):
    return jnp.concatenate([block * mask for mask in masks], axis=0)


def fold_heads(tall, masks):
    total = tall[:SLOT] * masks[0]
    for h in range(1, GROUP):
        total = total + tall[h * SLOT : (h + 1) * SLOT] * masks[h]
    return total


def centre(values):
    middle = jnp.mean(values, axis=-1, keepdims=True)
    centred = values - middle
    scale = lax.rsqrt(jnp.mean(centred * centred, axis=-1, keepdims=True) + EPS)
    return centred * scale, scale


KEPT = ("gp", "mid", "qkv", "prob", "x")
WEIGHTS = ("wq", "wo", "w1", "w2")
TOGETHER = 2


class Refs:
    pass


class Copies:
    def __init__(self, sems):
        self.sems, self.used, self.sent = sems, 0, []

    def sem(self, count=1):
        self.used += count
        return self.used - count

    def at(self, index):
        return self.sems.at[index]

    def ship(self, b, make):
        first = self.sem(TOGETHER)
        maker = lambda b: make(b, self.at(first + b))
        maker(b).start()
        self.sent.append(maker)

    def finish(self, count):
        for b in range(TOGETHER):

            @pl.when(b < count)
            def _(b=b):
                for maker in self.sent:
                    maker(b).wait()

        self.sent = []


def arrival(target, sem):
    return pltpu.make_async_copy(target, target, sem)


def load_weights(k, kinds, held, offsets):
    waits = {}
    for name in kinds:
        kind, target, sem = WEIGHTS.index(name), getattr(k, name), k.copies.at(k.copies.sem())
        waits[name] = arrival(target, sem)
        if held is None:
            pltpu.make_async_copy(getattr(k, name + "_whole"), target, sem).start()
            continue
        flat = len(target.shape) == 2
        shards = 4
        high = target.shape[-2] // (4 * shards if flat else 4)
        for number, places in enumerate(held):
            for piece, (bits, back) in enumerate(places):
                quarter = k.sec[1] ^ bits
                shard = lax.rem(k.sec[2] + (shards - back), shards)
                start = quarter * high
                if flat:
                    start = start + shard * (4 * high)
                rows = pl.ds(pl.multiple_of(start, high), high)
                place = target.at[rows, :] if flat else target.at[shard, rows, :]
                source = getattr(k, f"pieces_{number}").at[piece, pl.ds(offsets[kind], high), :]
                pltpu.make_async_copy(source, place, sem).start()
    return waits


def window_rows(w):
    return slice(w * SLOT, (w + 1) * SLOT)


def result(k, name, cols=None):
    def make(b, sem):
        src = getattr(k, name)
        src = src.at[0, b] if name in KEPT else src.at[b]
        dst = getattr(k, name + "_o").at[b]
        if cols is not None:
            src, dst = src.at[:, cols], dst.at[:, cols]
        return pltpu.make_async_copy(src, dst, sem)

    return make


def forward_part(k, wins, wait, b):
    x, qkv, prob, mid, gp = (getattr(k, name).at[0, b] for name in ("x", "qkv", "prob", "mid", "gp"))
    a, ctx, n2, act, y = (getattr(k, name).at[b] for name in ("a", "ctx", "n2", "act", "y"))
    ship = lambda name, cols=None: k.copies.ship(b, result(k, name, cols))

    @pl.when(k.sec[0] == 0)
    def _():
        x[...] = k.pin[b]

    if k.landed:

        @pl.when(k.sec[0] == 1)
        def _():
            joined = jnp.concatenate([k.p_main[b], k.p_row[b], k.p_col[b], k.p_cor[b]], axis=0)
            x[...] = mm(k.put[...], joined).astype(BF)

    for w in range(wins):
        rows = window_rows(w)
        hat, _ = centre(x[rows, :].astype(F32))
        a[rows, :] = (hat * k.vec[0:1, :] + k.vec[1:2, :]).astype(BF)
    ship("x")
    ship("a")
    wait("wq")
    lane = lax.broadcasted_iota(jnp.int32, (1, 3 * GROUP * 32), 1)
    factor = jnp.where(lane < GROUP * 32, 32 ** (-0.5), 1.0)
    for g in range(4):
        pr = mm(a[...], k.wq[g], NT) + k.bq[g : g + 1, :]
        qkv[:, g * 384 : (g + 1) * 384] = (pr * factor).astype(BF)
    ship("qkv")
    wait("bias")
    wait("region")
    masks, masks_f = head_masks(BF), head_masks(F32)
    for w in range(wins):
        rows = window_rows(w)
        for g in range(4):
            query = qkv[rows, g * 384 : g * 384 + 128]
            key = qkv[rows, g * 384 + 128 : g * 384 + 256]
            value = qkv[rows, g * 384 + 256 : g * 384 + 384]
            scores = mm(key, spread_heads(query, masks), NT) + k.bias[g] + k.region[w]
            top = jnp.max(scores, axis=0, keepdims=True)
            e = jnp.exp(scores - top)
            low = (e * (1.0 / jnp.sum(e, axis=0, keepdims=True))).astype(BF)
            prob[rows, g * 256 : (g + 1) * 256] = low
            ctx[rows, g * 128 : (g + 1) * 128] = fold_heads(mm(low, value, TN), masks_f).astype(BF)
    ship("prob")
    ship("ctx")
    wait("wo")
    mid[...] = x[...].astype(F32) + (mm(ctx[...], k.wo[...]) + k.vec[2:3, :])
    ship("mid")
    for w in range(wins):
        rows = window_rows(w)
        hat, _ = centre(mid[rows, :])
        n2[rows, :] = (hat * k.vec[3:4, :] + k.vec[4:5, :]).astype(BF)
    ship("n2")
    wait("w1")
    wait("w2")
    parts, _, width = k.w1.shape
    total = mid[...] + k.vec[5:6, :]
    for j in range(parts):
        cols = slice(j * width, (j + 1) * width)
        hidden = mm(n2[...], k.w1[j]) + k.b1[j : j + 1, :]
        phi = 0.5 + 0.5 * lax.erf(hidden * 0.7071067811865476)
        low = (hidden * phi).astype(BF)
        act[:, cols] = low
        gp[:, cols] = (phi + hidden * (jnp.exp(hidden * hidden * -0.5) * 0.3989422804014327)).astype(BF)
        ship("act", cols)
        ship("gp", cols)
        total = total + mm(low, k.w2[j])
    y[...] = total.astype(BF)
    ship("y")

    put_partner(k, 0, b, y)

    @pl.when(k.sec[0] == 0)
    def _():
        put_pieces(k, "s_", b, mm(k.pick[...], y[...]).astype(BF))

    @pl.when(k.sec[0] == 1)
    def _():
        put_neighbours(k, 0, b, y)


def put_pieces(k, first, b, joined):
    at = 0
    for name in PIECES:
        ref = getattr(k, first + name)
        ref[b] = joined[at : at + ref.shape[1]]
        at += ref.shape[1]


def put_partner(k, kind, b, result):
    if hasattr(k, "f_pair"):
        k.f_pair[kind, b] = mm(k.give[...], result[...], TN).astype(BF)


def put_neighbours(k, kind, b, result):
    if hasattr(k, "f_up"):
        k.f_up[kind, b] = mm(k.up[...], result[...], TN).astype(BF)
        return
    joined = mm(k.put[...], result[...], TN).astype(BF)
    at = 0
    for name in PIECES:
        ref = getattr(k, "h_" + name)
        ref[kind, b] = joined[at : at + ref.shape[2]]
        at += ref.shape[2]


def norm_back(grad, hat, scale, gain):
    inner = grad * gain
    return scale * (inner - jnp.mean(inner, axis=-1, keepdims=True) - hat * jnp.mean(inner * hat, axis=-1, keepdims=True))


def column_sum(values):
    return jnp.sum(values, axis=0, keepdims=True)


def backward_mlp(k, wins, wait, old, b):
    slot = 1 - k.sec[0]
    gp, mid = k.gp.at[slot, b], k.mid.at[slot, b]
    out_grad, dhs, gm, dmid = k.g.at[b], k.dh.at[b], k.gm.at[b], k.dmid.at[b]
    ship = lambda name, cols=None: k.copies.ship(b, result(k, name, cols))

    @pl.when(k.sec[0] == 0)
    def _():
        joined = jnp.concatenate([k.p_main[b], k.p_row[b], k.p_col[b], k.p_cor[b]], axis=0)
        out_grad[...] = mm(k.pick[...], joined, TN).astype(BF)

    @pl.when(k.sec[0] == 1)
    def _():
        joined = jnp.concatenate([k.c_main[b], k.c_row[b], k.c_col[b], k.c_cor[b]], axis=0)
        out_grad[...] = mm(k.put[...], joined).astype(BF)

    ship("g")
    parts, _, width = k.w1.shape
    wait("w2")
    wait("w1")
    old("gp", b)
    total = None
    for j in range(parts):
        cols = slice(j * width, (j + 1) * width)
        dh = (mm(out_grad[...], k.w2[j], NT) * gp[:, cols].astype(F32)).astype(BF)
        dhs[:, cols] = dh
        k.small[0:1, cols] += column_sum(dh.astype(F32))
        ship("dh", cols)
        part = mm(dh, k.w1[j], NT)
        total = part if total is None else total + part
    k.dn[...] = total
    old("mid", b)
    sums = [0.0] * 4
    for w in range(wins):
        rows = window_rows(w)
        grad = k.dn[rows, :]
        out = out_grad[rows, :].astype(F32)
        hat, scale = centre(mid[rows, :])
        whole = out + norm_back(grad, hat, scale, k.vec[3:4, :])
        dmid[rows, :] = whole
        low = whole.astype(BF)
        gm[rows, :] = low
        for i, term in enumerate((out, low.astype(F32), grad * hat, grad)):
            sums[i] = sums[i] + column_sum(term)
    ship("gm")
    if hasattr(k, "dmid_o"):
        ship("dmid")
    k.small[1:2, 0:512] += sums[0]
    k.small[1:2, 512:1024] += sums[1]
    k.small[2:3, 0:512] += sums[2]
    k.small[2:3, 512:1024] += sums[3]


def backward_attention(k, wins, wait, old, b, reload):
    slot = 1 - k.sec[0]
    qkv, prob, x = k.qkv.at[slot, b], k.prob.at[slot, b], k.x.at[slot, b]
    gm, dmid, dqkv, dx = k.gm.at[b], k.dmid.at[b], k.dqkv.at[b], k.dx.at[b]
    ship = lambda name, cols=None: k.copies.ship(b, result(k, name, cols))
    wait("wo")
    if reload:
        old("gm", b)
    k.dctx[...] = mm(gm[...], k.wo[...], NT).astype(BF)
    old("qkv", b)
    old("prob", b)
    masks, masks_f = head_masks(BF), head_masks(F32)
    for w in range(wins):
        rows = window_rows(w)
        for g in range(4):
            at = g * 384
            query = qkv[rows, at : at + 128]
            key = qkv[rows, at + 128 : at + 256]
            value = qkv[rows, at + 256 : at + 384]
            do = spread_heads(k.dctx[rows, g * 128 : (g + 1) * 128], masks)
            low = prob[rows, g * 256 : (g + 1) * 256]
            p = low.astype(F32)
            dp = mm(value, do, NT)
            ds = (p * (dp - column_sum(p * dp))).astype(BF)
            k.dbias[:, g * 256 : (g + 1) * 256] += ds.astype(F32)
            dv = mm(low, do).astype(BF)
            dk = mm(ds, spread_heads(query, masks)).astype(BF)
            dq = (fold_heads(mm(ds, key, TN), masks_f) * 32 ** (-0.5)).astype(BF)
            dqkv[rows, at : at + 128] = dq
            dqkv[rows, at + 128 : at + 256] = dk
            dqkv[rows, at + 256 : at + 384] = dv
    ship("dqkv")
    wait("wq")
    total = None
    for g in range(4):
        part = dqkv[:, g * 384 : (g + 1) * 384]
        k.small[3:4, g * 384 : (g + 1) * 384] += column_sum(part.astype(F32))
        part = mm(part, k.wq[g])
        total = part if total is None else total + part
    k.dn[...] = total
    old("x", b)
    if reload:
        old("dmid", b)
    sums = [0.0] * 2
    for w in range(wins):
        rows = window_rows(w)
        grad = k.dn[rows, :]
        hat, scale = centre(x[rows, :].astype(F32))
        dx[rows, :] = (dmid[rows, :] + norm_back(grad, hat, scale, k.vec[0:1, :])).astype(BF)
        sums[0] = sums[0] + column_sum(grad * hat)
        sums[1] = sums[1] + column_sum(grad)
    ship("dx")
    k.small[1:2, 1024:1536] += sums[0]
    k.small[1:2, 1536:2048] += sums[1]
    put_partner(k, 1, b, dx)
    if hasattr(k, "s_main"):

        @pl.when(k.sec[0] == 1)
        def _():
            put_pieces(k, "s_", b, mm(k.put[...], dx[...], TN).astype(BF))
            put_neighbours(k, 1, b, dx)


def loop(count, most, run):
    def once(b, carry):
        run(b)
        return carry

    if most:
        lax.fori_loop(0, count, once, 0)


def step_kernel(wins, held, offsets, counts, mlp, attention, k):
    k.copies = copies = Copies(k.sems)
    ahead, back = max(counts[:2]), max(counts[2:])
    number = lambda pair: jnp.where(k.sec[0] == 0, pair[0], pair[1])
    forwards, backwards = number(counts[:2]), number(counts[2:])
    kinds = WEIGHTS if ahead else (("w2", "w1") if mlp else ()) + (("wo", "wq") if attention else ())
    waits = load_weights(k, kinds[:1], held, offsets)
    if ahead:
        for name in ("bias", "region"):
            copy = pltpu.make_async_copy(getattr(k, name + "_h"), getattr(k, name), copies.at(copies.sem()))
            copy.start()
            waits[name] = copy
    fetched = {}
    if back:
        reload = attention and not mlp
        for name in (("gp", "mid") if mlp else ("gm", "dmid")) + (("qkv", "prob", "x") if attention else ()):
            first = copies.sem(TOGETHER)

            def fetch(b, name=name, first=first):
                target = getattr(k, name)
                target = target.at[1, b] if name in KEPT else target.at[b]
                return pltpu.make_async_copy(getattr(k, "old_" + name).at[b], target, copies.at(first + b))

            fetched[name] = fetch
            for b in range(back):
                pl.when((k.sec[0] == 0) & (b < backwards))(lambda b=b, fetch=fetch: fetch(b).start())
    waits |= load_weights(k, kinds[1:], held, offsets)

    def all_weights():
        for copy in waits.values():
            copy.wait()

    def old(name, b):
        if name in fetched:
            pl.when(k.sec[0] == 0)(lambda: fetched[name](b).wait())

    def forward(b):
        forward_part(k, wins, lambda name: pl.when(b == 0)(waits[name].wait), b)

    loop(forwards, ahead, forward)
    if ahead:
        pl.when(forwards == 0)(all_weights)
    sent_ahead, copies.sent = copies.sent, []
    if back:
        k.small[...] = jnp.zeros_like(k.small)
        if attention:
            k.dbias[...] = jnp.zeros_like(k.dbias)
        wait = lambda b: (lambda name: None) if ahead else (lambda name: pl.when(b == 0)(waits[name].wait))

        def backward(b):
            if mlp:
                backward_mlp(k, wins, wait(b), old, b)
            if attention:
                backward_attention(k, wins, wait(b), old, b, reload)

        loop(backwards, back, backward)
        if not ahead:
            pl.when(backwards == 0)(all_weights)
    copies.finish(backwards)
    copies.sent = sent_ahead
    copies.finish(forwards)


SMEM_SPEC = pl.BlockSpec(memory_space=pltpu.SMEM)
HBM_SPEC = pl.BlockSpec(memory_space=pl.ANY)
VMEM_SPEC = pl.BlockSpec(memory_space=pltpu.VMEM)


def shape_of(*shape, dtype=BF):
    return jax.ShapeDtypeStruct(shape, dtype)


def call(kernel, name, ins, outs, scratch, flops, moved):
    names = list(ins) + list(outs) + list(scratch)

    def wrapped(*refs):
        k = Refs()
        for key, ref in zip(names, refs):
            setattr(k, key, ref)
        kernel(k)

    results = pl.pallas_call(
        wrapped,
        grid=(1,),
        out_shape=[shape for shape, _ in outs.values()],
        in_specs=[spec for _, spec in ins.values()],
        out_specs=[spec for _, spec in outs.values()],
        scratch_shapes=list(scratch.values()),
        compiler_params=pltpu.CompilerParams(vmem_limit_bytes=VMEM_LIMIT),
        cost_estimate=pl.CostEstimate(flops=min(flops, 1), bytes_accessed=min(moved, 1), transcendentals=0),
        name=name,
    )(*[array for array, _ in ins.values()])
    return dict(zip(outs, results))


PIECES = ("main", "row", "col", "cor")


def vmem(array):
    return (array, VMEM_SPEC)


def hbm(array):
    return (array, HBM_SPEC)


def run_step(tables, static, landed, counts, groups, old, mlp=True, attention=True):
    sources, held, offsets, shapes = static["weights"]
    rows, wide = tables.rows, shapes[2][0] * shapes[2][2]
    ahead, back = max(counts[:2]), max(counts[2:])
    one = lambda array, index: (array, pl.BlockSpec((TOGETHER,) + array.shape[1:], lambda i: (index, 0, 0)))
    ins = {"sec": (static["sec"], SMEM_SPEC), "put": vmem(static["put"]), "pick": vmem(static["pick"]), "vec": vmem(static["vec"])}
    if landed is not None and (ahead or mlp):
        for name, piece in zip(PIECES, landed):
            ins["p_" + name] = vmem(piece)
    kinds = WEIGHTS if ahead else (("w1", "w2") if mlp else ()) + (("wq", "wo") if attention else ())
    outs, scratch = {}, {}
    for name, shape in zip(WEIGHTS, shapes):
        if name in kinds:
            scratch[name] = pltpu.VMEM(shape, BF)
            if held is None:
                ins[name + "_whole"] = hbm(sources[WEIGHTS.index(name)])
    if held is not None:
        for number, source in enumerate(sources):
            ins[f"pieces_{number}"] = hbm(source)
    widths = {"gp": (wide, BF), "mid": (512, F32), "qkv": (1536, BF), "prob": (1024, BF), "x": (512, BF)}
    for name, (cols, dtype) in widths.items():
        if ahead or (mlp if name in ("gp", "mid") else attention):
            scratch[name] = pltpu.VMEM((2, TOGETHER, rows, cols), dtype)
    local, passed = {}, {}
    if "give" in static and (ahead or attention):
        ins["give"] = vmem(static["give"])
        outs["f_pair"] = (shape_of(2, TOGETHER, static["give"].shape[1], 512), VMEM_SPEC)
        if ahead:
            ins["up"] = vmem(static["up"])
            outs["f_up"] = (shape_of(2, TOGETHER, static["up"].shape[1], 512), VMEM_SPEC)
    if ahead:
        ins["pin"] = one(static["pin"], groups[0])
        ins["bq"], ins["b1"] = vmem(static["bq"]), vmem(static["b1"])
        for name in ("bias", "region"):
            ins[name + "_h"] = hbm(static[name])
            scratch[name] = pltpu.VMEM(static[name].shape, F32)
        for name, size in zip(PIECES, tables.sizes):
            outs["s_" + name] = (shape_of(TOGETHER, size, 512), VMEM_SPEC)
            if "give" not in static:
                outs["h_" + name] = (shape_of(2, TOGETHER, size, 512), VMEM_SPEC)
        for name, (cols, dtype) in widths.items():
            outs[name + "_o"] = (shape_of(TOGETHER, rows, cols, dtype=dtype), HBM_SPEC)
        local |= {"a": (512, BF), "ctx": (512, BF), "n2": (512, BF), "act": (wide, BF), "y": (512, BF)}
    if back:
        if mlp:
            for name, target in zip(PIECES, static["targets"]):
                ins["c_" + name] = one(target, groups[1])
            local |= {"g": (512, BF), "dh": (wide, BF), "gm": (512, BF)}
            (passed if attention else local)["dmid"] = (512, F32)
        else:
            passed |= {"gm": (512, BF), "dmid": (512, F32)}
        for name in (("gp", "mid") if mlp else ("gm", "dmid")) + (("qkv", "prob", "x") if attention else ()):
            ins["old_" + name] = hbm(old[name + "_o"])
        if attention:
            local |= {"dqkv": (1536, BF), "dx": (512, BF)}
            scratch["dctx"] = pltpu.VMEM((rows, 512), BF)
            outs["dbias"] = (shape_of(SLOT, 1024, dtype=F32), VMEM_SPEC)
        scratch["dn"] = pltpu.VMEM((rows, 512), F32)
        outs["small"] = (shape_of(8, 2048, dtype=F32), VMEM_SPEC)
    for name, (cols, dtype) in local.items():
        outs[name + "_o"] = (shape_of(TOGETHER, rows, cols, dtype=dtype), HBM_SPEC)
        scratch[name] = pltpu.VMEM((TOGETHER, rows, cols), dtype)
    for name, (cols, dtype) in passed.items():
        scratch[name] = pltpu.VMEM((TOGETHER, rows, cols), dtype)
    scratch["sems"] = pltpu.SemaphoreType.DMA((192,))
    passes = 2 * ahead + 2 * back * (mlp + attention)
    kernel = functools.partial(step_kernel, tables.wins, held, offsets, counts, mlp, attention)

    def run(k):
        k.landed = landed is not None
        kernel(k)

    return call(run, "layer_step", ins, outs, scratch, 2 * passes * rows * TOGETHER * 3145728, 20_000_000)


def weight_grad_kernel(slots, terms, quartered, based, k):
    sems = iter(range(64))
    waits = {}
    for name in dict.fromkeys(name for term in terms for name in term[:2]):
        target, sem = getattr(k, name), k.sems.at[next(sems)]
        batches = len(slots[name][0])
        rows = target.shape[0] // batches
        for section in range(2):

            @pl.when(k.sec[0] == section)
            def _(name=name, section=section, target=target, sem=sem):
                for batch, (step, place) in enumerate(slots[name][section]):
                    source = getattr(k, f"{name}_{step}").at[place]
                    pltpu.make_async_copy(source, target.at[pl.ds(batch * rows, rows), :], sem).start()

        waits[name] = arrival(target, sem)
    for name in based:
        waits[name] = pltpu.make_async_copy(getattr(k, name + "_base"), getattr(k, name), k.sems.at[next(sems)])
        waits[name].start()
    leaving = []
    for number, (left, right, side, name, first, rows) in enumerate(terms):
        for needed in (left, right, name):
            if needed in waits:
                waits.pop(needed).wait()
        l, r, t = getattr(k, left), getattr(k, right), getattr(k, name)
        parts = t.shape[0]
        for part in range(parts):
            if side == "left":
                width = l.shape[1] // parts
                value = mm(l[:, part * width : (part + 1) * width], r[...], TN)
            else:
                width = r.shape[1] // parts
                value = mm(l[...], r[:, part * width : (part + 1) * width], TN)
            if name in based:
                value = value + t[part, first : first + rows, :].astype(F32)
            t[part, first : first + rows, :] = value.astype(BF)
        if any(name == term[3] for term in terms[number + 1 :]):
            continue
        sem = k.sems.at[next(sems)]
        if not quartered:
            copy = pltpu.make_async_copy(t, getattr(k, name + "_o"), sem)
            copy.start()
            leaving.append(copy)
            continue
        keep, send = getattr(k, name + "_keep"), getattr(k, name + "_send")
        high = t.shape[1] // 4
        for core in range(2):

            @pl.when(lax.rem(k.sec[1], 2) == core)
            def _(core=core, t=t, keep=keep, send=send, sem=sem, high=high):
                for quarter in range(4):
                    place = keep if quarter % 2 == core else send
                    pltpu.make_async_copy(t.at[:, pl.ds(quarter * high, high), :], place.at[:, quarter // 2], sem).start()

        leaving.append(arrival(t, sem))
    for copy in leaving:
        copy.wait()


def run_weight_grad(static, members, slots, terms, shapes, quartered, base):
    ins = {"sec": (static["sec"], SMEM_SPEC)}
    scratch, outs = {}, {}
    for name, arrays in members.items():
        for i, array in arrays.items():
            ins[f"{name}_{i}"] = hbm(array)
        scratch[name] = pltpu.VMEM((len(slots[name][0]) * array.shape[1], array.shape[2]), BF)
    for name, array in base.items():
        ins[name + "_base"] = hbm(array)
    for name, shape in shapes.items():
        scratch[name] = pltpu.VMEM(shape, BF)
        if quartered:
            for kind in ("_keep", "_send"):
                outs[name + kind] = (shape_of(shape[0], 2, shape[1] // 4, shape[2]), HBM_SPEC)
        else:
            outs[name + "_o"] = (shape_of(*shape), HBM_SPEC)
    scratch["sems"] = pltpu.SemaphoreType.DMA((64,))
    rows = scratch[next(iter(members))].shape[0]
    flops = 2 * rows * sum(int(np.prod(shape)) for shape in shapes.values())
    kernel = functools.partial(weight_grad_kernel, slots, terms, quartered, tuple(base))
    return call(kernel, "weight_grad", ins, outs, scratch, flops, 20_000_000)


def collect(arrays):
    ins = {f"{name}_{i}": vmem(array) for name, members in arrays.items() for i, array in enumerate(members)}
    outs = {name: (shape_of(len(members), *members[0].shape), VMEM_SPEC) for name, members in arrays.items()}

    def kernel(k):
        for name, members in arrays.items():
            for i in range(len(members)):
                getattr(k, name)[i] = getattr(k, f"{name}_{i}")[...]

    return call(kernel, "collect", ins, outs, {}, 0, 4_000_000)


def run_patches(static, plain, mains, halo, sizes):
    rows = plain[0][0].shape[1]
    batches = sum(sizes)
    ins = {"sec": (static["sec"], SMEM_SPEC), "pick": vmem(static["pick"])}
    for group, (pair, main) in enumerate(zip(plain, mains)):
        ins[f"plain_0_{group}"], ins[f"plain_1_{group}"], ins[f"main_{group}"] = vmem(pair[0]), vmem(pair[1]), vmem(main)
    for name, array in zip(PIECES[1:], halo):
        ins[name] = vmem(array)
    outs = {"patch": (shape_of(2 * batches, rows, 512), VMEM_SPEC)}

    def kernel(k):
        for kind in range(2):
            for group, size in enumerate(sizes):
                for b in range(size):
                    at = kind * batches + sum(sizes[:group]) + b

                    @pl.when(k.sec[0] == 0)
                    def _(at=at, kind=kind, group=group, b=b):
                        k.patch[at] = getattr(k, f"plain_{kind}_{group}")[b]

                    @pl.when(k.sec[0] == 1)
                    def _(at=at, kind=kind, group=group, b=b):
                        parts = [getattr(k, f"main_{group}")[kind, b]] + [getattr(k, name)[group, kind, b] for name in PIECES[1:]]
                        k.patch[at] = mm(k.pick[...], jnp.concatenate(parts, axis=0), TN).astype(BF)

    return call(kernel, "patches", ins, outs, {}, 0, 0)


def run_places(static, steps, pairs, ups, own, take, land, sizes, tokens):
    batches, groups = sum(sizes), len(sizes)
    ins = {"sec": (static["sec"], SMEM_SPEC), "own": vmem(own), "take": vmem(take), "land_0": vmem(land[0]), "land_1": vmem(land[1])}
    for step, done in enumerate(steps):
        for name in ("y_o", "dx_o"):
            if name in done:
                ins[f"{name}_{step}"] = vmem(done[name])
        ins[f"pair_{step}"] = vmem(pairs[step])
        for side, array in enumerate(ups[step]):
            ins[f"up_{side}_{step}"] = vmem(array)
    outs = {"first": (shape_of(batches, tokens, 512), VMEM_SPEC), "second": (shape_of(batches, tokens, 512, dtype=F32), VMEM_SPEC)}

    def kernel(k):
        for kind, name in enumerate(("y_o", "dx_o")):
            for group, size in enumerate(sizes):
                for b in range(size):
                    at = sum(sizes[:group]) + b

                    def put(value, at=at, kind=kind):
                        if kind == 0:
                            k.first[at] = value.astype(BF)
                        else:
                            k.second[at] = value

                    def here(step, kind=kind, name=name, b=b):
                        value = mm(k.own[...], getattr(k, f"{name}_{step}")[b], TN)
                        return value + mm(k.take[...], getattr(k, f"pair_{step}")[kind, b], TN)

                    @pl.when(k.sec[0] == 0)
                    def _(group=group, kind=kind, put=put, here=here):
                        put(here(group + 2 * kind))

                    @pl.when(k.sec[0] == 1)
                    def _(group=group, kind=kind, b=b, put=put, here=here):
                        value = here(group + 1)
                        for side in range(2):
                            value = value + mm(getattr(k, f"land_{side}")[...], getattr(k, f"up_{side}_{group + 1}")[kind, b], TN)
                        put(value)

    return call(kernel, "places", ins, outs, {}, 0, 0)


def table_onehot():
    code = np.full((SLOT, SLOT), -1, np.int32)
    for u in range(TOKENS):
        for t in range(TOKENS):
            code[u, t] = (t // WIN - u // WIN + WIN - 1) * (2 * WIN - 1) + t % WIN - u % WIN + WIN - 1
    side = (2 * WIN - 1) ** 2
    return (jnp.arange(side, dtype=jnp.int32)[:, None] == jnp.asarray(code.reshape(1, -1))).astype(F32)


def region_mask(layout, section):
    row, mp = lax.axis_index("row"), lax.axis_index("mp")
    window_row = row * WROWS + mp // layout.across
    window_col = (mp % layout.across) * layout.wins + jnp.arange(layout.wins)
    place = jnp.arange(SLOT)
    row_label = jnp.where(window_row == layout.high - 1, 1 + (place // WIN >= WIN - SHIFT).astype(jnp.int32), 0)
    col_label = jnp.where(
        (window_col == WCOLS - 1)[:, None], 1 + (place % WIN >= WIN - SHIFT).astype(jnp.int32)[None], 0
    )
    labels = 3 * row_label[None] + col_label
    differs = labels[:, :, None] != labels[:, None, :]
    term = jnp.where(differs & (section == 1), -100.0, 0.0).astype(F32)
    return jnp.tile(term, (1, 1, GROUP))


def full_patches(layout, mp, tokens):
    wins = layout.wins
    place = jnp.arange(wins * SLOT)
    window, inner = place // SLOT, place % SLOT
    row = (mp // layout.across) * WIN + inner // WIN
    col = ((mp % layout.across) * wins + window) * WIN + inner % WIN
    token = jnp.where(inner < TOKENS, row * (WCOLS * WIN) + col, -1)
    return (token[:, None] == jnp.arange(tokens)[None]).astype(BF)


def whole_patches(layout, mp, tokens_here):
    token = mp * tokens_here + jnp.arange(tokens_here)
    row, col = token // (WCOLS * WIN), token % (WCOLS * WIN)
    window = col // WIN
    owner = (row // WIN) * layout.across + window // layout.wins
    place = owner * layout.wins * SLOT + (window % layout.wins) * SLOT + (row % WIN) * WIN + col % WIN
    return (place[:, None] == jnp.arange(layout.mp_count * layout.wins * SLOT)[None]).astype(BF)


def low_dot(matrix, stack):
    return jnp.einsum("pr,nrd->npd", matrix, stack, preferred_element_type=F32).astype(BF)


def body(
    layer_input,
    out_cotangent,
    norm_one_gain,
    norm_one_bias,
    attend_weight,
    attend_bias,
    position_table,
    output_weight,
    output_bias,
    norm_two_gain,
    norm_two_bias,
    expand_weight,
    expand_bias,
    reduce_weight,
    reduce_bias,
):
    row_count, mp_count = lax.axis_size("row"), lax.axis_size("mp")
    section, mp = lax.axis_index("section"), lax.axis_index("mp")
    layout = Layout(row_count, mp_count)
    tables = Tables(layout.wins)
    put = jnp.asarray(tables.put, BF)
    pick = jnp.asarray(tables.pick, BF)
    batches, tokens_here, width = layer_input.shape
    heads_here = attend_weight.shape[2]
    hidden_here = expand_weight.shape[2]
    row = lax.axis_index("row")
    sec = jnp.stack([section, row, mp]).astype(jnp.int32)
    paired = layout.across == 2 and row_count == 4
    first = section == 0

    flat = jnp.concatenate([attend_bias[0].reshape(-1), position_table[0].reshape(-1), expand_bias[0].reshape(-1)])
    wq_rows = attend_weight[0].transpose(1, 2, 0).reshape(heads_here, 3, 32, width)
    if paired:
        quarter = lambda array: take_at(array.reshape(4, -1, width), row)
        shards = (wq_rows.transpose(1, 0, 2, 3), output_weight[0], expand_weight[0], reduce_weight[0])
        quarters = [quarter(array) for array in shards]
        offsets = np.cumsum([0] + [array.shape[0] for array in quarters])[:-1].tolist()
        pieces, last_in = gather_quarter(jnp.concatenate(quarters))
        last_in, flat, layer_input, out_cotangent = lax.optimization_barrier((last_in, flat, layer_input, out_cotangent))
        after = ring(flat, "mp")
        flat_all = natural_ring([flat, after, ring(after, "mp"), ring(flat, "mp", -1)], mp)
    else:
        wq_all = lax.all_gather(wq_rows, "mp", axis=0).reshape(4, GROUP, 3, 32, width).transpose(0, 2, 1, 3, 4)
        wq_all = wq_all.reshape(4, GROUP * 96, width)
        wo_all = lax.all_gather(output_weight[0], "mp", axis=0).reshape(-1, width)
        w1_all = lax.all_gather(expand_weight[0], "mp", axis=0)
        w2_all = lax.all_gather(reduce_weight[0], "mp", axis=0)
        flat_all = lax.all_gather(flat, "mp", axis=0)
        whole = (wq_all, wo_all, w1_all, w2_all)
        weights = (whole, None, None, tuple(array.shape for array in whole))
    cut_one = heads_here * 64
    cut_two = cut_one + heads_here * position_table.shape[2]
    bias_all = flat_all[:, :cut_one].reshape(4, GROUP, 2, 32)
    table_all = flat_all[:, cut_one:cut_two].reshape(-1, position_table.shape[2])
    b1 = flat_all[:, cut_two:]
    bq = jnp.stack([bias_all[:, :, 0], jnp.zeros_like(bias_all[:, :, 0]), bias_all[:, :, 1]], axis=1).reshape(4, -1)
    onehot = table_onehot()
    bias = jnp.dot(table_all, onehot, precision=highest).reshape(4, GROUP, SLOT, SLOT).transpose(0, 2, 1, 3)
    bias = bias.reshape(4, SLOT, GROUP * SLOT) + jnp.where(jnp.arange(SLOT) < TOKENS, 0.0, -1e30)[None, :, None]
    vec = jnp.concatenate(
        [norm_one_gain, norm_one_bias, output_bias, norm_two_gain, norm_two_bias, reduce_bias, jnp.zeros((2, width), F32)]
    )
    region = region_mask(layout, section)

    taken = jnp.where(first, layer_input, out_cotangent)
    if paired:
        keep, take, send = pair_tables(layout.wins)
        side = mp % 2
        keep = lax.dynamic_index_in_dim(jnp.asarray(keep, BF), side, 0, keepdims=False)
        take = lax.dynamic_index_in_dim(jnp.asarray(take, BF), side, 0, keepdims=False)
        send = jnp.asarray(send, BF)
        arrived = swap(low_dot(send, taken), "mp", 1)
        pin = low_dot(jnp.concatenate([keep, take], axis=1), jnp.concatenate([taken, arrived], axis=1))
        own, give, take, up, land = (jnp.asarray(table, BF) for table in placing_tables(layout.wins))
        own, give, take = (take_at(take_at(table, section), side) for table in (own, give, take))
        land = jnp.where((section == 1) & (side == 0), land, 0)
    else:
        everything = lax.all_gather(taken, "mp", axis=1, tiled=True)
        pin = low_dot(full_patches(layout, mp, everything.shape[1]), everything)
    groups = -(-batches // TOGETHER)
    sizes = [min(TOGETHER, batches - TOGETHER * group) for group in range(groups)]
    pin = jnp.pad(pin, ((0, TOGETHER * groups - batches), (0, 0), (0, 0)))
    cuts = np.cumsum(tables.sizes)[:-1].tolist()
    targets = halo_inside(layout, jnp.split(low_dot(pick, pin), cuts, axis=1), False)
    if paired:
        arrays = [array for array, _ in pieces]
        arrays[0], pin, targets, bias, region, bq, b1 = lax.optimization_barrier((arrays[0], pin, targets, bias, region, bq, b1))
        held = tuple(places for _, places in pieces)
        held += tuple(tuple((bits + 1, back) for bits, back in places) for places in held)
        weights = (
            arrays + [swap(array, "row", 1) for array in arrays],
            held,
            offsets,
            ((4, GROUP * 96, width), (4 * GROUP * 32, width), (mp_count, width, hidden_here), (mp_count, hidden_here, width)),
        )

    static = dict(
        sec=sec, weights=weights, pin=pin, targets=targets, put=put, pick=pick, vec=vec, bq=bq, b1=b1, bias=bias, region=region
    )
    if paired:
        static |= dict(give=give, up=up)
    size_of = lambda group: sizes[group] if 0 <= group < groups else 0
    landed = None
    steps, pairs, ups = [], [], []
    for step in range(groups + 1):
        counts = (size_of(step), size_of(step - 1), size_of(step - 2), size_of(step - 1))
        which = (min(step, groups - 1), max(step - 1, 0))
        done = run_step(tables, static, landed, counts, which, steps[max(step - 2, 0)] if step else None)
        steps.append(done)
        sends = [done["s_" + name] for name in PIECES]
        pair, up_piece = done.get("f_pair"), done.get("f_up")
        if step == groups:
            sends = [piece[: sizes[-1]] for piece in sends]
        if paired:
            sends, pairs, ups = lax.optimization_barrier((sends, pairs, ups))
        landed = halo_swap(layout, sends, step == groups)
        if paired:
            if step == groups:
                break
            landed, pair, up_piece = lax.optimization_barrier((landed, pair, up_piece))
            pairs = pairs + [swap(pair, "mp", 1)]
            ups = ups + [[lax.ppermute(up_piece, AXES, route) for route in layout.up_routes()] if step else []]

    if not paired:
        halo = collect({name: [done["h_" + name] for done in steps[1:]] for name in PIECES[1:]})
        halo = [halo[name] for name in PIECES[1:]]
        flat_halo = halo_inside(layout, [None] + [array.reshape((-1,) + array.shape[3:]) for array in halo], True)[1:]
        halo = [flat.reshape(array.shape) for flat, array in zip(flat_halo, halo)]

    ahead_names = ("act", "n2", "a", "ctx")
    early = TOGETHER * (groups - 1)

    def gradient(names, terms, shapes, within, quartered, base, after):
        members, slots = {}, {}
        for name in names:
            shifts = (0, 1) if name in ahead_names else (2, 1)
            slots[name] = [[(batch // TOGETHER + shift, batch % TOGETHER) for batch in within] for shift in shifts]
            used = sorted({step for places in slots[name] for step, _ in places})
            members[name] = {step: steps[step][name + "_o"] for step in used}
        return run_weight_grad(dict(static, sec=after), members, slots, terms, shapes, quartered, base)

    mlp_names = ("act", "g", "n2", "dh")
    mlp_terms = (("act", "g", "left", "d2", 0, hidden_here), ("n2", "dh", "right", "d1", 0, width))
    mlp_shapes = {"d2": (mp_count, hidden_here, width), "d1": (mp_count, width, hidden_here)}
    base = gradient(mlp_names, mlp_terms, mlp_shapes, range(early), False, {}, sec)
    base = {name: base[name + "_o"] for name in mlp_shapes}
    landed, base = lax.optimization_barrier((landed, base))
    after = sec
    if paired:
        base, pair, up_piece = lax.optimization_barrier((base, pair, up_piece[:, : sizes[-1]]))
        pairs = pairs + [swap(pair, "mp", 1)]
        ups = ups + [[lax.ppermute(up_piece, AXES, route) for route in layout.up_routes()]]
        after, pairs, ups = lax.optimization_barrier((sec, pairs, ups))

    counts = (0, 0, sizes[-1], 0)
    which = (groups - 1, groups - 1)
    last = run_step(tables, static, landed, counts, which, steps[-2], attention=False)
    steps.append(last)
    mlp = gradient(mlp_names, mlp_terms, mlp_shapes, range(early, batches), paired, base, after)
    end = run_step(tables, static, None, counts, which, {**steps[-3], **last}, mlp=False)
    smalls = [done["small"] for done in steps[1:]] + [end["small"]]
    biases = [done["dbias"] for done in steps[1:-1]] + [end["dbias"]]
    if paired:
        d2, d1 = (mlp[name + "_keep"] + swap(mlp[name + "_send"], "row", 1) for name in ("d2", "d1"))
        d2, d1, end_dqkv = lax.optimization_barrier((d2, d1, end["dqkv_o"]))
        end = {**end, "dqkv_o": end_dqkv}
    steps[-1] = {**last, **end}
    heads = gradient(
        ("dqkv", "a", "ctx", "gm"),
        (("dqkv", "a", "left", "da", 0, GROUP * 96), ("ctx", "gm", "left", "da", GROUP * 96, GROUP * 32)),
        {"da": (4, GROUP * 128, width)},
        range(batches),
        paired,
        {},
        sec,
    )
    smalls, biases, _ = lax.optimization_barrier((smalls, biases, heads))
    small, dbias = sum(smalls), sum(biases)
    table = dbias.reshape(SLOT, 4 * GROUP, SLOT).transpose(1, 0, 2).reshape(4 * GROUP, -1)
    table = jnp.dot(table, onehot.T, precision=highest)
    if paired:
        count = table.size
        table = jnp.pad(table.reshape(-1), (0, -count % 2048)).reshape(-1, 2048)
        sums = jnp.concatenate([small, table])
        high, core = row // 2, row % 2
        gate = lax.optimization_barrier
        term = lambda part, step: take_at(part, (mp - 2 - step) % mp_count)

        def joined(pair, crossed):
            whole = jnp.stack([jnp.where(core == 0, pair, crossed), jnp.where(core == 0, crossed, pair)], axis=1)
            return whole.astype(F32).reshape(-1, width)

        def ordered(mine, other):
            return jnp.stack([jnp.where(high == 0, mine, other), jnp.where(high == 0, other, mine)])

        da_came, pair_came, sums_came = swap(heads["da_send"], "row", 1), swap(end["f_pair"], "mp", 1), swap(sums, "row", 1)
        d2_came, d1_came = ring(take_at(d2, (mp - 1) % mp_count), "mp"), swap(take_at(d1, 1 - high, 1), "row", 2)
        da = heads["da_keep"] + da_came
        mine, other = take_at(da, high, 1), take_at(da, 1 - high, 1)
        da_came = swap(other, "row", 2)
        d2_came, d1_came, pair_came, sums_came, _ = gate((d2_came, d1_came, pair_came, sums_came, other))
        d2_total, d1, sums = d2_came + term(d2, 0), take_at(d1, high, 1) + d1_came, sums + sums_came
        d2_came, d1_came, sums_came = ring(d2_total, "mp"), ring(take_at(d1, (mp - 1) % mp_count), "mp"), swap(sums, "row", 2)
        placed = run_places(static, steps, pairs + [pair_came], ups + [[]], own, take, land, sizes, tokens_here)
        da_came, first_out, second_out = gate((da_came, placed["first"], placed["second"]))
        da = mine + da_came
        sending = take_at(da, (mp - 1) % mp_count)
        da_came = ring(sending, "mp")
        d2_came, d1_came, sums_came, _ = gate((d2_came, d1_came, sums_came, sending))
        d2_total, d1_total, sums = d2_came + term(d2, 1), d1_came + term(d1, 0), sums + sums_came
        d2_came, d1_came, sums_came = ring(d2_total, "mp"), ring(d1_total, "mp"), swap(sums, "mp", 1)
        sending = da_came + term(da, 0)
        da_came = ring(sending, "mp")
        d2_came, d1_came, sums_came, _ = gate((d2_came, d1_came, sums_came, sending))
        d2, d1_total, sums = d2_came + term(d2, 2), d1_came + term(d1, 1), sums + sums_came
        d2_came, d1_came, sums_came = swap(d2, "row", 2), ring(d1_total, "mp"), swap(sums, "mp", 2)
        sending = da_came + term(da, 1)
        da_came = ring(sending, "mp")
        d2_came, d1_came, sums_came, _ = gate((d2_came, d1_came, sums_came, sending))
        d2, d1, sums = d2 + d2_came, d1_came + term(d1, 2), sums + sums_came
        d2_came, d1_came = swap(d2, "row", 1), swap(d1, "row", 2)
        da = da_came + term(da, 2)
        da_came = swap(da, "row", 2)
        d2_came, d1_came, _ = gate((d2_came, d1_came, da))
        d2, d1 = joined(d2, d2_came), ordered(d1, d1_came)
        d1_came = swap(d1, "row", 1)
        da = ordered(da, da_came)
        d1 = joined(d1, d1_came)
        da = joined(da, swap(da, "row", 1))
        dq, do = da[: GROUP * 96].reshape(3, GROUP, 32, width), da[GROUP * 96 :]
        dq = dq.transpose(3, 1, 0, 2).reshape(attend_weight.shape[1:])
        small, table = sums[: small.shape[0]], sums[small.shape[0] :].reshape(-1)[:count].reshape(4 * GROUP, -1)
    else:

        def shared(parts):
            part = lax.psum_scatter(parts, "mp", scatter_dimension=0, tiled=False)
            return lax.psum(part, "row").astype(F32)

        da = heads["da_o"]
        dq = da[:, : GROUP * 96].reshape(4, 3, GROUP, 32, width).transpose(0, 2, 1, 3, 4).reshape(mp_count, heads_here * 96, width)
        d2, d1, do = shared(mlp["d2_o"]), shared(mlp["d1_o"]), shared(da[:, GROUP * 96 :].reshape(mp_count, heads_here * 32, width))
        dq = shared(dq).T.reshape(attend_weight.shape[1:])
        small, table = lax.psum((small, table), ("row", "mp"))
    shift = small[3, :1536].reshape(4, 3, GROUP, 32)
    shift = jnp.concatenate([shift[:, 0], shift[:, 2]], axis=-1).reshape(4 * GROUP, 64)
    mine = lambda array: lax.dynamic_index_in_dim(array.reshape((mp_count, -1) + array.shape[1:]), mp, 0, keepdims=False)

    if not paired:
        plain = [(steps[group]["y_o"], steps[group + 2]["dx_o"]) for group in range(groups)]
        mains = [steps[group + 1]["h_main"] for group in range(groups)]
        made = run_patches(static, plain, mains, halo, sizes)
        everything = lax.all_gather(made["patch"], "mp", axis=1, tiled=True)
        placed = low_dot(whole_patches(layout, mp, tokens_here), everything)
        first_out, second_out = placed[:batches], placed[batches:].astype(F32)

    return (
        first_out[None],
        second_out[None],
        small[1, 1024:1536][None],
        small[1, 1536:2048][None],
        dq[None],
        mine(shift)[None],
        mine(table)[None],
        do.reshape(output_weight.shape),
        small[1, 512:1024][None],
        small[2, 0:512][None],
        small[2, 512:1024][None],
        d1[None],
        mine(small[0])[None],
        d2[None],
        small[1, 0:512][None],
    )


def solution(mesh):
    return jax.shard_map(
        body,
        mesh=mesh,
        in_specs=(
            P(None, ("row", "mp"), None),
            P(None, ("row", "mp"), None),
            P("section", None),
            P("section", None),
            P("section", None, "mp", None),
            P("section", "mp", None),
            P("section", "mp", None),
            P("section", "mp", None, None),
            P("section", None),
            P("section", None),
            P("section", None),
            P("section", None, "mp"),
            P("section", "mp"),
            P("section", "mp", None),
            P("section", None),
        ),
        out_specs=(
            P("section", None, ("row", "mp"), None),
            P("section", None, ("row", "mp"), None),
            P("section", None),
            P("section", None),
            P("section", None, "mp", None),
            P("section", "mp", None),
            P("section", "mp", None),
            P("section", "mp", None, None),
            P("section", None),
            P("section", None),
            P("section", None),
            P("section", None, "mp"),
            P("section", "mp"),
            P("section", "mp", None),
            P("section", None),
        ),
        check_vma=False,
    )
```

time: 439 us -> 391 us (0.89)
  local copies, waits for them, and re-layouts: 71.3 us -> 32.2 us
  Pallas kernels: 130 us -> 139 us
  waiting for transfers between devices: 91.2 us -> 82.3 us
  matrix products: 13.9 us -> 7.89 us
    unnamed x239 -> x127, local copies, waits for them, and re-layouts: 47.2 us -> 4.74 us
    ppermute x24 -> x27, waiting for transfers between devices: 54.1 us -> 28.9 us  [swap(): lax.ppermute(shard, axis, [(i, i ^ bit) for i in range(lax.axis_size(axis...]
    ppermute x24 -> x22, waiting for transfers between devices: 3.07 us -> 20.3 us  [the longest x16 16.5 us: halo_swap(): lax.ppermute(part, AXES, [(b, a) for a, b in there] + ([] if back_only el...]
    ppermute x24 -> x27, starting transfers between devices: 34.5 us -> 23.5 us  [swap(): lax.ppermute(shard, axis, [(i, i ^ bit) for i in range(lax.axis_size(axis...]
    ppermute x15, waiting for transfers between devices: 34 us -> 24.6 us  [ring(): lax.ppermute(shard, axis, [(i, (i + by) % count) for i in range(count)])]
    ppermute x15, starting transfers between devices: 7.72 us -> 17 us  [ring(): lax.ppermute(shard, axis, [(i, (i + by) % count) for i in range(count)])]
    pallas_call x9 -> x10, Pallas kernels: 130 us -> 139 us  [call(): pl.pallas_call(wrapped, grid=(1,), out_shape=[shape for shape, _ in outs....]
    ppermute x6 -> x3, waiting for transfers between devices: 0.02 us -> 8.47 us  [halo_inside(): lax.ppermute(part, AXES, [(b, a) for a, b in there] if back else there)]
  transfers between devices with their start and end apart: 69 -> 67, of which waited for: 20 -> 23; matrix products, arithmetic and copies ran while one was open for 20% -> 13% of each run, Pallas kernels for 10% -> 32%
where the time goes in v3:
time: 391 us; the launch traced here: 383 us
  Pallas kernels  139 us (36%)
  starting transfers between devices  104 us (27%)
  waiting for transfers between devices  82.3 us (21%)
  local copies, waits for them, and re-layouts  32.2 us (8%)
  other arithmetic  15.3 us (4%)
  matrix products  7.89 us (2%)
    pallas_call x10, Pallas kernels, call(): pl.pallas_call(wrapped, grid=(1,), out_shape=[shape for shape, _ in outs....  139 us
    ppermute x16, starting transfers between devices, halo_swap(): lax.ppermute(part, AXES, [(b, a) for a, b in there] + ([] if back_only el...  29.7 us
    ppermute x27, waiting for transfers between devices, swap(): lax.ppermute(shard, axis, [(i, i ^ bit) for i in range(lax.axis_size(axis...  28.9 us
    ppermute x15, waiting for transfers between devices, ring(): lax.ppermute(shard, axis, [(i, (i + by) % count) for i in range(count)])  24.6 us
    ppermute x27, starting transfers between devices, swap(): lax.ppermute(shard, axis, [(i, i ^ bit) for i in range(lax.axis_size(axis...  23.5 us
    ppermute x6, starting transfers between devices, body(): lax.ppermute(up_piece, AXES, route)  20.2 us
    ppermute x15, starting transfers between devices, ring(): lax.ppermute(shard, axis, [(i, (i + by) % count) for i in range(count)])  17 us
    ppermute x16, waiting for transfers between devices, halo_swap(): lax.ppermute(part, AXES, [(b, a) for a, b in there] + ([] if back_only el...  16.5 us
  transfers between devices with their start and end apart: 67, of which 23 were waited for; matrix products, arithmetic and copies ran while one was open for 13% of the time, Pallas kernels for 32%

profile of v3, /device:TPU:3, one launch (start us, length us, event | category | flops | bytes accessed | tf_op | source)
XLA Modules:
  0.0 383.2 jit_solution(1234706564479453971)
XLA Ops:
  9.1 6.7 %collective-permute-done = bf16[384,512]{1,0:T(8,128)(2,1)S(1)} collective-permute-done((bf16[384,512]{1,0:T(8,128)(2,1)}, bf16[384,512]{1,0:T(8,128)(2,1)S(1)}, u32[]{:S(2)}, u32[]{:S(2)}) %collective-permute-start) | collective-permute-done | bytes 393248 | tf_op jit(solution)/shard_map/ppermute | solution.py:172
  22.2 4.0 %collective-permute-done.11 = bf16[384,512]{1,0:T(8,128)(2,1)} collective-permute-done((bf16[384,512]{1,0:T(8,128)(2,1)}, bf16[384,512]{1,0:T(8,128)(2,1)}, u32[]{:S(2)}, u32[]{:S(2)}) %collective-permute-start.11) | collective-permute-done | bytes 393248 | tf_op jit(solution)/shard_map/ppermute | solution.py:172
  26.2 5.3 %collective-permute-done.3 = bf16[384,512]{1,0:T(8,128)(2,1)} collective-permute-done((bf16[384,512]{1,0:T(8,128)(2,1)S(1)}, bf16[384,512]{1,0:T(8,128)(2,1)}, u32[]{:S(2)}, u32[]{:S(2)}) %collective-permute-start.3) | collective-permute-done | bytes 393248 | tf_op jit(solution)/shard_map/ppermute | solution.py:172
  41.3 4.6 %collective-permute-done.9 = f32[1444]{0:T(1024)S(1)} collective-permute-done((f32[1444]{0:T(1024)S(1)}, f32[1444]{0:T(1024)S(1)}, u32[]{:S(2)}, u32[]{:S(2)}) %collective-permute-start.9) | collective-permute-done | bytes 5808 | tf_op jit(solution)/shard_map/ppermute | solution.py:172
  53.6 5.4 %collective-permute-start.5 = (bf16[6,80,512]{2,1,0:T(8,128)(2,1)S(1)}, bf16[6,80,512]{2,1,0:T(8,128)(2,1)}, u32[]{:S(2)}, u32[]{:S(2)}) collective-permute-start(bf16[6,80,512]{2,1,0:T(8,128)(2,1)S(1)} %split.17), channel_id=1, source_target_pairs={{16,30},{17,31},{18,16},{19,17},{20,18},{21,19},{22,20},{23,21},{2... | collective-permute-start | bytes 1474568 | tf_op jit(solution)/shard_map/ppermute | solution.py:166
  59.7 4.1 %collective-permute-start.6 = (bf16[6,16,512]{2,1,0:T(8,128)(2,1)S(1)}, bf16[6,16,512]{2,1,0:T(8,128)(2,1)S(1)}, u32[]{:S(2)}, u32[]{:S(2)}) collective-permute-start(bf16[6,16,512]{2,1,0:T(8,128)(2,1)S(1)} %get-tuple-element.477), channel_id=1, source_target_pairs={{16,17},{17,16},{18,19},{19,18},{20,21},{21,20},{22,23},{23,22},{2... | collective-permute-start | bytes 294920 | tf_op jit(solution)/shard_map/ppermute | solution.py:166
  63.8 4.4 %collective-permute-start.7 = (bf16[6,16,512]{2,1,0:T(8,128)(2,1)S(1)}, bf16[6,16,512]{2,1,0:T(8,128)(2,1)S(1)}, u32[]{:S(2)}, u32[]{:S(2)}) collective-permute-start(bf16[6,16,512]{2,1,0:T(8,128)(2,1)S(1)} %get-tuple-element.476), channel_id=1, source_target_pairs={{16,31},{17,30},{18,17},{19,16},{20,19},{21,18},{22,21},{23,20},{2... | collective-permute-start | bytes 294920 | tf_op jit(solution)/shard_map/ppermute | solution.py:166
  73.3 7.4 %collective-permute-done.5.refs_20_.refs_13_ = bf16[6,80,512]{2,1,0:T(8,128)(2,1)} collective-permute-done((bf16[6,80,512]{2,1,0:T(8,128)(2,1)S(1)}, bf16[6,80,512]{2,1,0:T(8,128)(2,1)}, u32[]{:S(2)}, u32[]{:S(2)}) %collective-permute-start.5) | collective-permute-done | bytes 491552 | tf_op jit(solution)/shard_map/ppermute | solution.py:166
  87.0 7.1 %layer_step.6 = (bf16[2,2,96,512]{3,2,1,0:T(8,128)(2,1)}, bf16[2,2,96,512]{3,2,1,0:T(8,128)(2,1)}, bf16[2,112,512]{2,1,0:T(8,128)(2,1)}, bf16[2,80,512]{2,1,0:T(...) custom-call(s32[3]{0:T(128)} %pad_add_fusion.refs_0_, ...), custom_call_target="tpu_custom_call" | custom-call | flops 1 | bytes 1 | tf_op jit(solution)/shard_map/layer_step/pallas_call | solution.py:625
  94.2 6.3 %collective-permute-start.17 = (bf16[2,80,512]{2,1,0:T(8,128)(2,1)}, bf16[2,80,512]{2,1,0:T(8,128)(2,1)S(1)}, u32[]{:S(2)}, u32[]{:S(2)}) collective-permute-start(bf16[2,80,512]{2,1,0:T(8,128)(2,1)} %get-tuple-element.237), channel_id=1, source_target_pairs={{30,0},{31,1},{16,2},{17,3},{18,4},{19,5},{20,6},{21,7},{22,8},{23... | collective-permute-start | bytes 491528 | tf_op jit(solution)/shard_map/ppermute | solution.py:158
  110.0 33.3 %layer_step.7 = (bf16[2,2,96,512]{3,2,1,0:T(8,128)(2,1)}, bf16[2,2,96,512]{3,2,1,0:T(8,128)(2,1)}, bf16[2,112,512]{2,1,0:T(8,128)(2,1)}, bf16[2,80,512]{2,1,0:T(...) custom-call(s32[3]{0:T(128)} %pad_add_fusion.refs_0_, ...), custom_call_target="tpu_custom_call" | custom-call | flops 1 | bytes 1 | tf_op jit(solution)/shard_map/layer_step/pallas_call | solution.py:625
  156.4 5.6 %collective-permute-start.26 = (bf16[2,2,96,512]{3,2,1,0:T(8,128)(2,1)}, bf16[2,2,96,512]{3,2,1,0:T(8,128)(2,1)S(1)}, u32[]{:S(2)}, u32[]{:S(2)}) collective-permute-start(bf16[2,2,96,512]{3,2,1,0:T(8,128)(2,1)} %get-tuple-element.277), channel_id=1, source_target_pairs={{16,18},{18,20},{20,22},{22,24},{24,26},{26,28},{28,30},{30,16}} | collective-permute-start | bytes 1179656 | tf_op jit(solution)/shard_map/ppermute | solution.py:1058
  163.6 33.1 %layer_step.8 = (bf16[2,2,96,512]{3,2,1,0:T(8,128)(2,1)}, bf16[2,2,96,512]{3,2,1,0:T(8,128)(2,1)}, bf16[2,112,512]{2,1,0:T(8,128)(2,1)}, bf16[2,80,512]{2,1,0:T(...) custom-call(s32[3]{0:T(128)} %pad_add_fusion.refs_0_, ...), custom_call_target="tpu_custom_call" | custom-call | flops 1 | bytes 1 | tf_op jit(solution)/shard_map/layer_step/pallas_call | solution.py:625
  210.8 5.5 %collective-permute-start.33 = (bf16[2,2,96,512]{3,2,1,0:T(8,128)(2,1)}, bf16[2,2,96,512]{3,2,1,0:T(8,128)(2,1)S(1)}, u32[]{:S(2)}, u32[]{:S(2)}) collective-permute-start(bf16[2,2,96,512]{3,2,1,0:T(8,128)(2,1)} %get-tuple-element.303), channel_id=1, source_target_pairs={{16,18},{18,20},{20,22},{22,24},{24,26},{26,28},{28,30},{30,16}} | collective-permute-start | bytes 1179656 | tf_op jit(solution)/shard_map/ppermute | solution.py:1058
  217.6 19.4 %layer_step.9 = (bf16[2,2,96,512]{3,2,1,0:T(8,128)(2,1)}, bf16[2,2,96,512]{3,2,1,0:T(8,128)(2,1)}, bf16[2,112,512]{2,1,0:T(8,128)(2,1)}, bf16[2,80,512]{2,1,0:T(...) custom-call(s32[3]{0:T(128)} %pad_add_fusion.refs_0_, ...), custom_call_target="tpu_custom_call" | custom-call | flops 1 | bytes 1 | tf_op jit(solution)/shard_map/layer_step/pallas_call | solution.py:625
  248.0 9.9 %weight_grad.3 = (bf16[4,512,512]{2,1,0:T(8,128)(2,1)}, bf16[4,512,512]{2,1,0:T(8,128)(2,1)}) custom-call(s32[3]{0:T(128)} %pad_add_fusion.refs_0_, bf16[2,256,2048]{2,1,0:T(8,128)(2,1)} %get-tuple-element.311.refs_1_, bf16[2,256,2048]{2,1,0:T(8,128)(2,1)} %get-tuple-element.312.refs_2_, bf16[2,256,2048]{2,1,0:T(8,128)(2,1)} %get-tuple-element.313.refs_3_.refs_1_, ...), custom_call_target="tpu_custom_call" | custom-call | flops 1 | bytes 1 | tf_op jit(solution)/shard_map/weight_grad/pallas_call | solution.py:625
  258.5 5.0 %collective-permute-start.40 = (bf16[2,1,96,512]{3,2,1,0:T(8,128)(2,1)S(1)}, bf16[2,1,96,512]{3,2,1,0:T(8,128)(2,1)S(1)}, u32[]{:S(2)}, u32[]{:S(2)}) collective-permute-start(bf16[2,1,96,512]{3,2,1,0:T(8,128)(2,1)S(1)} %slice.96), channel_id=1, source_target_pairs={{16,18},{18,20},{20,22},{22,24},{24,26},{26,28},{28,30},{30,16}} | collective-permute-start | bytes 589832 | tf_op jit(solution)/shard_map/ppermute | solution.py:1088
  264.8 5.9 %layer_step.10 = (f32[8,2048]{1,0:T(8,128)}, bf16[2,256,512]{2,1,0:T(8,128)(2,1)}, bf16[2,256,2048]{2,1,0:T(8,128)(2,1)}, bf16[2,256,512]{2,1,0:T(8,128)(2,1)}, f32[2,256,512]{2,1,0:T(8,128)}) custom-call(s32[3]{0:T(128)} %pad_add_fusion.refs_0_, bf16[256,224]{1,0:T(8,128)(2,1)} %constant.336.clone.refs_1_, bf16[224,256]{1,0:T(8,128)(2,1)} %constant.337.clone.refs_2_, ...), custom_call_target="tpu_custom_call" | custom-call | flops 1 | bytes 1 | tf_op jit(solution)/shard_map/layer_step/pallas_call | solution.py:625
  276.5 7.2 %weight_grad.4 = (bf16[4,2,128,512]{3,2,1,0:T(8,128)(2,1)}, bf16[4,2,128,512]{3,2,1,0:T(8,128)(2,1)}, bf16[4,2,128,512]{3,2,1,0:T(8,128)(2,1)}, bf16[4,2,128,512]{3,2,1,0:T(8,128)(2,1)}) custom-call(s32[3]{0:T(128)} %pad_add_fusion.refs_0_, bf16[2,256,2048]{2,1,0:T(8,128)(2,1)} %get-tuple-element.313.refs_3_.refs_1_, ...), custom_call_target="tpu_custom_call" | custom-call | flops 1 | bytes 1 | tf_op jit(solution)/shard_map/weight_grad/pallas_call | solution.py:625
  289.2 5.3 %layer_step.11 = (bf16[2,2,96,512]{3,2,1,0:T(8,128)(2,1)}, f32[64,1024]{1,0:T(8,128)}, f32[8,2048]{1,0:T(8,128)}, bf16[2,256,1536]{2,1,0:T(8,128)(2,1)}, bf16[2,256,512]{2,1,0:T(8,128)(2,1)}) custom-call(s32[3]{0:T(128)} %pad_add_fusion.refs_0_, bf16[256,224]{1,0:T(8,128)(2,1)} %constant.336.clone.refs_1_, bf16[224,256]{1,0:T(8,128)(2,1)} %constant.337.clone.refs_2_, ...), custom_call_target="tpu_custom_call" | custom-call | flops 1 | bytes 1 | tf_op jit(solution)/shard_map/layer_step/pallas_call | solution.py:625
  296.1 8.2 %weight_grad.5 = (bf16[4,2,128,512]{3,2,1,0:T(8,128)(2,1)}, bf16[4,2,128,512]{3,2,1,0:T(8,128)(2,1)}) custom-call(s32[3]{0:T(128)} %pad_add_fusion.refs_0_, bf16[2,256,1536]{2,1,0:T(8,128)(2,1)} %get-tuple-element.254.refs_1_, bf16[2,256,1536]{2,1,0:T(8,128)(2,1)} %get-tuple-element.270.refs_2_, bf16[2,256,1536]{2,1,0:T(8,128)(2,1)} %get-tuple-element.293.refs_3_, ...), custom_call_target="tpu_custom_call" | custom-call | flops 1 | bytes 1 | tf_op jit(solution)/shard_map/weight_grad/pallas_call | solution.py:625
  324.3 9.2 %places.1 = (bf16[5,196,512]{2,1,0:T(8,128)(2,1)}, f32[5,196,512]{2,1,0:T(8,128)}) custom-call(s32[3]{0:T(128)} %pad_add_fusion.refs_0_, bf16[256,196]{1,0:T(8,128)(2,1)} %dynamic-slice_bitcast_fusion.5.refs_1_, bf16[96,196]{1,0:T(8,128)(2,1)} %dynamic-slice_bitcast_fusion.11.refs_2_, bf16[96,196]{1,0:T(8,128)(2,1)} %get-tuple-element.497.refs_3_, ...), custom_call_target="tpu_custom_call" | custom-call | tf_op jit(solution)/shard_map/places/pallas_call | solution.py:625
  342.9 10.7 %collective-permute-done.55 = f32[10,2048]{1,0:T(8,128)S(1)} collective-permute-done((f32[10,2048]{1,0:T(8,128)S(1)}, f32[10,2048]{1,0:T(8,128)S(1)}, u32[]{:S(2)}, u32[]{:S(2)}) %collective-permute-start.55) | collective-permute-done | bytes 81952 | tf_op jit(solution)/shard_map/ppermute | solution.py:176
  361.3 9.5 %collective-permute-done.59 = f32[10,2048]{1,0:T(8,128)S(1)} collective-permute-done((f32[10,2048]{1,0:T(8,128)S(1)}, f32[10,2048]{1,0:T(8,128)S(1)}, u32[]{:S(2)}, u32[]{:S(2)}) %collective-permute-start.59) | collective-permute-done | bytes 81952 | tf_op jit(solution)/shard_map/ppermute | solution.py:176
  (370 shorter events, 157.6 us)
Async XLA Ops:
  4.9 32.3 %collective-permute-start.1 = (bf16[384,512]{1,0:T(8,128)(2,1)}, bf16[384,512]{1,0:T(8,128)(2,1)}, u32[]{:S(2)}, u32[]{:S(2)}) collective-permute-start(bf16[384,512]{1,0:T(8,128)(2,1)} %get-tuple-element.485), channel_id=1, source_target_pairs={{0,8},{4,12},{8,0},{12,4},{1,9},{5,13},{9,1},{13,5},{2,10},{6,14},... | collective-permute-start | bytes 1179656 | tf_op jit(solution)/shard_map/ppermute | solution.py:176
  6.2 20.0 %collective-permute-start.11 = (bf16[384,512]{1,0:T(8,128)(2,1)}, bf16[384,512]{1,0:T(8,128)(2,1)}, u32[]{:S(2)}, u32[]{:S(2)}) collective-permute-start(bf16[384,512]{1,0:T(8,128)(2,1)} %get-tuple-element.485), channel_id=1, source_target_pairs={{0,3},{1,0},{2,1},{3,2},{4,7},{5,4},{6,5},{7,6},{8,11},{9,8},{10,9... | collective-permute-start | bytes 1179656 | tf_op jit(solution)/shard_map/ppermute | solution.py:172
  15.8 15.7 %collective-permute-start.3 = (bf16[384,512]{1,0:T(8,128)(2,1)S(1)}, bf16[384,512]{1,0:T(8,128)(2,1)}, u32[]{:S(2)}, u32[]{:S(2)}) collective-permute-start(bf16[384,512]{1,0:T(8,128)(2,1)S(1)} %collective-permute-done), channel_id=1, source_target_pairs={{0,1},{1,2},{2,3},{3,0},{4,5},{5,6},{6,7},{7,4},{8,9},{9,10},{10,1... | collective-permute-start | bytes 1179656 | tf_op jit(solution)/shard_map/ppermute | solution.py:172
  21.0 17.7 %collective-permute-start.2 = (bf16[384,512]{1,0:T(8,128)(2,1)S(1)}, bf16[384,512]{1,0:T(8,128)(2,1)S(1)}, u32[]{:S(2)}, u32[]{:S(2)}) collective-permute-start(bf16[384,512]{1,0:T(8,128)(2,1)S(1)} %collective-permute-done), channel_id=1, source_target_pairs={{0,8},{4,12},{8,0},{12,4},{1,9},{5,13},{9,1},{13,5},{2,10},{6,14},... | collective-permute-start | bytes 1179656 | tf_op jit(solution)/shard_map/ppermute | solution.py:176
  26.2 42.1 %collective-permute-start.12 = (bf16[384,512]{1,0:T(8,128)(2,1)}, bf16[384,512]{1,0:T(8,128)(2,1)}, u32[]{:S(2)}, u32[]{:S(2)}) collective-permute-start(bf16[384,512]{1,0:T(8,128)(2,1)} %collective-permute-done.11), channel_id=1, source_target_pairs={{0,8},{4,12},{8,0},{12,4},{1,9},{5,13},{9,1},{13,5},{2,10},{6,14},... | collective-permute-start | bytes 1179656 | tf_op jit(solution)/shard_map/ppermute | solution.py:176
  39.9 28.3 %collective-permute-start.13 = (bf16[384,512]{1,0:T(8,128)(2,1)}, bf16[384,512]{1,0:T(8,128)(2,1)}, u32[]{:S(2)}, u32[]{:S(2)}) collective-permute-start(bf16[384,512]{1,0:T(8,128)(2,1)} %collective-permute-done.3), channel_id=1, source_target_pairs={{0,8},{4,12},{8,0},{12,4},{1,9},{5,13},{9,1},{13,5},{2,10},{6,14},... | collective-permute-start | bytes 1179656 | tf_op jit(solution)/shard_map/ppermute | solution.py:176
  53.6 27.1 %collective-permute-start.5 = (bf16[6,80,512]{2,1,0:T(8,128)(2,1)S(1)}, bf16[6,80,512]{2,1,0:T(8,128)(2,1)}, u32[]{:S(2)}, u32[]{:S(2)}) collective-permute-start(bf16[6,80,512]{2,1,0:T(8,128)(2,1)S(1)} %split.17), channel_id=1, source_target_pairs={{16,30},{17,31},{18,16},{19,17},{20,18},{21,19},{22,20},{23,21},{2... | collective-permute-start | bytes 1474568 | tf_op jit(solution)/shard_map/ppermute | solution.py:166
  69.8 16.7 %collective-permute-start.15 = (bf16[4,384,512]{2,1,0:T(8,128)(2,1)S(1)}, bf16[4,384,512]{2,1,0:T(8,128)(2,1)}, u32[]{:S(2)}, u32[]{:S(2)}) collective-permute-start(bf16[4,384,512]{2,1,0:T(8,128)(2,1)S(1)} %pad_maximum_fusion.1.refs_5_.refs_9_), channel_id=1, source_target_pairs={{0,4},{4,0},{8,12},{12,8},{1,5},{5,1},{9,13},{13,9},{2,6},{6,2},{1... | collective-permute-start | bytes 4718600 | tf_op jit(solution)/shard_map/ppermute | solution.py:176
  108.9 34.4 %collective-permute-start.20 = (bf16[2,2,96,512]{3,2,1,0:T(8,128)(2,1)}, bf16[2,2,96,512]{3,2,1,0:T(8,128)(2,1)S(1)}, u32[]{:S(2)}, u32[]{:S(2)}) collective-permute-start(bf16[2,2,96,512]{3,2,1,0:T(8,128)(2,1)} %get-tuple-element.259), channel_id=1, source_target_pairs={{0,1},{1,0},{2,3},{3,2},{4,5},{5,4},{6,7},{7,6},{8,9},{9,8},{10,11... | collective-permute-start | bytes 1179656 | tf_op jit(solution)/shard_map/ppermute | solution.py:176
  155.2 41.5 %collective-permute-start.25 = (bf16[2,2,96,512]{3,2,1,0:T(8,128)(2,1)}, bf16[2,2,96,512]{3,2,1,0:T(8,128)(2,1)S(1)}, u32[]{:S(2)}, u32[]{:S(2)}) collective-permute-start(bf16[2,2,96,512]{3,2,1,0:T(8,128)(2,1)} %get-tuple-element.276), channel_id=1, source_target_pairs={{0,1},{1,0},{2,3},{3,2},{4,5},{5,4},{6,7},{7,6},{8,9},{9,8},{10,11... | collective-permute-start | bytes 1179656 | tf_op jit(solution)/shard_map/ppermute | solution.py:176
  156.4 40.3 %collective-permute-start.26 = (bf16[2,2,96,512]{3,2,1,0:T(8,128)(2,1)}, bf16[2,2,96,512]{3,2,1,0:T(8,128)(2,1)S(1)}, u32[]{:S(2)}, u32[]{:S(2)}) collective-permute-start(bf16[2,2,96,512]{3,2,1,0:T(8,128)(2,1)} %get-tuple-element.277), channel_id=1, source_target_pairs={{16,18},{18,20},{20,22},{22,24},{24,26},{26,28},{28,30},{30,16}} | collective-permute-start | bytes 1179656 | tf_op jit(solution)/shard_map/ppermute | solution.py:1058
  162.0 34.7 %collective-permute-start.27 = (bf16[2,2,96,512]{3,2,1,0:T(8,128)(2,1)}, bf16[2,2,96,512]{3,2,1,0:T(8,128)(2,1)S(1)}, u32[]{:S(2)}, u32[]{:S(2)}) collective-permute-start(bf16[2,2,96,512]{3,2,1,0:T(8,128)(2,1)} %get-tuple-element.277), channel_id=1, source_target_pairs={{17,18},{19,20},{21,22},{23,24},{25,26},{27,28},{29,30},{31,16}} | collective-permute-start | bytes 1179656 | tf_op jit(solution)/shard_map/ppermute | solution.py:1058
  208.7 31.6 %collective-permute-start.32 = (bf16[2,2,96,512]{3,2,1,0:T(8,128)(2,1)}, bf16[2,2,96,512]{3,2,1,0:T(8,128)(2,1)S(1)}, u32[]{:S(2)}, u32[]{:S(2)}) collective-permute-start(bf16[2,2,96,512]{3,2,1,0:T(8,128)(2,1)} %get-tuple-element.300), channel_id=1, source_target_pairs={{0,1},{1,0},{2,3},{3,2},{4,5},{5,4},{6,7},{7,6},{8,9},{9,8},{10,11... | collective-permute-start | bytes 1179656 | tf_op jit(solution)/shard_map/ppermute | solution.py:176
  210.8 29.5 %collective-permute-start.33 = (bf16[2,2,96,512]{3,2,1,0:T(8,128)(2,1)}, bf16[2,2,96,512]{3,2,1,0:T(8,128)(2,1)S(1)}, u32[]{:S(2)}, u32[]{:S(2)}) collective-permute-start(bf16[2,2,96,512]{3,2,1,0:T(8,128)(2,1)} %get-tuple-element.303), channel_id=1, source_target_pairs={{16,18},{18,20},{20,22},{22,24},{24,26},{26,28},{28,30},{30,16}} | collective-permute-start | bytes 1179656 | tf_op jit(solution)/shard_map/ppermute | solution.py:1058
  216.3 24.0 %collective-permute-start.34 = (bf16[2,2,96,512]{3,2,1,0:T(8,128)(2,1)}, bf16[2,2,96,512]{3,2,1,0:T(8,128)(2,1)S(1)}, u32[]{:S(2)}, u32[]{:S(2)}) collective-permute-start(bf16[2,2,96,512]{3,2,1,0:T(8,128)(2,1)} %get-tuple-element.303), channel_id=1, source_target_pairs={{17,18},{19,20},{21,22},{23,24},{25,26},{27,28},{29,30},{31,16}} | collective-permute-start | bytes 1179656 | tf_op jit(solution)/shard_map/ppermute | solution.py:1058
  240.3 17.8 %collective-permute-start.35 = (bf16[1,112,512]{2,1,0:T(8,128)(2,1)S(1)}, bf16[1,112,512]{2,1,0:T(8,128)(2,1)S(1)}, u32[]{:S(2)}, u32[]{:S(2)}) collective-permute-start(bf16[1,112,512]{2,1,0:T(8,128)(2,1)S(1)} %slice.92), channel_id=1, source_target_pairs={{16,0},{17,1},{18,2},{19,3},{20,4},{21,5},{22,6},{23,7},{24,8},{25... | collective-permute-start | bytes 344072 | tf_op jit(solution)/shard_map/ppermute | solution.py:158
  241.8 16.3 %collective-permute-start.36 = (bf16[1,80,512]{2,1,0:T(8,128)(2,1)S(1)}, bf16[1,80,512]{2,1,0:T(8,128)(2,1)S(1)}, u32[]{:S(2)}, u32[]{:S(2)}) collective-permute-start(bf16[1,80,512]{2,1,0:T(8,128)(2,1)S(1)} %slice.93), channel_id=1, source_target_pairs={{30,0},{31,1},{16,2},{17,3},{18,4},{19,5},{20,6},{21,7},{22,8},{23... | collective-permute-start | bytes 245768 | tf_op jit(solution)/shard_map/ppermute | solution.py:158
  258.1 18.4 %collective-permute-start.39 = (bf16[2,2,96,512]{3,2,1,0:T(8,128)(2,1)S(1)}, bf16[2,2,96,512]{3,2,1,0:T(8,128)(2,1)S(1)}, u32[]{:S(2)}, u32[]{:S(2)}) collective-permute-start(bf16[2,2,96,512]{3,2,1,0:T(8,128)(2,1)S(1)} %copy-done.61), channel_id=1, source_target_pairs={{0,1},{1,0},{2,3},{3,2},{4,5},{5,4},{6,7},{7,6},{8,9},{9,8},{10,11... | collective-permute-start | bytes 1179656 | tf_op jit(solution)/shard_map/ppermute | solution.py:176
  294.5 20.7 %collective-permute-start.48 = (bf16[2,2,96,512]{3,2,1,0:T(8,128)(2,1)}, bf16[2,2,96,512]{3,2,1,0:T(8,128)(2,1)}, u32[]{:S(2)}, u32[]{:S(2)}) collective-permute-start(bf16[2,2,96,512]{3,2,1,0:T(8,128)(2,1)} %get-tuple-element.392), channel_id=1, source_target_pairs={{0,1},{1,0},{2,3},{3,2},{4,5},{5,4},{6,7},{7,6},{8,9},{9,8},{10,11... | collective-permute-start | bytes 1179656 | tf_op jit(solution)/shard_map/ppermute | solution.py:176
  313.6 19.9 %collective-permute-start.45 = (bf16[4,128,512]{2,1,0:T(8,128)(2,1)S(1)}, bf16[4,128,512]{2,1,0:T(8,128)(2,1)S(1)}, u32[]{:S(2)}, u32[]{:S(2)}) collective-permute-start(bf16[4,128,512]{2,1,0:T(8,128)(2,1)S(1)} %dynamic-slice_bitcast_fusion.1), channel_id=1, source_target_pairs={{0,8},{4,12},{8,0},{12,4},{1,9},{5,13},{9,1},{13,5},{2,10},{6,14},... | collective-permute-start | bytes 1572872 | tf_op jit(solution)/shard_map/ppermute | solution.py:176
  334.1 19.4 %collective-permute-start.53 = (bf16[2,128,512]{2,1,0:T(8,128)(2,1)S(1)}, bf16[2,128,512]{2,1,0:T(8,128)(2,1)S(1)}, u32[]{:S(2)}, u32[]{:S(2)}) collective-permute-start(bf16[2,128,512]{2,1,0:T(8,128)(2,1)S(1)} %bitcast_add_fusion.3), channel_id=1, source_target_pairs={{0,1},{1,2},{2,3},{3,0},{4,5},{5,6},{6,7},{7,4},{8,9},{9,10},{10,1... | collective-permute-start | bytes 786440 | tf_op jit(solution)/shard_map/ppermute | solution.py:172
  336.0 17.6 %collective-permute-start.54 = (bf16[128,512]{1,0:T(8,128)(2,1)S(1)}, bf16[128,512]{1,0:T(8,128)(2,1)S(1)}, u32[]{:S(2)}, u32[]{:S(2)}) collective-permute-start(bf16[128,512]{1,0:T(8,128)(2,1)S(1)} %bitcast_add_fusion.10), channel_id=1, source_target_pairs={{0,1},{1,2},{2,3},{3,0},{4,5},{5,6},{6,7},{7,4},{8,9},{9,10},{10,1... | collective-permute-start | bytes 393224 | tf_op jit(solution)/shard_map/ppermute | solution.py:172
  337.9 15.6 %collective-permute-start.55 = (f32[10,2048]{1,0:T(8,128)S(1)}, f32[10,2048]{1,0:T(8,128)S(1)}, u32[]{:S(2)}, u32[]{:S(2)}) collective-permute-start(f32[10,2048]{1,0:T(8,128)S(1)} %add.321), channel_id=1, source_target_pairs={{0,1},{1,0},{2,3},{3,2},{4,5},{5,4},{6,7},{7,6},{8,9},{9,8},{10,11... | collective-permute-start | bytes 245768 | tf_op jit(solution)/shard_map/ppermute | solution.py:176
  353.6 17.2 %collective-permute-start.57 = (bf16[2,128,512]{2,1,0:T(8,128)(2,1)S(1)}, bf16[2,128,512]{2,1,0:T(8,128)(2,1)S(1)}, u32[]{:S(2)}, u32[]{:S(2)}) collective-permute-start(bf16[2,128,512]{2,1,0:T(8,128)(2,1)S(1)} %bitcast_add_fusion.2), channel_id=1, source_target_pairs={{0,8},{4,12},{8,0},{12,4},{1,9},{5,13},{9,1},{13,5},{2,10},{6,14},... | collective-permute-start | bytes 786440 | tf_op jit(solution)/shard_map/ppermute | solution.py:176
  (106 other events, 1158.1 us)
